TPU v7x, 512 devices: a whole 4x8x8 slice. The times are simulated.
512 devices in a mesh: sector: 64 (over x, y, core), chan: 8 (over z).
Axes of the slice: x: 4, y: 8, z: 8, core: 2. Of those that a mesh axis runs over, the one named last changes fastest.
Arguments:
- surface_functions: bfloat16 [128, 256, 4096], P('sector', 'chan'), may hold values from -6 to 6, as said below
- channel_rates: float32 [128, 256], P('sector'), may hold values from 0.5 to 12
- coupling: bfloat16 [128, 256, 256], P('sector'), may hold values from -1 to 6, as said below
Outputs:
- r_inner: float32 [256, 256], P('chan', 'sector')
- r_couple: float32 [256, 256], P('chan', 'sector')
- r_outer: float32 [256, 256], P('chan', 'sector')
Inputs may be any that keep to these rules, and one draw needn't show every extreme that they name: `surface_functions`: the sum of a surface function shared by all sectors and a smaller part of each sector. `coupling`: each sector's matrix is symmetric, and each diagonal entry exceeds the sum of the magnitudes of the other entries of its row.
All inputs are finite; a program needn't handle non-finite values.
Results may differ from a plain program's by a relative error of at most 0.0003.
Values may be sent and summed in bfloat16 or wider, within the bound.
No kernel may reach another device: no remote copies, remote signals or barrier semaphores. Data moves between devices by JAX's collectives and lax.ppermute only.
A program may use at most 64 MiB of HBM per device.

v0:
```python
import functools

import jax
import jax.numpy as jnp
from jax import lax
from jax.experimental import pallas as pl
from jax.experimental.pallas import tpu as pltpu
from jax.sharding import PartitionSpec as P

F32 = jnp.float32
BF16 = jnp.bfloat16
NN = (((1,), (0,)), ((), ()))
NT = (((1,), (1,)), ((), ()))
TN = (((0,), (0,)), ((), ()))
TOLERANCE = 1e-5
STEPS = 8
SQUARINGS = (4, 4, 5, 6, 7, 8, 8)
PARAMS = pltpu.CompilerParams(vmem_limit_bytes=32 * 2**20)
VMEM = pl.BlockSpec(memory_space=pltpu.VMEM)
SMEM = pl.BlockSpec(memory_space=pltpu.SMEM)


def parts(x):
    high = x.astype(BF16)
    rest = x - high.astype(F32)
    middle = rest.astype(BF16)
    return high, middle, (rest - middle.astype(F32)).astype(BF16)


def dot1(a, b, dims=NN):
    return lax.dot_general(a, b, dims, preferred_element_type=F32)


def dot3(a, b, dims=NN):
    return dot1(a[0], b[0], dims) + (dot1(a[0], b[1], dims) + dot1(a[1], b[0], dims))


def dot6(a, b, dims=NN):
    low = dot1(a[0], b[2], dims) + dot1(a[1], b[1], dims) + dot1(a[2], b[0], dims)
    return dot1(a[0], b[0], dims) + ((dot1(a[0], b[1], dims) + dot1(a[1], b[0], dims)) + low)


def grid_of(n):
    return (
        lax.broadcasted_iota(jnp.int32, (n, n), 0),
        lax.broadcasted_iota(jnp.int32, (n, n), 1),
    )


def unit(n):
    row, column = grid_of(n)
    return jnp.where(row == column, F32(1), F32(0))


def step_size(d):
    return 1.9 / jnp.max(jnp.sum(jnp.abs(d), axis=0, keepdims=True), axis=1, keepdims=True)


def first_inverse(d, squarings):
    n = d.shape[0]
    one = unit(n)
    alpha = step_size(d)
    e = one - alpha * d
    c = jnp.sum(jnp.sum(e * one, axis=0, keepdims=True), axis=1, keepdims=True) / n
    f = e - c * one
    p, y = 1 + c, f
    for _ in range(squarings):
        rounded = f.astype(BF16)
        f = 2 * c * f + dot1(rounded, rounded)
        c = c * c
        y = p * f + (1 + c) * y + dot1(y.astype(BF16), f.astype(BF16))
        p = p * (1 + c)
    return alpha * (p * one + y)


def newton(d_parts, x, dot):
    x_parts = parts(x)
    residual = unit(x.shape[0]) - dot(d_parts, x_parts)
    return x + dot3(x_parts, parts(residual)), residual


def combine(left, right, x, out_ref):
    b1, b2, x = parts(left(1)), parts(right(1)), parts(x)
    w1, w2 = parts(dot6(b1, x)), parts(dot6(x, b2))
    out_ref[0] = left(0) - dot6(w1, b1, NT)
    out_ref[1] = dot6(w1, b2)
    out_ref[2] = right(2) - dot6(b2, w2, TN)


def merge_blocks(d, left, right, depth, out_ref, d_ref, x_ref, after):
    d_ref[...] = d
    x_ref[...], _ = newton(parts(d), first_inverse(d, SQUARINGS[min(depth, len(SQUARINGS) - 1)]), dot3)

    def going(state):
        return jnp.logical_and(state[0] < 9 * STEPS, jnp.logical_not(state[1] < TOLERANCE))

    def again(state):
        @pl.when(state[0] == STEPS)
        def _():
            x_ref[...] = step_size(d_ref[...]) * unit(d_ref.shape[0])

        x, residual = newton(parts(d_ref[...]), x_ref[...], dot6)
        x_ref[...] = x
        combine(left, right, x, out_ref)
        after()
        return state[0] + 1, jnp.sum(residual * residual)

    lax.while_loop(going, again, (0, F32(1)))


def pack(core, out_ref, send_ref):
    n = out_ref.shape[-1]
    row, column = grid_of(n)
    last = out_ref[2]
    both = jnp.where(row >= column, out_ref[0], last)
    send_ref[0:n] = jnp.where(core == 0, both, out_ref[1])
    diagonal = jnp.sum(jnp.where(row == column, last, F32(0)), axis=0, keepdims=True)
    send_ref[n : n + 8] = jnp.broadcast_to(diagonal, (8, n))


def leaf_kernel(flags_ref, margin_ref, cot_ref, csc_ref, coupling_ref, out_ref, d_ref, x_ref, a_ref, b_ref, c_ref):
    n = d_ref.shape[0]
    row, column = grid_of(n)
    half_step = 0.5 / (2 * flags_ref[1]).astype(F32)

    def sector(s):
        margin = margin_ref[:, s].reshape(n, n)
        if s == 0:
            margin = jnp.where(flags_ref[0] == 0, unit(n), margin)
        inner = jnp.where(row == column, cot_ref[s : s + 1, :], F32(0)) + half_step * coupling_ref[s].astype(F32)
        m = parts(margin)
        a_ref[s] = dot6(parts(dot6(m, parts(inner))), m, NT)
        b_ref[s] = margin * csc_ref[s : s + 1, :]
        c_ref[s] = inner

    sector(1)
    sector(0)
    blocks = (a_ref, b_ref, c_ref)
    merge_blocks(
        c_ref[0] + a_ref[1],
        lambda i: blocks[i][0],
        lambda i: blocks[i][1],
        0, out_ref, d_ref, x_ref, lambda: None,
    )


def leaf(flags, margin, cot, csc, coupling):
    n = coupling.shape[-1]
    return pl.pallas_call(
        leaf_kernel,
        out_shape=jax.ShapeDtypeStruct((3, n, n), F32),
        in_specs=[SMEM, VMEM, VMEM, VMEM, VMEM],
        out_specs=VMEM,
        scratch_shapes=[pltpu.VMEM((n, n), F32)] * 2 + [pltpu.VMEM((2, n, n), F32)] * 3,
        compiler_params=PARAMS,
        name="leaf",
    )(flags, margin, cot, csc, coupling)


def merge_refs(upper, own_ref, other_ref, depth, out_ref, d_ref, x_ref, after):
    merge_blocks(
        jnp.where(upper, other_ref[2] + own_ref[0], own_ref[2] + other_ref[0]),
        lambda i: jnp.where(upper, other_ref[i], own_ref[i]),
        lambda i: jnp.where(upper, own_ref[i], other_ref[i]),
        depth, out_ref, d_ref, x_ref, after,
    )


def core_kernel(flags_ref, own_ref, other_ref, out_ref, send_ref, d_ref, x_ref):
    core = flags_ref[2]
    merge_refs(core == 1, own_ref, other_ref, 1, out_ref, d_ref, x_ref, lambda: pack(core, out_ref, send_ref))


def core_merge(flags, own, other):
    n = own.shape[-1]
    return pl.pallas_call(
        core_kernel,
        out_shape=(jax.ShapeDtypeStruct((3, n, n), F32), jax.ShapeDtypeStruct((n + 8, n), F32)),
        in_specs=[SMEM, VMEM, VMEM],
        out_specs=(VMEM, VMEM),
        scratch_shapes=[pltpu.VMEM((n, n), F32)] * 2,
        compiler_params=PARAMS,
        name="core_merge",
    )(flags, own, other)


def unpack(core, came_ref, swapped_ref, other_ref):
    n = other_ref.shape[-1]
    row, column = grid_of(n)
    both = jnp.where(core == 0, came_ref[0:n], swapped_ref[0:n])
    diagonal = jnp.where(core == 0, came_ref[n : n + 1], swapped_ref[n : n + 1])
    turned = both.T
    other_ref[0] = jnp.where(row >= column, both, turned)
    other_ref[1] = jnp.where(core == 0, swapped_ref[0:n], came_ref[0:n])
    other_ref[2] = jnp.where(row == column, diagonal, jnp.where(row < column, both, turned))


def chip_kernel(level, flags_ref, own_ref, came_ref, swapped_ref, out_ref, send_ref, d_ref, x_ref, other_ref):
    core = flags_ref[2]
    active = flags_ref[4 + 2 * level] == 1

    @pl.when(active)
    def _():
        unpack(core, came_ref, swapped_ref, other_ref)
        merge_refs(
            flags_ref[5 + 2 * level] == 1, own_ref, other_ref, level + 2, out_ref, d_ref, x_ref,
            lambda: pack(core, out_ref, send_ref),
        )

    @pl.when(jnp.logical_not(active))
    def _():
        out_ref[...] = own_ref[...]
        send_ref[...] = jnp.zeros_like(send_ref)


def chip_merge(level, flags, own, came, swapped):
    n = own.shape[-1]
    return pl.pallas_call(
        functools.partial(chip_kernel, level),
        out_shape=(jax.ShapeDtypeStruct((3, n, n), F32), jax.ShapeDtypeStruct((n + 8, n), F32)),
        in_specs=[SMEM, VMEM, VMEM, VMEM],
        out_specs=(VMEM, VMEM),
        scratch_shapes=[pltpu.VMEM((n, n), F32)] * 2 + [pltpu.VMEM((3, n, n), F32)],
        compiler_params=PARAMS,
        name="chip_merge",
    )(flags, own, came, swapped)


def last_kernel(level, flags_ref, own_ref, came_ref, swapped_ref, mine_ref, next_ref, d_ref, x_ref, other_ref, out_ref):
    n = d_ref.shape[0]
    core = flags_ref[2]
    wide, rows = mine_ref.shape[1:]
    active = flags_ref[4 + 2 * level] == 1

    def piece(chip, to_ref):
        chip_rows = pl.ds(pl.multiple_of(chip * (2 * wide), 2 * wide), 2 * wide)
        for i in range(3):
            source = other_ref if i == 1 else out_ref
            both = source[0 if i == 1 else i, chip_rows, :]
            moved = pltpu.roll(both, (n - flags_ref[3] * rows) % n, axis=1)[:, :rows]
            to_ref[i] = jnp.where(core == 0, moved[:wide], moved[wide:])

    @pl.when(active)
    def _():
        unpack(core, came_ref, swapped_ref, other_ref)
        merge_refs(
            flags_ref[5 + 2 * level] == 1, own_ref, other_ref, level + 2, out_ref, d_ref, x_ref, lambda: None
        )
        other_ref[0] = out_ref[1].T
        chip = flags_ref[0] // 2
        piece(chip, mine_ref)
        piece(chip + 1 - 2 * (chip % 2), next_ref)

    @pl.when(jnp.logical_not(active))
    def _():
        mine_ref[...] = jnp.zeros_like(mine_ref)
        next_ref[...] = jnp.zeros_like(next_ref)


def last_merge(level, flags, own, came, swapped, wide, rows):
    n = own.shape[-1]
    return pl.pallas_call(
        functools.partial(last_kernel, level),
        out_shape=(jax.ShapeDtypeStruct((3, wide, rows), F32),) * 2,
        in_specs=[SMEM, VMEM, VMEM, VMEM],
        out_specs=(VMEM, VMEM),
        scratch_shapes=[pltpu.VMEM((n, n), F32)] * 2 + [pltpu.VMEM((3, n, n), F32)] * 2,
        compiler_params=PARAMS,
        name="last_merge",
    )(flags, own, came, swapped)


def pick_kernel(flags_ref, mine_ref, brought_ref, a_ref, b_ref, c_ref):
    for i, ref in enumerate((a_ref, b_ref, c_ref)):
        ref[...] = jnp.where(flags_ref[0] == 1, mine_ref[i], brought_ref[i])


def pick(flag, mine, brought):
    return pl.pallas_call(
        pick_kernel,
        out_shape=(jax.ShapeDtypeStruct(mine.shape[1:], F32),) * 3,
        in_specs=[SMEM, VMEM, VMEM],
        out_specs=(VMEM,) * 3,
        name="pick",
    )(flag, mine, brought)


def margin_kernel(own_ref, before_ref, out_ref):
    shards, _, rows, depth = own_ref.shape
    n = shards * rows
    first = own_ref[:, 0].reshape(n, depth)
    second = own_ref[:, 1].reshape(n, depth)
    out_ref[:, 1] = dot1(first, second, NT).reshape(shards, rows, n)
    out_ref[:, 0] = dot1(before_ref[...].reshape(n, depth), first, NT).reshape(shards, rows, n)


def margin_parts(own, before):
    shards, sectors, rows, _ = own.shape
    return pl.pallas_call(
        margin_kernel,
        out_shape=jax.ShapeDtypeStruct((shards, sectors, rows, shards * rows), F32),
        in_specs=[VMEM, VMEM],
        out_specs=VMEM,
        compiler_params=PARAMS,
        name="margin_parts",
    )(own, before)


def total_kernel(points, partial_ref, out_ref):
    total = partial_ref[0]
    for shard in range(1, partial_ref.shape[0]):
        total = total + partial_ref[shard]
    total = total / points
    for shard in range(partial_ref.shape[0]):
        out_ref[shard] = total


def total_for_all(partial, points):
    return pl.pallas_call(
        functools.partial(total_kernel, points),
        out_shape=jax.ShapeDtypeStruct(partial.shape, F32),
        in_specs=[VMEM],
        out_specs=VMEM,
        compiler_params=PARAMS,
        name="total_for_all",
    )(partial)


def exchange(array):
    return lax.all_to_all(array, "chan", split_axis=0, concat_axis=0, tiled=True)


YS = 8
ENDS = (0, 3, 4, 7)


def place(position):
    return position // (2 * YS), position // 2 % YS, position % 2


def spot(x, y, core):
    return (x * YS + y) * 2 + core


def levels(xs):
    result = [
        (lambda x, y: (x, y ^ 1), range(YS), ("y", 0)),
        (lambda x, y: (x, y ^ 2), ENDS, ("y", 1)),
        (lambda x, y: (x, YS - 1 - y), ENDS, ("y", 2)),
    ]
    for bit in range(xs.bit_length() - 1):
        mask = 2 ** (bit + 1) - 1
        result.append((lambda x, y, mask=mask: (x ^ mask, y), ENDS, ("x", bit)))
    return result


def per_device(surface_functions, channel_rates, coupling):
    sectors, rows, points = surface_functions.shape
    n = channel_rates.shape[1]
    shards = lax.axis_size("chan")
    count = lax.axis_size("sector")
    position = lax.axis_index("sector")
    plan = levels(count // (2 * YS))
    x, y, core = place(position)
    at_end = (y == ENDS[0]) | (y == ENDS[1]) | (y == ENDS[2]) | (y == ENDS[3])
    words = [position, jnp.int32(count), core, lax.axis_index("chan")]
    for _, takers, (axis, bit) in plan:
        words.append(jnp.int32(1) if len(takers) == YS else at_end.astype(jnp.int32))
        words.append((x if axis == "x" else y) >> bit & 1)
    flags = jnp.stack([jnp.asarray(word, jnp.int32) for word in words])

    step = 1.0 / (sectors * count)
    cot = channel_rates / jnp.tanh(channel_rates * step)
    csc = channel_rates / jnp.sinh(channel_rates * step)

    cut = surface_functions.reshape(sectors, rows, shards, points // shards)
    own = exchange(jnp.transpose(cut, (2, 0, 1, 3)))
    before = lax.ppermute(own[:, sectors - 1], "sector", [(i, i + 1) for i in range(count - 1)])
    partial = exchange(margin_parts(own, before))
    ready = total_for_all(partial, points)
    ready, flags, cot, csc = lax.optimization_barrier((ready, flags, cot, csc))
    margin = exchange(ready)

    packed = leaf(flags, margin, cot, csc, coupling)
    cores = [(i, i ^ 1) for i in range(count)]
    packed, send = core_merge(flags, packed, lax.ppermute(packed, "sector", cores))
    wide = n // count
    for level, (partner, takers, _) in enumerate(plan):
        pairs = []
        for i in range(count):
            xi, yi, ci = place(i)
            if yi in takers:
                pairs.append((spot(*partner(xi, yi), ci), i))
        came = lax.ppermute(send, "sector", pairs)
        swapped = lax.ppermute(came, "sector", cores)
        if level < len(plan) - 1:
            packed, send = chip_merge(level, flags, packed, came, swapped)
        else:
            mine, for_next = last_merge(level, flags, packed, came, swapped, wide, rows)
    pairs = []
    for i in range(count):
        xi, yi, ci = place(i)
        if yi not in ENDS:
            pairs.append((spot(xi, yi ^ 1, ci), i))
    brought = lax.ppermute(for_next, "sector", pairs)
    return tuple(block.T for block in pick(at_end.astype(jnp.int32)[None], mine, brought))


def solution(mesh):
    placed = (P("sector", "chan", None), P("sector", None), P("sector", None, None))
    return jax.shard_map(
        per_device,
        mesh=mesh,
        in_specs=placed,
        out_specs=(P("chan", "sector"), P("chan", "sector"), P("chan", "sector")),
        check_vma=False,
    )
```

profile of v0, /device:TPU:22, one launch (start us, length us, event | category | flops | bytes accessed | tf_op | source)
XLA Modules:
  0.0 203.2 jit_solution(13625917512343487550)
XLA Ops:
  0.6 1.2 copy.12
  1.9 0.2 copy.9
  2.1 27.6 %all_to_all.15.own_ref = bf16[8,2,32,512]{3,2,1,0:T(8,128)(2,1)S(1)} all-to-all(bf16[8,2,32,512]{3,2,1,0:T(8,128)(2,1)S(1)} %copy.9), channel_id=1, replica_groups=mesh['sector'=64,'chan'=8] {'chan'}, dimensions={0} | all-to-all | bytes 1048576 | tf_op jit(solution)/shard_map/all_to_all | solution.py:330
  29.7 1.9 collective-permute-start
  31.6 5.8 %collective-permute-done.before_ref = bf16[8,32,512]{2,1,0:T(8,128)(2,1)S(1)} collective-permute-done((bf16[8,32,512]{2,1,0:T(8,128)(2,1)S(1)}, bf16[8,32,512]{2,1,0:T(8,128)(2,1)S(1)}, u32[]{:S(2)}, u32[]{:S(2)}) %collective-permute-start) | collective-permute-done | bytes 262176 | tf_op jit(solution)/shard_map/ppermute | solution.py:378
  37.4 1.1 margin_parts.1
  38.5 3.5 %all-to-all-start.1 = ((f32[8,2,32,256]{3,2,1,0:T(8,128)}), f32[8,2,32,256]{3,2,1,0:T(8,128)S(1)}, u32[]{:S(2)}, u32[]{:S(2)}) async-start(f32[8,2,32,256]{3,2,1,0:T(8,128)} %margin_parts.1), calls=%async_computation.1 | async-start | bytes 1048576 | tf_op jit(solution)/shard_map/all_to_all | solution.py:330
  42.1 0.0 copy-start.3
  42.1 0.1 stack.39.flags_ref
  42.2 0.6 copy-done.3
  42.8 16.3 %all-to-all-done.1.partial_ref = f32[8,2,32,256]{3,2,1,0:T(8,128)S(1)} async-done(((f32[8,2,32,256]{3,2,1,0:T(8,128)}), f32[8,2,32,256]{3,2,1,0:T(8,128)S(1)}, u32[]{:S(2)}, u32[]{:S(2)}) %all-to-all-start.1) | async-done | bytes 524320 | tf_op jit(solution)/shard_map/all_to_all | solution.py:330
  59.1 0.0 copy-start
  59.1 19.3 %all_to_all.16.margin_ref = f32[8,2,32,256]{3,2,1,0:T(8,128)S(1)} all-to-all(f32[8,2,32,256]{3,2,1,0:T(8,128)S(1)} %total_for_all.1), channel_id=1, replica_groups=mesh['sector'=64,'chan'=8] {'chan'}, dimensions={0} | all-to-all | bytes 1048576 | tf_op jit(solution)/shard_map/all_to_all | solution.py:330
  78.4 0.0 copy-done
  78.4 5.8 %leaf.1.own_ref = f32[3,256,256]{2,1,0:T(8,128)S(1)} custom-call(s32[14]{0:T(128)S(1)} %stack.39.flags_ref, f32[8,2,32,256]{3,2,1,0:T(8,128)S(1)} %all_to_all.16.margin_ref, f32[2,256]{1,0:T(2,128)S(1)} %get-tuple-element.24.cot_ref, f32[2,256]{1,0:T(2,128)S(1)} %get-tuple-element.25.csc_ref, bf16[2,256,256]{2,1,0:T(8,128)(2,1)S(1)} %copy-done), custom_call_target="tpu_custom_call" | custom-call | tf_op jit(solution)/shard_map/leaf/pallas_call | solution.py:149
  84.2 1.9 collective-permute-start.1
  86.1 2.3 %collective-permute-done.1.other_ref = f32[3,256,256]{2,1,0:T(8,128)S(1)} collective-permute-done((f32[3,256,256]{2,1,0:T(8,128)S(1)}, f32[3,256,256]{2,1,0:T(8,128)S(1)}, u32[]{:S(2)}, u32[]{:S(2)}) %collective-permute-start.1) | collective-permute-done | bytes 786464 | tf_op jit(solution)/shard_map/ppermute | solution.py:386
  88.4 4.8 %core_merge.1 = (f32[3,256,256]{2,1,0:T(8,128)S(1)}, f32[264,256]{1,0:T(8,128)S(1)}) custom-call(s32[14]{0:T(128)S(1)} %stack.39.flags_ref, f32[3,256,256]{2,1,0:T(8,128)S(1)} %leaf.1.own_ref, f32[3,256,256]{2,1,0:T(8,128)S(1)} %collective-permute-done.1.other_ref), custom_call_target="tpu_custom_call" | custom-call | tf_op jit(solution)/shard_map/core_merge/pallas_call | solution.py:176
  93.3 6.0 %collective-permute-start.2 = (f32[264,256]{1,0:T(8,128)S(1)}, f32[264,256]{1,0:T(8,128)S(1)}, u32[]{:S(2)}, u32[]{:S(2)}) collective-permute-start(f32[264,256]{1,0:T(8,128)S(1)} %get-tuple-element.27), channel_id=1, source_target_pairs={{16,0},{24,8},{0,16},{8,24},{48,32},{56,40},{32,48},{40,56},{80,64... | collective-permute-start | bytes 811016 | tf_op jit(solution)/shard_map/ppermute | solution.py:394
  99.2 6.8 %collective-permute-done.2.came_ref = f32[264,256]{1,0:T(8,128)S(1)} collective-permute-done((f32[264,256]{1,0:T(8,128)S(1)}, f32[264,256]{1,0:T(8,128)S(1)}, u32[]{:S(2)}, u32[]{:S(2)}) %collective-permute-start.2) | collective-permute-done | bytes 270368 | tf_op jit(solution)/shard_map/ppermute | solution.py:394
  106.0 1.9 collective-permute-start.3
  107.9 1.5 collective-permute-done.3.swapped_ref
  109.4 5.1 %chip_merge.4 = (f32[3,256,256]{2,1,0:T(8,128)S(1)}, f32[264,256]{1,0:T(8,128)S(1)}) custom-call(s32[14]{0:T(128)S(1)} %stack.39.flags_ref, f32[3,256,256]{2,1,0:T(8,128)S(1)} %get-tuple-element.26.own_ref, f32[264,256]{1,0:T(8,128)S(1)} %collective-permute-done.2.came_ref, f32[264,256]{1,0:T(8,128)S(1)} %collective-permute-done.3.swapped_ref), custom_call_target="tpu_custom_call" | custom-call | tf_op jit(solution)/shard_map/chip_merge/pallas_call | solution.py:218
  114.5 1.3 collective-permute-start.4
  115.9 6.3 %collective-permute-done.4.came_ref = f32[264,256]{1,0:T(8,128)S(1)} collective-permute-done((f32[264,256]{1,0:T(8,128)S(1)}, f32[264,256]{1,0:T(8,128)S(1)}, u32[]{:S(2)}, u32[]{:S(2)}) %collective-permute-start.4) | collective-permute-done | bytes 270368 | tf_op jit(solution)/shard_map/ppermute | solution.py:394
  122.2 1.9 collective-permute-start.5
  124.1 1.5 collective-permute-done.5.swapped_ref
  125.6 0.8 chip_merge.5
  126.4 0.7 collective-permute-start.6
  127.1 0.0 collective-permute-done.6.came_ref
  127.1 2.0 %collective-permute-start.7 = (f32[264,256]{1,0:T(8,128)S(1)}, f32[264,256]{1,0:T(8,128)S(1)}, u32[]{:S(2)}, u32[]{:S(2)}) collective-permute-start(f32[264,256]{1,0:T(8,128)S(1)} %collective-permute-done.6.came_ref), channel_id=1, source_target_pairs={{0,8},{8,0},{16,24},{24,16},{32,40},{40,32},{48,56},{56,48},{64,72... | collective-permute-start | bytes 811016 | tf_op jit(solution)/shard_map/ppermute | solution.py:395
  129.1 1.4 collective-permute-done.7.swapped_ref
  130.5 0.6 chip_merge.6
  131.2 0.7 collective-permute-start.8
  131.8 0.0 collective-permute-done.8.came_ref
  131.8 2.0 %collective-permute-start.9 = (f32[264,256]{1,0:T(8,128)S(1)}, f32[264,256]{1,0:T(8,128)S(1)}, u32[]{:S(2)}, u32[]{:S(2)}) collective-permute-start(f32[264,256]{1,0:T(8,128)S(1)} %collective-permute-done.8.came_ref), channel_id=1, source_target_pairs={{0,8},{8,0},{16,24},{24,16},{32,40},{40,32},{48,56},{56,48},{64,72... | collective-permute-start | bytes 811016 | tf_op jit(solution)/shard_map/ppermute | solution.py:395
  133.9 1.4 collective-permute-done.9.swapped_ref
  135.3 0.6 chip_merge.7
  135.9 0.7 collective-permute-start.10
  136.6 0.0 collective-permute-done.10.came_ref
  136.6 2.0 %collective-permute-start.11 = (f32[264,256]{1,0:T(8,128)S(1)}, f32[264,256]{1,0:T(8,128)S(1)}, u32[]{:S(2)}, u32[]{:S(2)}) collective-permute-start(f32[264,256]{1,0:T(8,128)S(1)} %collective-permute-done.10.came_ref), channel_id=1, source_target_pairs={{0,8},{8,0},{16,24},{24,16},{32,40},{40,32},{48,56},{56,48},{64,72... | collective-permute-start | bytes 811016 | tf_op jit(solution)/shard_map/ppermute | solution.py:395
  138.7 1.4 collective-permute-done.11.swapped_ref
  140.1 0.8 last_merge.1
  140.8 0.0 copy-start.1
  140.8 0.6 copy-done.1
  141.4 1.3 collective-permute-start.12
  142.7 58.6 %collective-permute-done.12.brought_ref = f32[3,4,32]{2,1,0:T(4,128)S(1)} collective-permute-done((f32[3,4,32]{2,1,0:T(4,128)S(1)}, f32[3,4,32]{2,1,0:T(4,128)S(1)}, u32[]{:S(2)}, u32[]{:S(2)}) %collective-permute-start.12) | collective-permute-done | bytes 1568 | tf_op jit(solution)/shard_map/ppermute | solution.py:405
  201.3 0.0 copy-start.2
  201.3 0.6 copy-done.2
  201.9 1.3 pick.1
  (4 shorter events, 0.1 us)
Async XLA Ops:
  29.7 7.7 %collective-permute-start = (bf16[8,32,512]{2,1,0:T(8,128)(2,1)S(1)}, bf16[8,32,512]{2,1,0:T(8,128)(2,1)S(1)}, u32[]{:S(2)}, u32[]{:S(2)}) collective-permute-start(bf16[8,32,512]{2,1,0:T(8,128)(2,1)S(1)} %slice_bitcast_fusion), channel_id=1, source_target_pairs={{0,8},{8,16},{16,24},{24,32},{32,40},{40,48},{48,56},{56,64},{64,7... | collective-permute-start | bytes 786440 | tf_op jit(solution)/shard_map/ppermute | solution.py:378
  38.5 20.6 %all-to-all-start.1 = ((f32[8,2,32,256]{3,2,1,0:T(8,128)}), f32[8,2,32,256]{3,2,1,0:T(8,128)S(1)}, u32[]{:S(2)}, u32[]{:S(2)}) async-start(f32[8,2,32,256]{3,2,1,0:T(8,128)} %margin_parts.1), calls=%async_computation.1 | async-start | bytes 1048576 | tf_op jit(solution)/shard_map/all_to_all | solution.py:330
  42.1 0.7 copy-start.3
  59.1 19.3 %copy-start = (bf16[2,256,256]{2,1,0:T(8,128)(2,1)S(1)}, bf16[2,256,256]{2,1,0:T(8,128)(2,1)}, u32[]{:S(2)}) copy-start(bf16[2,256,256]{2,1,0:T(8,128)(2,1)} %coupling_ref.1) | copy-start | bytes 786436
  84.2 4.2 %collective-permute-start.1 = (f32[3,256,256]{2,1,0:T(8,128)S(1)}, f32[3,256,256]{2,1,0:T(8,128)S(1)}, u32[]{:S(2)}, u32[]{:S(2)}) collective-permute-start(f32[3,256,256]{2,1,0:T(8,128)S(1)} %leaf.1.own_ref), channel_id=1, source_target_pairs={{0,8},{8,0},{16,24},{24,16},{32,40},{40,32},{48,56},{56,48},{64,72... | collective-permute-start | bytes 2359304 | tf_op jit(solution)/shard_map/ppermute | solution.py:386
  93.3 12.7 %collective-permute-start.2 = (f32[264,256]{1,0:T(8,128)S(1)}, f32[264,256]{1,0:T(8,128)S(1)}, u32[]{:S(2)}, u32[]{:S(2)}) collective-permute-start(f32[264,256]{1,0:T(8,128)S(1)} %get-tuple-element.27), channel_id=1, source_target_pairs={{16,0},{24,8},{0,16},{8,24},{48,32},{56,40},{32,48},{40,56},{80,64... | collective-permute-start | bytes 811016 | tf_op jit(solution)/shard_map/ppermute | solution.py:394
  106.0 3.4 %collective-permute-start.3 = (f32[264,256]{1,0:T(8,128)S(1)}, f32[264,256]{1,0:T(8,128)S(1)}, u32[]{:S(2)}, u32[]{:S(2)}) collective-permute-start(f32[264,256]{1,0:T(8,128)S(1)} %collective-permute-done.2.came_ref), channel_id=1, source_target_pairs={{0,8},{8,0},{16,24},{24,16},{32,40},{40,32},{48,56},{56,48},{64,72... | collective-permute-start | bytes 811016 | tf_op jit(solution)/shard_map/ppermute | solution.py:395
  114.5 7.6 %collective-permute-start.4 = (f32[264,256]{1,0:T(8,128)S(1)}, f32[264,256]{1,0:T(8,128)S(1)}, u32[]{:S(2)}, u32[]{:S(2)}) collective-permute-start(f32[264,256]{1,0:T(8,128)S(1)} %get-tuple-element.29), channel_id=1, source_target_pairs={{32,0},{40,8},{16,48},{24,56},{96,64},{104,72},{80,112},{88,120},{... | collective-permute-start | bytes 811016 | tf_op jit(solution)/shard_map/ppermute | solution.py:394
  122.2 3.4 %collective-permute-start.5 = (f32[264,256]{1,0:T(8,128)S(1)}, f32[264,256]{1,0:T(8,128)S(1)}, u32[]{:S(2)}, u32[]{:S(2)}) collective-permute-start(f32[264,256]{1,0:T(8,128)S(1)} %collective-permute-done.4.came_ref), channel_id=1, source_target_pairs={{0,8},{8,0},{16,24},{24,16},{32,40},{40,32},{48,56},{56,48},{64,72... | collective-permute-start | bytes 811016 | tf_op jit(solution)/shard_map/ppermute | solution.py:395
  126.4 0.7 collective-permute-start.6
  127.1 3.4 %collective-permute-start.7 = (f32[264,256]{1,0:T(8,128)S(1)}, f32[264,256]{1,0:T(8,128)S(1)}, u32[]{:S(2)}, u32[]{:S(2)}) collective-permute-start(f32[264,256]{1,0:T(8,128)S(1)} %collective-permute-done.6.came_ref), channel_id=1, source_target_pairs={{0,8},{8,0},{16,24},{24,16},{32,40},{40,32},{48,56},{56,48},{64,72... | collective-permute-start | bytes 811016 | tf_op jit(solution)/shard_map/ppermute | solution.py:395
  131.2 0.7 collective-permute-start.8
  131.8 3.4 %collective-permute-start.9 = (f32[264,256]{1,0:T(8,128)S(1)}, f32[264,256]{1,0:T(8,128)S(1)}, u32[]{:S(2)}, u32[]{:S(2)}) collective-permute-start(f32[264,256]{1,0:T(8,128)S(1)} %collective-permute-done.8.came_ref), channel_id=1, source_target_pairs={{0,8},{8,0},{16,24},{24,16},{32,40},{40,32},{48,56},{56,48},{64,72... | collective-permute-start | bytes 811016 | tf_op jit(solution)/shard_map/ppermute | solution.py:395
  135.9 0.7 collective-permute-start.10
  136.6 3.4 %collective-permute-start.11 = (f32[264,256]{1,0:T(8,128)S(1)}, f32[264,256]{1,0:T(8,128)S(1)}, u32[]{:S(2)}, u32[]{:S(2)}) collective-permute-start(f32[264,256]{1,0:T(8,128)S(1)} %collective-permute-done.10.came_ref), channel_id=1, source_target_pairs={{0,8},{8,0},{16,24},{24,16},{32,40},{40,32},{48,56},{56,48},{64,72... | collective-permute-start | bytes 811016 | tf_op jit(solution)/shard_map/ppermute | solution.py:395
  140.8 0.6 copy-start.1
  141.4 59.9 %collective-permute-start.12 = (f32[3,4,32]{2,1,0:T(4,128)S(1)}, f32[3,4,32]{2,1,0:T(4,128)S(1)}, u32[]{:S(2)}, u32[]{:S(2)}) collective-permute-start(f32[3,4,32]{2,1,0:T(4,128)S(1)} %get-tuple-element.37), channel_id=1, source_target_pairs={{0,16},{8,24},{48,32},{56,40},{64,80},{72,88},{112,96},{120,104},{... | collective-permute-start | bytes 4616 | tf_op jit(solution)/shard_map/ppermute | solution.py:405
  201.3 0.6 copy-start.2
where the time goes:
time: 204 us; the launch traced here: 203 us
  waiting for transfers between devices  103 us (50%)
  blocking collectives  46.9 us (23%)
  starting transfers between devices  27.9 us (14%)
  Pallas kernels  21 us (10%)
  local copies, waits for them, and re-layouts  3.29 us (2%)
    ppermute x1, waiting for transfers between devices, per_device(): brought = lax.ppermute(for_next, 'sector', pairs)  58.6 us
    all_to_all x2, blocking collectives, exchange(): lax.all_to_all(array, 'chan', split_axis=0, concat_axis=0, tiled=True)  46.9 us
    all_to_all x1, waiting for transfers between devices, exchange(): lax.all_to_all(array, 'chan', split_axis=0, concat_axis=0, tiled=True)  16.3 us
    ppermute x5, waiting for transfers between devices, per_device(): came = lax.ppermute(send, 'sector', pairs)  13.1 us
    ppermute x5, starting transfers between devices, per_device(): swapped = lax.ppermute(came, 'sector', cores)  9.95 us
    ppermute x5, starting transfers between devices, per_device(): came = lax.ppermute(send, 'sector', pairs)  9.32 us
    ppermute x5, waiting for transfers between devices, per_device(): swapped = lax.ppermute(came, 'sector', cores)  7.19 us
    pallas_call x4, Pallas kernels, chip_merge(): pl.pallas_call(functools.partial(chip_kernel, level), out_shape=(jax.Shap...  7.14 us
  transfers between devices with their start and end apart: 14, of which 11 were waited for; matrix products, arithmetic and copies ran while one was open for 0% of the time, Pallas kernels for 0%

commit v1 on v0

--- a/solution.py
+++ b/solution.py
@@ -226,7 +226,33 @@
     )(flags, own, came, swapped)
 
 
-def last_kernel(level, flags_ref, own_ref, came_ref, swapped_ref, mine_ref, next_ref, d_ref, x_ref, other_ref, out_ref):
+def pair_kernel(level, flags_ref, came_ref, swapped_ref, came2_ref, swapped2_ref, out_ref, d_ref, x_ref, one_ref, other_ref):
+    core = flags_ref[2]
+    active = flags_ref[4 + 2 * level] == 1
+
+    @pl.when(active)
+    def _():
+        unpack(core, came_ref, swapped_ref, one_ref)
+        unpack(core, came2_ref, swapped2_ref, other_ref)
+        merge_refs(
+            flags_ref[5 + 2 * level] == 1, one_ref, other_ref, level + 2, out_ref, d_ref, x_ref, lambda: None
+        )
+
+
+def pair_merge(level, flags, one, other):
+    n = one[0].shape[-1]
+    return pl.pallas_call(
+        functools.partial(pair_kernel, level),
+        out_shape=jax.ShapeDtypeStruct((3, n, n), F32),
+        in_specs=[SMEM] + [VMEM] * 4,
+        out_specs=VMEM,
+        scratch_shapes=[pltpu.VMEM((n, n), F32)] * 2 + [pltpu.VMEM((3, n, n), F32)] * 2,
+        compiler_params=PARAMS,
+        name="pair_merge",
+    )(flags, *one, *other)
+
+
+def last_kernel(level, flags_ref, own_ref, other_ref, mine_ref, next_ref, d_ref, x_ref, turned_ref, out_ref):
     n = d_ref.shape[0]
     core = flags_ref[2]
     wide, rows = mine_ref.shape[1:]
@@ -235,18 +261,16 @@
     def piece(chip, to_ref):
         chip_rows = pl.ds(pl.multiple_of(chip * (2 * wide), 2 * wide), 2 * wide)
         for i in range(3):
-            source = other_ref if i == 1 else out_ref
-            both = source[0 if i == 1 else i, chip_rows, :]
+            both = turned_ref[chip_rows, :] if i == 1 else out_ref[i, chip_rows, :]
             moved = pltpu.roll(both, (n - flags_ref[3] * rows) % n, axis=1)[:, :rows]
             to_ref[i] = jnp.where(core == 0, moved[:wide], moved[wide:])
 
     @pl.when(active)
     def _():
-        unpack(core, came_ref, swapped_ref, other_ref)
         merge_refs(
             flags_ref[5 + 2 * level] == 1, own_ref, other_ref, level + 2, out_ref, d_ref, x_ref, lambda: None
         )
-        other_ref[0] = out_ref[1].T
+        turned_ref[...] = out_ref[1].T
         chip = flags_ref[0] // 2
         piece(chip, mine_ref)
         piece(chip + 1 - 2 * (chip % 2), next_ref)
@@ -257,32 +281,32 @@
         next_ref[...] = jnp.zeros_like(next_ref)
 
 
-def last_merge(level, flags, own, came, swapped, wide, rows):
+def last_merge(level, flags, own, other, wide, rows):
     n = own.shape[-1]
     return pl.pallas_call(
         functools.partial(last_kernel, level),
         out_shape=(jax.ShapeDtypeStruct((3, wide, rows), F32),) * 2,
-        in_specs=[SMEM, VMEM, VMEM, VMEM],
+        in_specs=[SMEM, VMEM, VMEM],
         out_specs=(VMEM, VMEM),
-        scratch_shapes=[pltpu.VMEM((n, n), F32)] * 2 + [pltpu.VMEM((3, n, n), F32)] * 2,
+        scratch_shapes=[pltpu.VMEM((n, n), F32)] * 3 + [pltpu.VMEM((3, n, n), F32)],
         compiler_params=PARAMS,
         name="last_merge",
-    )(flags, own, came, swapped)
-
-
-def pick_kernel(flags_ref, mine_ref, brought_ref, a_ref, b_ref, c_ref):
+    )(flags, own, other)
+
+
+def pick_kernel(level, flags_ref, mine_ref, brought_ref, a_ref, b_ref, c_ref):
     for i, ref in enumerate((a_ref, b_ref, c_ref)):
-        ref[...] = jnp.where(flags_ref[0] == 1, mine_ref[i], brought_ref[i])
-
-
-def pick(flag, mine, brought):
-    return pl.pallas_call(
-        pick_kernel,
+        ref[...] = jnp.where(flags_ref[4 + 2 * level] == 1, mine_ref[i], brought_ref[i])
+
+
+def pick(level, flags, mine, brought):
+    return pl.pallas_call(
+        functools.partial(pick_kernel, level),
         out_shape=(jax.ShapeDtypeStruct(mine.shape[1:], F32),) * 3,
         in_specs=[SMEM, VMEM, VMEM],
         out_specs=(VMEM,) * 3,
         name="pick",
-    )(flag, mine, brought)
+    )(flags, mine, brought)
 
 
 def margin_kernel(own_ref, before_ref, out_ref):
@@ -384,26 +408,32 @@
     packed = leaf(flags, margin, cot, csc, coupling)
     cores = [(i, i ^ 1) for i in range(count)]
     packed, send = core_merge(flags, packed, lax.ppermute(packed, "sector", cores))
-    wide = n // count
-    for level, (partner, takers, _) in enumerate(plan):
+    def fetched(partner, takers):
         pairs = []
         for i in range(count):
             xi, yi, ci = place(i)
             if yi in takers:
                 pairs.append((spot(*partner(xi, yi), ci), i))
-        came = lax.ppermute(send, "sector", pairs)
-        swapped = lax.ppermute(came, "sector", cores)
-        if level < len(plan) - 1:
-            packed, send = chip_merge(level, flags, packed, came, swapped)
-        else:
-            mine, for_next = last_merge(level, flags, packed, came, swapped, wide, rows)
+        return lax.ppermute(send, "sector", pairs)
+
+    def both(came):
+        return came, lax.ppermute(came, "sector", cores)
+
+    for level, (partner, takers, _) in enumerate(plan[:3]):
+        packed, send = chip_merge(level, flags, packed, *both(fetched(partner, takers)))
+    across = fetched(lambda x, y: (x ^ 2, y), ENDS)
+    near = fetched(lambda x, y: (x ^ 1, y), ENDS)
+    far = fetched(lambda x, y: (x ^ 3, y), ENDS)
+    packed, _ = chip_merge(3, flags, packed, *both(near))
+    other = pair_merge(3, flags, both(across), both(far))
+    mine, for_next = last_merge(4, flags, packed, other, n // count, rows)
     pairs = []
     for i in range(count):
         xi, yi, ci = place(i)
         if yi not in ENDS:
             pairs.append((spot(xi, yi ^ 1, ci), i))
     brought = lax.ppermute(for_next, "sector", pairs)
-    return tuple(block.T for block in pick(at_end.astype(jnp.int32)[None], mine, brought))
+    return tuple(block.T for block in pick(4, flags, mine, brought))
 
 
 def solution(mesh):

time: 204 us -> 208 us (1.020)
  the two profiles are of different devices: /device:TPU:22 before, /device:TPU:16 now
where the time goes in v1:
time: 208 us; the launch traced here: 207 us
  waiting for transfers between devices  102 us (49%)
  blocking collectives  46.9 us (23%)
  starting transfers between devices  30.8 us (15%)
  Pallas kernels  22.3 us (11%)
  local copies, waits for them, and re-layouts  3.28 us (2%)
    ppermute x1, waiting for transfers between devices, per_device(): brought = lax.ppermute(for_next, 'sector', pairs)  60.6 us
    all_to_all x2, blocking collectives, exchange(): lax.all_to_all(array, 'chan', split_axis=0, concat_axis=0, tiled=True)  46.9 us
    all_to_all x1, waiting for transfers between devices, exchange(): lax.all_to_all(array, 'chan', split_axis=0, concat_axis=0, tiled=True)  16.3 us
    ppermute x6, waiting for transfers between devices, fetched(): return lax.ppermute(send, 'sector', pairs)  13.1 us
    ppermute x6, starting transfers between devices, both(): return (came, lax.ppermute(came, 'sector', cores))  12.2 us
    ppermute x6, starting transfers between devices, fetched(): return lax.ppermute(send, 'sector', pairs)  10 us
    pallas_call x4, Pallas kernels, chip_merge(): pl.pallas_call(functools.partial(chip_kernel, level), out_shape=(jax.Shap...  7.84 us
    ppermute x1, waiting for transfers between devices, per_device(): lax.ppermute(own[:, sectors - 1], 'sector', [(i, i + 1) for i in range(co...  5.76 us
  transfers between devices with their start and end apart: 16, of which 10 were waited for; matrix products, arithmetic and copies ran while one was open for 0% of the time, Pallas kernels for 1%

profile of v1, /device:TPU:16, one launch (start us, length us, event | category | flops | bytes accessed | tf_op | source)
XLA Modules:
  0.0 206.8 jit_solution(9503109947437943098)
XLA Ops:
  0.6 1.2 copy.12
  1.9 0.2 copy.9
  2.1 27.6 %all_to_all.15.own_ref = bf16[8,2,32,512]{3,2,1,0:T(8,128)(2,1)S(1)} all-to-all(bf16[8,2,32,512]{3,2,1,0:T(8,128)(2,1)S(1)} %copy.9), channel_id=1, replica_groups=mesh['sector'=64,'chan'=8] {'chan'}, dimensions={0} | all-to-all | bytes 1048576 | tf_op jit(solution)/shard_map/all_to_all | solution.py:354
  29.7 1.9 collective-permute-start
  31.6 5.8 %collective-permute-done.before_ref = bf16[8,32,512]{2,1,0:T(8,128)(2,1)S(1)} collective-permute-done((bf16[8,32,512]{2,1,0:T(8,128)(2,1)S(1)}, bf16[8,32,512]{2,1,0:T(8,128)(2,1)S(1)}, u32[]{:S(2)}, u32[]{:S(2)}) %collective-permute-start) | collective-permute-done | bytes 262176 | tf_op jit(solution)/shard_map/ppermute | solution.py:402
  37.4 1.1 margin_parts.1
  38.5 3.5 %all-to-all-start.1 = ((f32[8,2,32,256]{3,2,1,0:T(8,128)}), f32[8,2,32,256]{3,2,1,0:T(8,128)S(1)}, u32[]{:S(2)}, u32[]{:S(2)}) async-start(f32[8,2,32,256]{3,2,1,0:T(8,128)} %margin_parts.1), calls=%async_computation.1 | async-start | bytes 1048576 | tf_op jit(solution)/shard_map/all_to_all | solution.py:354
  42.1 0.0 copy-start.4
  42.1 0.1 stack.46.flags_ref
  42.2 0.6 copy-done.4
  42.8 0.0 copy-start.1
  42.8 16.3 %all-to-all-done.1.partial_ref = f32[8,2,32,256]{3,2,1,0:T(8,128)S(1)} async-done(((f32[8,2,32,256]{3,2,1,0:T(8,128)}), f32[8,2,32,256]{3,2,1,0:T(8,128)S(1)}, u32[]{:S(2)}, u32[]{:S(2)}) %all-to-all-start.1) | async-done | bytes 524320 | tf_op jit(solution)/shard_map/all_to_all | solution.py:354
  59.1 0.0 copy-start
  59.1 19.3 %all_to_all.16.margin_ref = f32[8,2,32,256]{3,2,1,0:T(8,128)S(1)} all-to-all(f32[8,2,32,256]{3,2,1,0:T(8,128)S(1)} %total_for_all.1), channel_id=1, replica_groups=mesh['sector'=64,'chan'=8] {'chan'}, dimensions={0} | all-to-all | bytes 1048576 | tf_op jit(solution)/shard_map/all_to_all | solution.py:354
  78.5 0.0 copy-done
  78.5 5.8 %leaf.1.own_ref = f32[3,256,256]{2,1,0:T(8,128)S(1)} custom-call(s32[14]{0:T(128)S(1)} %stack.46.flags_ref, f32[8,2,32,256]{3,2,1,0:T(8,128)S(1)} %all_to_all.16.margin_ref, f32[2,256]{1,0:T(2,128)S(1)} %get-tuple-element.23.cot_ref, f32[2,256]{1,0:T(2,128)S(1)} %get-tuple-element.24.csc_ref, bf16[2,256,256]{2,1,0:T(8,128)(2,1)S(1)} %copy-done), custom_call_target="tpu_custom_call" | custom-call | tf_op jit(solution)/shard_map/leaf/pallas_call | solution.py:149
  84.2 1.9 collective-permute-start.1
  86.2 2.3 %collective-permute-done.1.other_ref = f32[3,256,256]{2,1,0:T(8,128)S(1)} collective-permute-done((f32[3,256,256]{2,1,0:T(8,128)S(1)}, f32[3,256,256]{2,1,0:T(8,128)S(1)}, u32[]{:S(2)}, u32[]{:S(2)}) %collective-permute-start.1) | collective-permute-done | bytes 786464 | tf_op jit(solution)/shard_map/ppermute | solution.py:410
  88.4 4.8 %core_merge.1 = (f32[3,256,256]{2,1,0:T(8,128)S(1)}, f32[264,256]{1,0:T(8,128)S(1)}) custom-call(s32[14]{0:T(128)S(1)} %stack.46.flags_ref, f32[3,256,256]{2,1,0:T(8,128)S(1)} %leaf.1.own_ref, f32[3,256,256]{2,1,0:T(8,128)S(1)} %collective-permute-done.1.other_ref), custom_call_target="tpu_custom_call" | custom-call | tf_op jit(solution)/shard_map/core_merge/pallas_call | solution.py:176
  93.3 6.0 %collective-permute-start.2 = (f32[264,256]{1,0:T(8,128)S(1)}, f32[264,256]{1,0:T(8,128)S(1)}, u32[]{:S(2)}, u32[]{:S(2)}) collective-permute-start(f32[264,256]{1,0:T(8,128)S(1)} %get-tuple-element.26), channel_id=1, source_target_pairs={{16,0},{24,8},{0,16},{8,24},{48,32},{56,40},{32,48},{40,56},{80,64... | collective-permute-start | bytes 811016 | tf_op jit(solution)/shard_map/ppermute | solution.py:417
  99.2 6.8 %collective-permute-done.2.came_ref = f32[264,256]{1,0:T(8,128)S(1)} collective-permute-done((f32[264,256]{1,0:T(8,128)S(1)}, f32[264,256]{1,0:T(8,128)S(1)}, u32[]{:S(2)}, u32[]{:S(2)}) %collective-permute-start.2) | collective-permute-done | bytes 270368 | tf_op jit(solution)/shard_map/ppermute | solution.py:417
  106.0 1.9 collective-permute-start.3
  107.9 1.5 collective-permute-done.3.swapped_ref
  109.4 5.1 %chip_merge.4 = (f32[3,256,256]{2,1,0:T(8,128)S(1)}, f32[264,256]{1,0:T(8,128)S(1)}) custom-call(s32[14]{0:T(128)S(1)} %stack.46.flags_ref, f32[3,256,256]{2,1,0:T(8,128)S(1)} %get-tuple-element.25.own_ref, f32[264,256]{1,0:T(8,128)S(1)} %collective-permute-done.2.came_ref, f32[264,256]{1,0:T(8,128)S(1)} %collective-permute-done.3.swapped_ref), custom_call_target="tpu_custom_call" | custom-call | tf_op jit(solution)/shard_map/chip_merge/pallas_call | solution.py:218
  114.6 1.3 collective-permute-start.4
  115.9 6.3 %collective-permute-done.4.came_ref = f32[264,256]{1,0:T(8,128)S(1)} collective-permute-done((f32[264,256]{1,0:T(8,128)S(1)}, f32[264,256]{1,0:T(8,128)S(1)}, u32[]{:S(2)}, u32[]{:S(2)}) %collective-permute-start.4) | collective-permute-done | bytes 270368 | tf_op jit(solution)/shard_map/ppermute | solution.py:417
  122.2 1.9 collective-permute-start.5
  124.1 1.5 collective-permute-done.5.swapped_ref
  125.6 0.8 chip_merge.5
  126.4 0.7 collective-permute-start.6
  127.1 0.0 collective-permute-done.6.came_ref
  127.1 2.0 collective-permute-start.7
  129.2 1.4 collective-permute-done.7.swapped_ref
  130.5 0.6 chip_merge.6
  131.2 0.7 collective-permute-start.8
  131.9 0.7 collective-permute-start.10
  132.5 0.7 collective-permute-start.12
  133.2 0.0 collective-permute-done.8.came_ref
  133.2 2.0 collective-permute-start.9
  135.3 0.0 collective-permute-done.10.came_ref
  135.3 2.3 %collective-permute-start.11 = (f32[264,256]{1,0:T(8,128)S(1)}, f32[264,256]{1,0:T(8,128)S(1)}, u32[]{:S(2)}, u32[]{:S(2)}) collective-permute-start(f32[264,256]{1,0:T(8,128)S(1)} %collective-permute-done.10.came_ref), channel_id=1, source_target_pairs={{0,8},{8,0},{16,24},{24,16},{32,40},{40,32},{48,56},{56,48},{64,72... | collective-permute-start | bytes 811016 | tf_op jit(solution)/shard_map/ppermute | solution.py:420
  137.6 0.0 collective-permute-done.12.came2_ref
  137.6 2.0 collective-permute-start.13
  139.7 0.0 collective-permute-done.9.swapped_ref
  139.7 1.3 chip_merge.7
  141.0 0.0 collective-permute-done.11.swapped_ref
  141.0 0.1 collective-permute-done.13.swapped2_ref
  141.0 0.8 pair_merge.1.other_ref
  141.8 0.0 copy-done.1
  141.8 0.6 last_merge.1
  142.4 0.0 copy-start.2
  142.4 0.6 copy-done.2
  143.0 1.3 collective-permute-start.14
  144.3 60.6 %collective-permute-done.14.brought_ref = f32[3,4,32]{2,1,0:T(4,128)S(1)} collective-permute-done((f32[3,4,32]{2,1,0:T(4,128)S(1)}, f32[3,4,32]{2,1,0:T(4,128)S(1)}, u32[]{:S(2)}, u32[]{:S(2)}) %collective-permute-start.14) | collective-permute-done | bytes 1568 | tf_op jit(solution)/shard_map/ppermute | solution.py:435
  204.9 0.0 copy-start.3
  204.9 0.6 copy-done.3
  205.5 1.3 pick.1
  (4 shorter events, 0.1 us)
Async XLA Ops:
  29.7 7.7 %collective-permute-start = (bf16[8,32,512]{2,1,0:T(8,128)(2,1)S(1)}, bf16[8,32,512]{2,1,0:T(8,128)(2,1)S(1)}, u32[]{:S(2)}, u32[]{:S(2)}) collective-permute-start(bf16[8,32,512]{2,1,0:T(8,128)(2,1)S(1)} %slice_bitcast_fusion), channel_id=1, source_target_pairs={{0,8},{8,16},{16,24},{24,32},{32,40},{40,48},{48,56},{56,64},{64,7... | collective-permute-start | bytes 786440 | tf_op jit(solution)/shard_map/ppermute | solution.py:402
  38.5 20.6 %all-to-all-start.1 = ((f32[8,2,32,256]{3,2,1,0:T(8,128)}), f32[8,2,32,256]{3,2,1,0:T(8,128)S(1)}, u32[]{:S(2)}, u32[]{:S(2)}) async-start(f32[8,2,32,256]{3,2,1,0:T(8,128)} %margin_parts.1), calls=%async_computation.1 | async-start | bytes 1048576 | tf_op jit(solution)/shard_map/all_to_all | solution.py:354
  42.1 0.7 copy-start.4
  42.8 99.1 %copy-start.1 = (s32[14]{0:T(128)}, s32[14]{0:T(128)S(1)}, u32[]{:S(2)}) copy-start(s32[14]{0:T(128)S(1)} %stack.46.flags_ref) | copy-start | bytes 172
  59.1 19.3 %copy-start = (bf16[2,256,256]{2,1,0:T(8,128)(2,1)S(1)}, bf16[2,256,256]{2,1,0:T(8,128)(2,1)}, u32[]{:S(2)}) copy-start(bf16[2,256,256]{2,1,0:T(8,128)(2,1)} %coupling_ref.1) | copy-start | bytes 786436
  84.2 4.2 %collective-permute-start.1 = (f32[3,256,256]{2,1,0:T(8,128)S(1)}, f32[3,256,256]{2,1,0:T(8,128)S(1)}, u32[]{:S(2)}, u32[]{:S(2)}) collective-permute-start(f32[3,256,256]{2,1,0:T(8,128)S(1)} %leaf.1.own_ref), channel_id=1, source_target_pairs={{0,8},{8,0},{16,24},{24,16},{32,40},{40,32},{48,56},{56,48},{64,72... | collective-permute-start | bytes 2359304 | tf_op jit(solution)/shard_map/ppermute | solution.py:410
  93.3 12.8 %collective-permute-start.2 = (f32[264,256]{1,0:T(8,128)S(1)}, f32[264,256]{1,0:T(8,128)S(1)}, u32[]{:S(2)}, u32[]{:S(2)}) collective-permute-start(f32[264,256]{1,0:T(8,128)S(1)} %get-tuple-element.26), channel_id=1, source_target_pairs={{16,0},{24,8},{0,16},{8,24},{48,32},{56,40},{32,48},{40,56},{80,64... | collective-permute-start | bytes 811016 | tf_op jit(solution)/shard_map/ppermute | solution.py:417
  106.0 3.4 %collective-permute-start.3 = (f32[264,256]{1,0:T(8,128)S(1)}, f32[264,256]{1,0:T(8,128)S(1)}, u32[]{:S(2)}, u32[]{:S(2)}) collective-permute-start(f32[264,256]{1,0:T(8,128)S(1)} %collective-permute-done.2.came_ref), channel_id=1, source_target_pairs={{0,8},{8,0},{16,24},{24,16},{32,40},{40,32},{48,56},{56,48},{64,72... | collective-permute-start | bytes 811016 | tf_op jit(solution)/shard_map/ppermute | solution.py:420
  114.6 7.6 %collective-permute-start.4 = (f32[264,256]{1,0:T(8,128)S(1)}, f32[264,256]{1,0:T(8,128)S(1)}, u32[]{:S(2)}, u32[]{:S(2)}) collective-permute-start(f32[264,256]{1,0:T(8,128)S(1)} %get-tuple-element.28), channel_id=1, source_target_pairs={{32,0},{40,8},{16,48},{24,56},{96,64},{104,72},{80,112},{88,120},{... | collective-permute-start | bytes 811016 | tf_op jit(solution)/shard_map/ppermute | solution.py:417
  122.2 3.4 %collective-permute-start.5 = (f32[264,256]{1,0:T(8,128)S(1)}, f32[264,256]{1,0:T(8,128)S(1)}, u32[]{:S(2)}, u32[]{:S(2)}) collective-permute-start(f32[264,256]{1,0:T(8,128)S(1)} %collective-permute-done.4.came_ref), channel_id=1, source_target_pairs={{0,8},{8,0},{16,24},{24,16},{32,40},{40,32},{48,56},{56,48},{64,72... | collective-permute-start | bytes 811016 | tf_op jit(solution)/shard_map/ppermute | solution.py:420
  126.4 0.7 collective-permute-start.6
  127.1 3.4 %collective-permute-start.7 = (f32[264,256]{1,0:T(8,128)S(1)}, f32[264,256]{1,0:T(8,128)S(1)}, u32[]{:S(2)}, u32[]{:S(2)}) collective-permute-start(f32[264,256]{1,0:T(8,128)S(1)} %collective-permute-done.6.came_ref), channel_id=1, source_target_pairs={{0,8},{8,0},{16,24},{24,16},{32,40},{40,32},{48,56},{56,48},{64,72... | collective-permute-start | bytes 811016 | tf_op jit(solution)/shard_map/ppermute | solution.py:420
  131.2 2.1 collective-permute-start.8
  131.9 3.4 %collective-permute-start.10 = (f32[264,256]{1,0:T(8,128)S(1)}, f32[264,256]{1,0:T(8,128)S(1)}, u32[]{:S(2)}, u32[]{:S(2)}) collective-permute-start(f32[264,256]{1,0:T(8,128)S(1)} %get-tuple-element.32), channel_id=1, source_target_pairs={{256,0},{264,8},{304,48},{312,56},{320,64},{328,72},{368,112},{376... | collective-permute-start | bytes 811016 | tf_op jit(solution)/shard_map/ppermute | solution.py:417
  132.5 5.1 %collective-permute-start.12 = (f32[264,256]{1,0:T(8,128)S(1)}, f32[264,256]{1,0:T(8,128)S(1)}, u32[]{:S(2)}, u32[]{:S(2)}) collective-permute-start(f32[264,256]{1,0:T(8,128)S(1)} %get-tuple-element.32), channel_id=1, source_target_pairs={{384,0},{392,8},{432,48},{440,56},{448,64},{456,72},{496,112},{504... | collective-permute-start | bytes 811016 | tf_op jit(solution)/shard_map/ppermute | solution.py:417
  133.2 6.4 %collective-permute-start.9 = (f32[264,256]{1,0:T(8,128)S(1)}, f32[264,256]{1,0:T(8,128)S(1)}, u32[]{:S(2)}, u32[]{:S(2)}) collective-permute-start(f32[264,256]{1,0:T(8,128)S(1)} %collective-permute-done.8.came_ref), channel_id=1, source_target_pairs={{0,8},{8,0},{16,24},{24,16},{32,40},{40,32},{48,56},{56,48},{64,72... | collective-permute-start | bytes 811016 | tf_op jit(solution)/shard_map/ppermute | solution.py:420
  135.3 5.7 %collective-permute-start.11 = (f32[264,256]{1,0:T(8,128)S(1)}, f32[264,256]{1,0:T(8,128)S(1)}, u32[]{:S(2)}, u32[]{:S(2)}) collective-permute-start(f32[264,256]{1,0:T(8,128)S(1)} %collective-permute-done.10.came_ref), channel_id=1, source_target_pairs={{0,8},{8,0},{16,24},{24,16},{32,40},{40,32},{48,56},{56,48},{64,72... | collective-permute-start | bytes 811016 | tf_op jit(solution)/shard_map/ppermute | solution.py:420
  137.6 3.4 %collective-permute-start.13 = (f32[264,256]{1,0:T(8,128)S(1)}, f32[264,256]{1,0:T(8,128)S(1)}, u32[]{:S(2)}, u32[]{:S(2)}) collective-permute-start(f32[264,256]{1,0:T(8,128)S(1)} %collective-permute-done.12.came2_ref), channel_id=1, source_target_pairs={{0,8},{8,0},{16,24},{24,16},{32,40},{40,32},{48,56},{56,48},{64,72... | collective-permute-start | bytes 811016 | tf_op jit(solution)/shard_map/ppermute | solution.py:420
  142.4 0.6 copy-start.2
  143.0 61.9 %collective-permute-start.14 = (f32[3,4,32]{2,1,0:T(4,128)S(1)}, f32[3,4,32]{2,1,0:T(4,128)S(1)}, u32[]{:S(2)}, u32[]{:S(2)}) collective-permute-start(f32[3,4,32]{2,1,0:T(4,128)S(1)} %get-tuple-element.35), channel_id=1, source_target_pairs={{0,16},{8,24},{48,32},{56,40},{64,80},{72,88},{112,96},{120,104},{... | collective-permute-start | bytes 4616 | tf_op jit(solution)/shard_map/ppermute | solution.py:435
  204.9 0.6 copy-start.3

commit v2 on v0

--- a/solution.py
+++ b/solution.py
@@ -270,19 +270,20 @@
     )(flags, own, came, swapped)
 
 
-def pick_kernel(flags_ref, mine_ref, brought_ref, a_ref, b_ref, c_ref):
+def pick_kernel(level, flags_ref, mine_ref, brought_ref, a_ref, b_ref, c_ref):
     for i, ref in enumerate((a_ref, b_ref, c_ref)):
-        ref[...] = jnp.where(flags_ref[0] == 1, mine_ref[i], brought_ref[i])
-
-
-def pick(flag, mine, brought):
-    return pl.pallas_call(
-        pick_kernel,
+        ref[...] = jnp.where(flags_ref[4 + 2 * level] == 1, mine_ref[i], brought_ref[i])
+
+
+def pick(level, flags, mine, brought):
+    return pl.pallas_call(
+        functools.partial(pick_kernel, level),
         out_shape=(jax.ShapeDtypeStruct(mine.shape[1:], F32),) * 3,
         in_specs=[SMEM, VMEM, VMEM],
         out_specs=(VMEM,) * 3,
+        compiler_params=pltpu.CompilerParams(vmem_limit_bytes=2**20),
         name="pick",
-    )(flag, mine, brought)
+    )(flags, mine, brought)
 
 
 def margin_kernel(own_ref, before_ref, out_ref):
@@ -374,12 +375,11 @@
     csc = channel_rates / jnp.sinh(channel_rates * step)
 
     cut = surface_functions.reshape(sectors, rows, shards, points // shards)
-    own = exchange(jnp.transpose(cut, (2, 0, 1, 3)))
+    cut, flags, cot, csc = lax.optimization_barrier((jnp.transpose(cut, (2, 0, 1, 3)), flags, cot, csc))
+    own = exchange(cut)
     before = lax.ppermute(own[:, sectors - 1], "sector", [(i, i + 1) for i in range(count - 1)])
     partial = exchange(margin_parts(own, before))
-    ready = total_for_all(partial, points)
-    ready, flags, cot, csc = lax.optimization_barrier((ready, flags, cot, csc))
-    margin = exchange(ready)
+    margin = exchange(total_for_all(partial, points))
 
     packed = leaf(flags, margin, cot, csc, coupling)
     cores = [(i, i ^ 1) for i in range(count)]
@@ -403,7 +403,7 @@
         if yi not in ENDS:
             pairs.append((spot(xi, yi ^ 1, ci), i))
     brought = lax.ppermute(for_next, "sector", pairs)
-    return tuple(block.T for block in pick(at_end.astype(jnp.int32)[None], mine, brought))
+    return tuple(block.T for block in pick(len(plan) - 1, flags, mine, brought))
 
 
 def solution(mesh):

time: 204 us -> 201 us (0.985)
  blocking collectives: 46.9 us -> 65.8 us
  waiting for transfers between devices: 103 us -> 86.8 us
  starting transfers between devices: 27.9 us -> 25.1 us
    all_to_all x2 -> x3, blocking collectives: 46.9 us -> 65.8 us  [exchange(): lax.all_to_all(array, 'chan', split_axis=0, concat_axis=0, tiled=True)]
    all_to_all x1 -> x0, waiting for transfers between devices: 16.3 us -> none  [exchange(): lax.all_to_all(array, 'chan', split_axis=0, concat_axis=0, tiled=True)]
    all_to_all x1 -> x0, starting transfers between devices: 3.49 us -> none  [exchange(): lax.all_to_all(array, 'chan', split_axis=0, concat_axis=0, tiled=True)]
  transfers between devices with their start and end apart: 14 -> 13, of which waited for: 11 -> 10; matrix products, arithmetic and copies ran while one was open for 0% -> 0% of each run, Pallas kernels for 0% -> 0%
where the time goes in v2:
time: 201 us
  waiting for transfers between devices  86.8 us (43%)
  blocking collectives  65.8 us (33%)
  starting transfers between devices  25.1 us (12%)
  Pallas kernels  20 us (10%)
  local copies, waits for them, and re-layouts  2.2 us (1%)
    all_to_all x3, blocking collectives, exchange(): lax.all_to_all(array, 'chan', split_axis=0, concat_axis=0, tiled=True)  65.8 us
    ppermute x1, waiting for transfers between devices, per_device(): brought = lax.ppermute(for_next, 'sector', pairs)  58.5 us
    ppermute x5, waiting for transfers between devices, per_device(): came = lax.ppermute(send, 'sector', pairs)  13.1 us
    ppermute x5, starting transfers between devices, per_device(): came = lax.ppermute(send, 'sector', pairs)  10 us
    ppermute x5, starting transfers between devices, per_device(): swapped = lax.ppermute(came, 'sector', cores)  9.95 us
    ppermute x5, waiting for transfers between devices, per_device(): swapped = lax.ppermute(came, 'sector', cores)  7.19 us
    pallas_call x4, Pallas kernels, chip_merge(): pl.pallas_call(functools.partial(chip_kernel, level), out_shape=(jax.Shap...  7.14 us
    ppermute x1, waiting for transfers between devices, per_device(): lax.ppermute(own[:, sectors - 1], 'sector', [(i, i + 1) for i in range(co...  5.76 us
  transfers between devices with their start and end apart: 13, of which 10 were waited for; matrix products, arithmetic and copies ran while one was open for 0% of the time, Pallas kernels for 0%

profile of v2, /device:TPU:22, one launch (start us, length us, event | category | flops | bytes accessed | tf_op | source)
XLA Modules:
  0.0 200.8 jit_solution(5229940281210863905)
XLA Ops:
  0.7 0.0 copy-start.1
  0.7 0.7 copy-done.1
  1.4 1.2 copy.12
  2.7 0.1 stack.46.flags_ref
  2.8 0.2 copy.9
  2.9 27.6 %all_to_all.15.own_ref = bf16[8,2,32,512]{3,2,1,0:T(8,128)(2,1)S(1)} all-to-all(bf16[8,2,32,512]{3,2,1,0:T(8,128)(2,1)S(1)} %copy.9), channel_id=1, replica_groups=mesh['sector'=64,'chan'=8] {'chan'}, dimensions={0} | all-to-all | bytes 1048576 | tf_op jit(solution)/shard_map/all_to_all | solution.py:331
  30.6 1.9 collective-permute-start
  32.5 5.8 %collective-permute-done.before_ref = bf16[8,32,512]{2,1,0:T(8,128)(2,1)S(1)} collective-permute-done((bf16[8,32,512]{2,1,0:T(8,128)(2,1)S(1)}, bf16[8,32,512]{2,1,0:T(8,128)(2,1)S(1)}, u32[]{:S(2)}, u32[]{:S(2)}) %collective-permute-start) | collective-permute-done | bytes 262176 | tf_op jit(solution)/shard_map/ppermute | solution.py:380
  38.3 0.3 margin_parts.1
  38.6 19.6 %all_to_all.16.partial_ref = f32[8,2,32,256]{3,2,1,0:T(8,128)S(1)} all-to-all(f32[8,2,32,256]{3,2,1,0:T(8,128)S(1)} %margin_parts.1), channel_id=1, replica_groups=mesh['sector'=64,'chan'=8] {'chan'}, dimensions={0} | all-to-all | bytes 1048576 | tf_op jit(solution)/shard_map/all_to_all | solution.py:331
  58.2 0.0 copy-start
  58.2 18.6 %all_to_all.17.margin_ref = f32[8,2,32,256]{3,2,1,0:T(8,128)S(1)} all-to-all(f32[8,2,32,256]{3,2,1,0:T(8,128)S(1)} %total_for_all.1), channel_id=1, replica_groups=mesh['sector'=64,'chan'=8] {'chan'}, dimensions={0} | all-to-all | bytes 1048576 | tf_op jit(solution)/shard_map/all_to_all | solution.py:331
  76.8 0.0 copy-done
  76.8 5.8 %leaf.1.own_ref = f32[3,256,256]{2,1,0:T(8,128)S(1)} custom-call(s32[14]{0:T(128)S(1)} %stack.46.flags_ref, f32[8,2,32,256]{3,2,1,0:T(8,128)S(1)} %all_to_all.17.margin_ref, f32[2,256]{1,0:T(2,128)S(1)} %get-tuple-element.24.cot_ref, f32[2,256]{1,0:T(2,128)S(1)} %get-tuple-element.25.csc_ref, bf16[2,256,256]{2,1,0:T(8,128)(2,1)S(1)} %copy-done), custom_call_target="tpu_custom_call" | custom-call | tf_op jit(solution)/shard_map/leaf/pallas_call | solution.py:149
  82.6 1.9 collective-permute-start.1
  84.5 2.3 %collective-permute-done.1.other_ref = f32[3,256,256]{2,1,0:T(8,128)S(1)} collective-permute-done((f32[3,256,256]{2,1,0:T(8,128)S(1)}, f32[3,256,256]{2,1,0:T(8,128)S(1)}, u32[]{:S(2)}, u32[]{:S(2)}) %collective-permute-start.1) | collective-permute-done | bytes 786464 | tf_op jit(solution)/shard_map/ppermute | solution.py:386
  86.7 4.8 %core_merge.1 = (f32[3,256,256]{2,1,0:T(8,128)S(1)}, f32[264,256]{1,0:T(8,128)S(1)}) custom-call(s32[14]{0:T(128)S(1)} %stack.46.flags_ref, f32[3,256,256]{2,1,0:T(8,128)S(1)} %leaf.1.own_ref, f32[3,256,256]{2,1,0:T(8,128)S(1)} %collective-permute-done.1.other_ref), custom_call_target="tpu_custom_call" | custom-call | tf_op jit(solution)/shard_map/core_merge/pallas_call | solution.py:176
  91.6 6.7 %collective-permute-start.2 = (f32[264,256]{1,0:T(8,128)S(1)}, f32[264,256]{1,0:T(8,128)S(1)}, u32[]{:S(2)}, u32[]{:S(2)}) collective-permute-start(f32[264,256]{1,0:T(8,128)S(1)} %get-tuple-element.27), channel_id=1, source_target_pairs={{16,0},{24,8},{0,16},{8,24},{48,32},{56,40},{32,48},{40,56},{80,64... | collective-permute-start | bytes 811016 | tf_op jit(solution)/shard_map/ppermute | solution.py:394
  98.3 6.8 %collective-permute-done.2.came_ref = f32[264,256]{1,0:T(8,128)S(1)} collective-permute-done((f32[264,256]{1,0:T(8,128)S(1)}, f32[264,256]{1,0:T(8,128)S(1)}, u32[]{:S(2)}, u32[]{:S(2)}) %collective-permute-start.2) | collective-permute-done | bytes 270368 | tf_op jit(solution)/shard_map/ppermute | solution.py:394
  105.0 1.9 collective-permute-start.3
  106.9 1.5 collective-permute-done.3.swapped_ref
  108.5 5.1 %chip_merge.4 = (f32[3,256,256]{2,1,0:T(8,128)S(1)}, f32[264,256]{1,0:T(8,128)S(1)}) custom-call(s32[14]{0:T(128)S(1)} %stack.46.flags_ref, f32[3,256,256]{2,1,0:T(8,128)S(1)} %get-tuple-element.26.own_ref, f32[264,256]{1,0:T(8,128)S(1)} %collective-permute-done.2.came_ref, f32[264,256]{1,0:T(8,128)S(1)} %collective-permute-done.3.swapped_ref), custom_call_target="tpu_custom_call" | custom-call | tf_op jit(solution)/shard_map/chip_merge/pallas_call | solution.py:218
  113.6 1.3 collective-permute-start.4
  114.9 6.3 %collective-permute-done.4.came_ref = f32[264,256]{1,0:T(8,128)S(1)} collective-permute-done((f32[264,256]{1,0:T(8,128)S(1)}, f32[264,256]{1,0:T(8,128)S(1)}, u32[]{:S(2)}, u32[]{:S(2)}) %collective-permute-start.4) | collective-permute-done | bytes 270368 | tf_op jit(solution)/shard_map/ppermute | solution.py:394
  121.2 1.9 collective-permute-start.5
  123.1 1.5 collective-permute-done.5.swapped_ref
  124.6 0.8 chip_merge.5
  125.4 0.7 collective-permute-start.6
  126.1 0.0 collective-permute-done.6.came_ref
  126.1 2.0 %collective-permute-start.7 = (f32[264,256]{1,0:T(8,128)S(1)}, f32[264,256]{1,0:T(8,128)S(1)}, u32[]{:S(2)}, u32[]{:S(2)}) collective-permute-start(f32[264,256]{1,0:T(8,128)S(1)} %collective-permute-done.6.came_ref), channel_id=1, source_target_pairs={{0,8},{8,0},{16,24},{24,16},{32,40},{40,32},{48,56},{56,48},{64,72... | collective-permute-start | bytes 811016 | tf_op jit(solution)/shard_map/ppermute | solution.py:395
  128.2 1.4 collective-permute-done.7.swapped_ref
  129.6 0.6 chip_merge.6
  130.2 0.7 collective-permute-start.8
  130.9 0.0 collective-permute-done.8.came_ref
  130.9 2.0 %collective-permute-start.9 = (f32[264,256]{1,0:T(8,128)S(1)}, f32[264,256]{1,0:T(8,128)S(1)}, u32[]{:S(2)}, u32[]{:S(2)}) collective-permute-start(f32[264,256]{1,0:T(8,128)S(1)} %collective-permute-done.8.came_ref), channel_id=1, source_target_pairs={{0,8},{8,0},{16,24},{24,16},{32,40},{40,32},{48,56},{56,48},{64,72... | collective-permute-start | bytes 811016 | tf_op jit(solution)/shard_map/ppermute | solution.py:395
  132.9 1.4 collective-permute-done.9.swapped_ref
  134.3 0.6 chip_merge.7
  134.9 0.7 collective-permute-start.10
  135.6 0.0 collective-permute-done.10.came_ref
  135.6 2.0 %collective-permute-start.11 = (f32[264,256]{1,0:T(8,128)S(1)}, f32[264,256]{1,0:T(8,128)S(1)}, u32[]{:S(2)}, u32[]{:S(2)}) collective-permute-start(f32[264,256]{1,0:T(8,128)S(1)} %collective-permute-done.10.came_ref), channel_id=1, source_target_pairs={{0,8},{8,0},{16,24},{24,16},{32,40},{40,32},{48,56},{56,48},{64,72... | collective-permute-start | bytes 811016 | tf_op jit(solution)/shard_map/ppermute | solution.py:395
  137.7 1.4 collective-permute-done.11.swapped_ref
  139.1 0.8 last_merge.1
  139.9 1.3 collective-permute-start.12
  141.2 58.5 %collective-permute-done.12.brought_ref = f32[3,4,32]{2,1,0:T(4,128)S(1)} collective-permute-done((f32[3,4,32]{2,1,0:T(4,128)S(1)}, f32[3,4,32]{2,1,0:T(4,128)S(1)}, u32[]{:S(2)}, u32[]{:S(2)}) %collective-permute-start.12) | collective-permute-done | bytes 1568 | tf_op jit(solution)/shard_map/ppermute | solution.py:405
  199.7 1.1 pick.1
  (4 shorter events, 0.1 us)
Async XLA Ops:
  0.7 0.7 copy-start.1
  30.6 7.7 %collective-permute-start = (bf16[8,32,512]{2,1,0:T(8,128)(2,1)S(1)}, bf16[8,32,512]{2,1,0:T(8,128)(2,1)S(1)}, u32[]{:S(2)}, u32[]{:S(2)}) collective-permute-start(bf16[8,32,512]{2,1,0:T(8,128)(2,1)S(1)} %slice_bitcast_fusion), channel_id=1, source_target_pairs={{0,8},{8,16},{16,24},{24,32},{32,40},{40,48},{48,56},{56,64},{64,7... | collective-permute-start | bytes 786440 | tf_op jit(solution)/shard_map/ppermute | solution.py:380
  58.2 18.6 %copy-start = (bf16[2,256,256]{2,1,0:T(8,128)(2,1)S(1)}, bf16[2,256,256]{2,1,0:T(8,128)(2,1)}, u32[]{:S(2)}) copy-start(bf16[2,256,256]{2,1,0:T(8,128)(2,1)} %coupling_ref.1) | copy-start | bytes 786436
  82.6 4.2 %collective-permute-start.1 = (f32[3,256,256]{2,1,0:T(8,128)S(1)}, f32[3,256,256]{2,1,0:T(8,128)S(1)}, u32[]{:S(2)}, u32[]{:S(2)}) collective-permute-start(f32[3,256,256]{2,1,0:T(8,128)S(1)} %leaf.1.own_ref), channel_id=1, source_target_pairs={{0,8},{8,0},{16,24},{24,16},{32,40},{40,32},{48,56},{56,48},{64,72... | collective-permute-start | bytes 2359304 | tf_op jit(solution)/shard_map/ppermute | solution.py:386
  91.6 13.4 %collective-permute-start.2 = (f32[264,256]{1,0:T(8,128)S(1)}, f32[264,256]{1,0:T(8,128)S(1)}, u32[]{:S(2)}, u32[]{:S(2)}) collective-permute-start(f32[264,256]{1,0:T(8,128)S(1)} %get-tuple-element.27), channel_id=1, source_target_pairs={{16,0},{24,8},{0,16},{8,24},{48,32},{56,40},{32,48},{40,56},{80,64... | collective-permute-start | bytes 811016 | tf_op jit(solution)/shard_map/ppermute | solution.py:394
  105.0 3.4 %collective-permute-start.3 = (f32[264,256]{1,0:T(8,128)S(1)}, f32[264,256]{1,0:T(8,128)S(1)}, u32[]{:S(2)}, u32[]{:S(2)}) collective-permute-start(f32[264,256]{1,0:T(8,128)S(1)} %collective-permute-done.2.came_ref), channel_id=1, source_target_pairs={{0,8},{8,0},{16,24},{24,16},{32,40},{40,32},{48,56},{56,48},{64,72... | collective-permute-start | bytes 811016 | tf_op jit(solution)/shard_map/ppermute | solution.py:395
  113.6 7.6 %collective-permute-start.4 = (f32[264,256]{1,0:T(8,128)S(1)}, f32[264,256]{1,0:T(8,128)S(1)}, u32[]{:S(2)}, u32[]{:S(2)}) collective-permute-start(f32[264,256]{1,0:T(8,128)S(1)} %get-tuple-element.29), channel_id=1, source_target_pairs={{32,0},{40,8},{16,48},{24,56},{96,64},{104,72},{80,112},{88,120},{... | collective-permute-start | bytes 811016 | tf_op jit(solution)/shard_map/ppermute | solution.py:394
  121.2 3.4 %collective-permute-start.5 = (f32[264,256]{1,0:T(8,128)S(1)}, f32[264,256]{1,0:T(8,128)S(1)}, u32[]{:S(2)}, u32[]{:S(2)}) collective-permute-start(f32[264,256]{1,0:T(8,128)S(1)} %collective-permute-done.4.came_ref), channel_id=1, source_target_pairs={{0,8},{8,0},{16,24},{24,16},{32,40},{40,32},{48,56},{56,48},{64,72... | collective-permute-start | bytes 811016 | tf_op jit(solution)/shard_map/ppermute | solution.py:395
  125.4 0.7 collective-permute-start.6
  126.1 3.4 %collective-permute-start.7 = (f32[264,256]{1,0:T(8,128)S(1)}, f32[264,256]{1,0:T(8,128)S(1)}, u32[]{:S(2)}, u32[]{:S(2)}) collective-permute-start(f32[264,256]{1,0:T(8,128)S(1)} %collective-permute-done.6.came_ref), channel_id=1, source_target_pairs={{0,8},{8,0},{16,24},{24,16},{32,40},{40,32},{48,56},{56,48},{64,72... | collective-permute-start | bytes 811016 | tf_op jit(solution)/shard_map/ppermute | solution.py:395
  130.2 0.7 collective-permute-start.8
  130.9 3.4 %collective-permute-start.9 = (f32[264,256]{1,0:T(8,128)S(1)}, f32[264,256]{1,0:T(8,128)S(1)}, u32[]{:S(2)}, u32[]{:S(2)}) collective-permute-start(f32[264,256]{1,0:T(8,128)S(1)} %collective-permute-done.8.came_ref), channel_id=1, source_target_pairs={{0,8},{8,0},{16,24},{24,16},{32,40},{40,32},{48,56},{56,48},{64,72... | collective-permute-start | bytes 811016 | tf_op jit(solution)/shard_map/ppermute | solution.py:395
  134.9 0.7 collective-permute-start.10
  135.6 3.4 %collective-permute-start.11 = (f32[264,256]{1,0:T(8,128)S(1)}, f32[264,256]{1,0:T(8,128)S(1)}, u32[]{:S(2)}, u32[]{:S(2)}) collective-permute-start(f32[264,256]{1,0:T(8,128)S(1)} %collective-permute-done.10.came_ref), channel_id=1, source_target_pairs={{0,8},{8,0},{16,24},{24,16},{32,40},{40,32},{48,56},{56,48},{64,72... | collective-permute-start | bytes 811016 | tf_op jit(solution)/shard_map/ppermute | solution.py:395
  139.9 59.8 %collective-permute-start.12 = (f32[3,4,32]{2,1,0:T(4,128)S(1)}, f32[3,4,32]{2,1,0:T(4,128)S(1)}, u32[]{:S(2)}, u32[]{:S(2)}) collective-permute-start(f32[3,4,32]{2,1,0:T(4,128)S(1)} %get-tuple-element.37), channel_id=1, source_target_pairs={{0,16},{8,24},{48,32},{56,40},{64,80},{72,88},{112,96},{120,104},{... | collective-permute-start | bytes 4616 | tf_op jit(solution)/shard_map/ppermute | solution.py:405

commit v3 on v2

--- a/solution.py
+++ b/solution.py
@@ -14,7 +14,8 @@
 TN = (((0,), (0,)), ((), ()))
 TOLERANCE = 1e-5
 STEPS = 8
-SQUARINGS = (4, 4, 5, 6, 7, 8, 8)
+SQUARINGS = (3, 3, 4, 5, 6, 7, 7)
+WORK = pl.CostEstimate(flops=10**9, bytes_accessed=2 * 10**6, transcendentals=0)
 PARAMS = pltpu.CompilerParams(vmem_limit_bytes=32 * 2**20)
 VMEM = pl.BlockSpec(memory_space=pltpu.VMEM)
 SMEM = pl.BlockSpec(memory_space=pltpu.SMEM)
@@ -76,7 +77,7 @@
 def newton(d_parts, x, dot):
     x_parts = parts(x)
     residual = unit(x.shape[0]) - dot(d_parts, x_parts)
-    return x + dot3(x_parts, parts(residual)), residual
+    return x + (dot1(x_parts[0], residual.astype(BF16)) if dot is dot3 else dot3(x_parts, parts(residual))), residual
 
 
 def combine(left, right, x, out_ref):
@@ -286,25 +287,45 @@
     )(flags, mine, brought)
 
 
-def margin_kernel(own_ref, before_ref, out_ref):
+def inner_kernel(own_ref, out_ref):
     shards, _, rows, depth = own_ref.shape
     n = shards * rows
     first = own_ref[:, 0].reshape(n, depth)
     second = own_ref[:, 1].reshape(n, depth)
-    out_ref[:, 1] = dot1(first, second, NT).reshape(shards, rows, n)
+    out_ref[...] = dot1(first, second, NT).reshape(shards, rows, n)
+
+
+def margin_kernel(own_ref, before_ref, inner_ref, out_ref):
+    shards, _, rows, depth = own_ref.shape
+    n = shards * rows
+    first = own_ref[:, 0].reshape(n, depth)
     out_ref[:, 0] = dot1(before_ref[...].reshape(n, depth), first, NT).reshape(shards, rows, n)
-
-
-def margin_parts(own, before):
+    out_ref[:, 1] = inner_ref[...]
+
+
+def inner_parts(own):
+    shards, _, rows, _ = own.shape
+    return pl.pallas_call(
+        inner_kernel,
+        out_shape=jax.ShapeDtypeStruct((shards, rows, shards * rows), F32),
+        in_specs=[VMEM],
+        out_specs=VMEM,
+        compiler_params=PARAMS,
+        cost_estimate=WORK,
+        name="inner_parts",
+    )(own)
+
+
+def margin_parts(own, before, inner):
     shards, sectors, rows, _ = own.shape
     return pl.pallas_call(
         margin_kernel,
         out_shape=jax.ShapeDtypeStruct((shards, sectors, rows, shards * rows), F32),
-        in_specs=[VMEM, VMEM],
+        in_specs=[VMEM, VMEM, VMEM],
         out_specs=VMEM,
         compiler_params=PARAMS,
         name="margin_parts",
-    )(own, before)
+    )(own, before, inner)
 
 
 def total_kernel(points, partial_ref, out_ref):
@@ -375,10 +396,10 @@
     csc = channel_rates / jnp.sinh(channel_rates * step)
 
     cut = surface_functions.reshape(sectors, rows, shards, points // shards)
-    cut, flags, cot, csc = lax.optimization_barrier((jnp.transpose(cut, (2, 0, 1, 3)), flags, cot, csc))
-    own = exchange(cut)
+    own = exchange(jnp.transpose(cut, (2, 0, 1, 3)))
     before = lax.ppermute(own[:, sectors - 1], "sector", [(i, i + 1) for i in range(count - 1)])
-    partial = exchange(margin_parts(own, before))
+    inner, cot, csc, flags, before = lax.optimization_barrier((inner_parts(own), cot, csc, flags, before))
+    partial = exchange(margin_parts(own, before, inner))
     margin = exchange(total_for_all(partial, points))
 
     packed = leaf(flags, margin, cot, csc, coupling)

time: 201 us -> 199 us (0.990)
  blocking collectives: 65.8 us -> 38.1 us
  waiting for transfers between devices: 86.8 us -> 103 us
  starting transfers between devices: 25.1 us -> 35.4 us
    all_to_all x3 -> x2, blocking collectives: 65.8 us -> 38.1 us  [exchange(): lax.all_to_all(array, 'chan', split_axis=0, concat_axis=0, tiled=True)]
    all_to_all x0 -> x1, waiting for transfers between devices: none -> 17.4 us  [exchange(): lax.all_to_all(array, 'chan', split_axis=0, concat_axis=0, tiled=True)]
    all_to_all x0 -> x1, starting transfers between devices: none -> 10.3 us  [exchange(): lax.all_to_all(array, 'chan', split_axis=0, concat_axis=0, tiled=True)]
  transfers between devices with their start and end apart: 13 -> 14, of which waited for: 10 -> 11; matrix products, arithmetic and copies ran while one was open for 0% -> 0% of each run, Pallas kernels for 0% -> 0%
where the time goes in v3:
time: 199 us
  waiting for transfers between devices  103 us (52%)
  blocking collectives  38.1 us (19%)
  starting transfers between devices  35.4 us (18%)
  Pallas kernels  19.2 us (10%)
  local copies, waits for them, and re-layouts  2.33 us (1%)
    ppermute x1, waiting for transfers between devices, per_device(): brought = lax.ppermute(for_next, 'sector', pairs)  57.2 us
    all_to_all x2, blocking collectives, exchange(): lax.all_to_all(array, 'chan', split_axis=0, concat_axis=0, tiled=True)  38.1 us
    all_to_all x1, waiting for transfers between devices, exchange(): lax.all_to_all(array, 'chan', split_axis=0, concat_axis=0, tiled=True)  17.4 us
    ppermute x5, waiting for transfers between devices, per_device(): came = lax.ppermute(send, 'sector', pairs)  13 us
    all_to_all x1, starting transfers between devices, exchange(): lax.all_to_all(array, 'chan', split_axis=0, concat_axis=0, tiled=True)  10.3 us
    ppermute x5, starting transfers between devices, per_device(): came = lax.ppermute(send, 'sector', pairs)  10 us
    ppermute x5, starting transfers between devices, per_device(): swapped = lax.ppermute(came, 'sector', cores)  9.95 us
    ppermute x5, waiting for transfers between devices, per_device(): swapped = lax.ppermute(came, 'sector', cores)  7.19 us
  transfers between devices with their start and end apart: 14, of which 11 were waited for; matrix products, arithmetic and copies ran while one was open for 0% of the time, Pallas kernels for 0%

profile of v3, /device:TPU:22, one launch (start us, length us, event | category | flops | bytes accessed | tf_op | source)
XLA Modules:
  0.0 198.5 jit_solution(11024409148138372778)
XLA Ops:
  0.6 1.2 copy.14
  1.9 1.0 copy.11
  2.9 10.3 %all-to-all-start = ((bf16[8,2,32,512]{3,2,1,0:T(8,128)(2,1)}), bf16[8,2,32,512]{3,2,1,0:T(8,128)(2,1)S(1)}, u32[]{:S(2)}, u32[]{:S(2)}) async-start(bf16[8,2,32,512]{3,2,1,0:T(8,128)(2,1)} %copy.11), calls=%async_computation | async-start | bytes 1048576 | tf_op jit(solution)/shard_map/all_to_all | solution.py:352
  13.2 0.1 stack.46.flags_ref
  13.3 0.0 copy-start.1
  13.3 17.4 %all-to-all-done.own_ref = bf16[8,2,32,512]{3,2,1,0:T(8,128)(2,1)S(1)} async-done(((bf16[8,2,32,512]{3,2,1,0:T(8,128)(2,1)}), bf16[8,2,32,512]{3,2,1,0:T(8,128)(2,1)S(1)}, u32[]{:S(2)}, u32[]{:S(2)}) %all-to-all-start) | async-done | bytes 524320 | tf_op jit(solution)/shard_map/all_to_all | solution.py:352
  30.7 1.9 collective-permute-start
  32.6 0.0 copy-done.1
  32.7 0.3 inner_parts.1.inner_ref
  32.9 5.4 %collective-permute-done.before_ref = bf16[8,32,512]{2,1,0:T(8,128)(2,1)S(1)} collective-permute-done((bf16[8,32,512]{2,1,0:T(8,128)(2,1)S(1)}, bf16[8,32,512]{2,1,0:T(8,128)(2,1)S(1)}, u32[]{:S(2)}, u32[]{:S(2)}) %collective-permute-start) | collective-permute-done | bytes 262176 | tf_op jit(solution)/shard_map/ppermute | solution.py:400
  38.4 0.3 margin_parts.1
  38.7 19.6 %all_to_all.15.partial_ref = f32[8,2,32,256]{3,2,1,0:T(8,128)S(1)} all-to-all(f32[8,2,32,256]{3,2,1,0:T(8,128)S(1)} %margin_parts.1), channel_id=1, replica_groups=mesh['sector'=64,'chan'=8] {'chan'}, dimensions={0} | all-to-all | bytes 1048576 | tf_op jit(solution)/shard_map/all_to_all | solution.py:352
  58.3 0.0 copy-start
  58.3 18.6 %all_to_all.16.margin_ref = f32[8,2,32,256]{3,2,1,0:T(8,128)S(1)} all-to-all(f32[8,2,32,256]{3,2,1,0:T(8,128)S(1)} %total_for_all.1), channel_id=1, replica_groups=mesh['sector'=64,'chan'=8] {'chan'}, dimensions={0} | all-to-all | bytes 1048576 | tf_op jit(solution)/shard_map/all_to_all | solution.py:352
  76.8 0.0 copy-done
  76.8 5.4 %leaf.1.own_ref = f32[3,256,256]{2,1,0:T(8,128)S(1)} custom-call(s32[14]{0:T(128)S(1)} %stack.46.flags_ref, f32[8,2,32,256]{3,2,1,0:T(8,128)S(1)} %all_to_all.16.margin_ref, f32[2,256]{1,0:T(2,128)S(1)} %get-tuple-element.26.cot_ref, f32[2,256]{1,0:T(2,128)S(1)} %get-tuple-element.27.csc_ref, bf16[2,256,256]{2,1,0:T(8,128)(2,1)S(1)} %copy-done), custom_call_target="tpu_custom_call" | custom-call | tf_op jit(solution)/shard_map/leaf/pallas_call | solution.py:150
  82.2 1.9 collective-permute-start.1
  84.2 2.3 %collective-permute-done.1.other_ref = f32[3,256,256]{2,1,0:T(8,128)S(1)} collective-permute-done((f32[3,256,256]{2,1,0:T(8,128)S(1)}, f32[3,256,256]{2,1,0:T(8,128)S(1)}, u32[]{:S(2)}, u32[]{:S(2)}) %collective-permute-start.1) | collective-permute-done | bytes 786464 | tf_op jit(solution)/shard_map/ppermute | solution.py:407
  86.4 4.5 %core_merge.1 = (f32[3,256,256]{2,1,0:T(8,128)S(1)}, f32[264,256]{1,0:T(8,128)S(1)}) custom-call(s32[14]{0:T(128)S(1)} %stack.46.flags_ref, f32[3,256,256]{2,1,0:T(8,128)S(1)} %leaf.1.own_ref, f32[3,256,256]{2,1,0:T(8,128)S(1)} %collective-permute-done.1.other_ref), custom_call_target="tpu_custom_call" | custom-call | tf_op jit(solution)/shard_map/core_merge/pallas_call | solution.py:177
  90.9 6.7 %collective-permute-start.2 = (f32[264,256]{1,0:T(8,128)S(1)}, f32[264,256]{1,0:T(8,128)S(1)}, u32[]{:S(2)}, u32[]{:S(2)}) collective-permute-start(f32[264,256]{1,0:T(8,128)S(1)} %get-tuple-element.29), channel_id=1, source_target_pairs={{16,0},{24,8},{0,16},{8,24},{48,32},{56,40},{32,48},{40,56},{80,64... | collective-permute-start | bytes 811016 | tf_op jit(solution)/shard_map/ppermute | solution.py:415
  97.6 6.8 %collective-permute-done.2.came_ref = f32[264,256]{1,0:T(8,128)S(1)} collective-permute-done((f32[264,256]{1,0:T(8,128)S(1)}, f32[264,256]{1,0:T(8,128)S(1)}, u32[]{:S(2)}, u32[]{:S(2)}) %collective-permute-start.2) | collective-permute-done | bytes 270368 | tf_op jit(solution)/shard_map/ppermute | solution.py:415
  104.4 1.9 collective-permute-start.3
  106.3 1.5 collective-permute-done.3.swapped_ref
  107.8 4.8 %chip_merge.4 = (f32[3,256,256]{2,1,0:T(8,128)S(1)}, f32[264,256]{1,0:T(8,128)S(1)}) custom-call(s32[14]{0:T(128)S(1)} %stack.46.flags_ref, f32[3,256,256]{2,1,0:T(8,128)S(1)} %get-tuple-element.28.own_ref, f32[264,256]{1,0:T(8,128)S(1)} %collective-permute-done.2.came_ref, f32[264,256]{1,0:T(8,128)S(1)} %collective-permute-done.3.swapped_ref), custom_call_target="tpu_custom_call" | custom-call | tf_op jit(solution)/shard_map/chip_merge/pallas_call | solution.py:219
  112.6 1.3 collective-permute-start.4
  113.9 6.3 %collective-permute-done.4.came_ref = f32[264,256]{1,0:T(8,128)S(1)} collective-permute-done((f32[264,256]{1,0:T(8,128)S(1)}, f32[264,256]{1,0:T(8,128)S(1)}, u32[]{:S(2)}, u32[]{:S(2)}) %collective-permute-start.4) | collective-permute-done | bytes 270368 | tf_op jit(solution)/shard_map/ppermute | solution.py:415
  120.2 1.9 collective-permute-start.5
  122.1 1.5 collective-permute-done.5.swapped_ref
  123.6 0.8 chip_merge.5
  124.4 0.7 collective-permute-start.6
  125.1 0.0 collective-permute-done.6.came_ref
  125.1 2.0 %collective-permute-start.7 = (f32[264,256]{1,0:T(8,128)S(1)}, f32[264,256]{1,0:T(8,128)S(1)}, u32[]{:S(2)}, u32[]{:S(2)}) collective-permute-start(f32[264,256]{1,0:T(8,128)S(1)} %collective-permute-done.6.came_ref), channel_id=1, source_target_pairs={{0,8},{8,0},{16,24},{24,16},{32,40},{40,32},{48,56},{56,48},{64,72... | collective-permute-start | bytes 811016 | tf_op jit(solution)/shard_map/ppermute | solution.py:416
  127.2 1.4 collective-permute-done.7.swapped_ref
  128.6 0.6 chip_merge.6
  129.2 0.7 collective-permute-start.8
  129.9 0.0 collective-permute-done.8.came_ref
  129.9 2.0 %collective-permute-start.9 = (f32[264,256]{1,0:T(8,128)S(1)}, f32[264,256]{1,0:T(8,128)S(1)}, u32[]{:S(2)}, u32[]{:S(2)}) collective-permute-start(f32[264,256]{1,0:T(8,128)S(1)} %collective-permute-done.8.came_ref), channel_id=1, source_target_pairs={{0,8},{8,0},{16,24},{24,16},{32,40},{40,32},{48,56},{56,48},{64,72... | collective-permute-start | bytes 811016 | tf_op jit(solution)/shard_map/ppermute | solution.py:416
  132.0 1.4 collective-permute-done.9.swapped_ref
  133.3 0.6 chip_merge.7
  134.0 0.7 collective-permute-start.10
  134.7 0.0 collective-permute-done.10.came_ref
  134.7 2.0 %collective-permute-start.11 = (f32[264,256]{1,0:T(8,128)S(1)}, f32[264,256]{1,0:T(8,128)S(1)}, u32[]{:S(2)}, u32[]{:S(2)}) collective-permute-start(f32[264,256]{1,0:T(8,128)S(1)} %collective-permute-done.10.came_ref), channel_id=1, source_target_pairs={{0,8},{8,0},{16,24},{24,16},{32,40},{40,32},{48,56},{56,48},{64,72... | collective-permute-start | bytes 811016 | tf_op jit(solution)/shard_map/ppermute | solution.py:416
  136.7 1.4 collective-permute-done.11.swapped_ref
  138.1 0.8 last_merge.1
  138.9 1.3 collective-permute-start.12
  140.2 57.2 %collective-permute-done.12.brought_ref = f32[3,4,32]{2,1,0:T(4,128)S(1)} collective-permute-done((f32[3,4,32]{2,1,0:T(4,128)S(1)}, f32[3,4,32]{2,1,0:T(4,128)S(1)}, u32[]{:S(2)}, u32[]{:S(2)}) %collective-permute-start.12) | collective-permute-done | bytes 1568 | tf_op jit(solution)/shard_map/ppermute | solution.py:426
  197.4 1.1 pick.1
  (4 shorter events, 0.1 us)
Async XLA Ops:
  2.9 27.8 %all-to-all-start = ((bf16[8,2,32,512]{3,2,1,0:T(8,128)(2,1)}), bf16[8,2,32,512]{3,2,1,0:T(8,128)(2,1)S(1)}, u32[]{:S(2)}, u32[]{:S(2)}) async-start(bf16[8,2,32,512]{3,2,1,0:T(8,128)(2,1)} %copy.11), calls=%async_computation | async-start | bytes 1048576 | tf_op jit(solution)/shard_map/all_to_all | solution.py:352
  13.3 19.4 %copy-start.1 = (f32[2,256]{1,0:T(2,128)S(1)}, f32[2,256]{1,0:T(2,128)}, u32[]{:S(2)}) copy-start(f32[2,256]{1,0:T(2,128)} %param.4) | copy-start | bytes 6148
  30.7 7.7 %collective-permute-start = (bf16[8,32,512]{2,1,0:T(8,128)(2,1)S(1)}, bf16[8,32,512]{2,1,0:T(8,128)(2,1)S(1)}, u32[]{:S(2)}, u32[]{:S(2)}) collective-permute-start(bf16[8,32,512]{2,1,0:T(8,128)(2,1)S(1)} %slice_bitcast_fusion), channel_id=1, source_target_pairs={{0,8},{8,16},{16,24},{24,32},{32,40},{40,48},{48,56},{56,64},{64,7... | collective-permute-start | bytes 786440 | tf_op jit(solution)/shard_map/ppermute | solution.py:400
  58.3 18.6 %copy-start = (bf16[2,256,256]{2,1,0:T(8,128)(2,1)S(1)}, bf16[2,256,256]{2,1,0:T(8,128)(2,1)}, u32[]{:S(2)}) copy-start(bf16[2,256,256]{2,1,0:T(8,128)(2,1)} %coupling_ref.1) | copy-start | bytes 786436
  82.2 4.2 %collective-permute-start.1 = (f32[3,256,256]{2,1,0:T(8,128)S(1)}, f32[3,256,256]{2,1,0:T(8,128)S(1)}, u32[]{:S(2)}, u32[]{:S(2)}) collective-permute-start(f32[3,256,256]{2,1,0:T(8,128)S(1)} %leaf.1.own_ref), channel_id=1, source_target_pairs={{0,8},{8,0},{16,24},{24,16},{32,40},{40,32},{48,56},{56,48},{64,72... | collective-permute-start | bytes 2359304 | tf_op jit(solution)/shard_map/ppermute | solution.py:407
  90.9 13.5 %collective-permute-start.2 = (f32[264,256]{1,0:T(8,128)S(1)}, f32[264,256]{1,0:T(8,128)S(1)}, u32[]{:S(2)}, u32[]{:S(2)}) collective-permute-start(f32[264,256]{1,0:T(8,128)S(1)} %get-tuple-element.29), channel_id=1, source_target_pairs={{16,0},{24,8},{0,16},{8,24},{48,32},{56,40},{32,48},{40,56},{80,64... | collective-permute-start | bytes 811016 | tf_op jit(solution)/shard_map/ppermute | solution.py:415
  104.4 3.4 %collective-permute-start.3 = (f32[264,256]{1,0:T(8,128)S(1)}, f32[264,256]{1,0:T(8,128)S(1)}, u32[]{:S(2)}, u32[]{:S(2)}) collective-permute-start(f32[264,256]{1,0:T(8,128)S(1)} %collective-permute-done.2.came_ref), channel_id=1, source_target_pairs={{0,8},{8,0},{16,24},{24,16},{32,40},{40,32},{48,56},{56,48},{64,72... | collective-permute-start | bytes 811016 | tf_op jit(solution)/shard_map/ppermute | solution.py:416
  112.6 7.6 %collective-permute-start.4 = (f32[264,256]{1,0:T(8,128)S(1)}, f32[264,256]{1,0:T(8,128)S(1)}, u32[]{:S(2)}, u32[]{:S(2)}) collective-permute-start(f32[264,256]{1,0:T(8,128)S(1)} %get-tuple-element.31), channel_id=1, source_target_pairs={{32,0},{40,8},{16,48},{24,56},{96,64},{104,72},{80,112},{88,120},{... | collective-permute-start | bytes 811016 | tf_op jit(solution)/shard_map/ppermute | solution.py:415
  120.2 3.4 %collective-permute-start.5 = (f32[264,256]{1,0:T(8,128)S(1)}, f32[264,256]{1,0:T(8,128)S(1)}, u32[]{:S(2)}, u32[]{:S(2)}) collective-permute-start(f32[264,256]{1,0:T(8,128)S(1)} %collective-permute-done.4.came_ref), channel_id=1, source_target_pairs={{0,8},{8,0},{16,24},{24,16},{32,40},{40,32},{48,56},{56,48},{64,72... | collective-permute-start | bytes 811016 | tf_op jit(solution)/shard_map/ppermute | solution.py:416
  124.4 0.7 collective-permute-start.6
  125.1 3.4 %collective-permute-start.7 = (f32[264,256]{1,0:T(8,128)S(1)}, f32[264,256]{1,0:T(8,128)S(1)}, u32[]{:S(2)}, u32[]{:S(2)}) collective-permute-start(f32[264,256]{1,0:T(8,128)S(1)} %collective-permute-done.6.came_ref), channel_id=1, source_target_pairs={{0,8},{8,0},{16,24},{24,16},{32,40},{40,32},{48,56},{56,48},{64,72... | collective-permute-start | bytes 811016 | tf_op jit(solution)/shard_map/ppermute | solution.py:416
  129.2 0.7 collective-permute-start.8
  129.9 3.4 %collective-permute-start.9 = (f32[264,256]{1,0:T(8,128)S(1)}, f32[264,256]{1,0:T(8,128)S(1)}, u32[]{:S(2)}, u32[]{:S(2)}) collective-permute-start(f32[264,256]{1,0:T(8,128)S(1)} %collective-permute-done.8.came_ref), channel_id=1, source_target_pairs={{0,8},{8,0},{16,24},{24,16},{32,40},{40,32},{48,56},{56,48},{64,72... | collective-permute-start | bytes 811016 | tf_op jit(solution)/shard_map/ppermute | solution.py:416
  134.0 0.7 collective-permute-start.10
  134.7 3.4 %collective-permute-start.11 = (f32[264,256]{1,0:T(8,128)S(1)}, f32[264,256]{1,0:T(8,128)S(1)}, u32[]{:S(2)}, u32[]{:S(2)}) collective-permute-start(f32[264,256]{1,0:T(8,128)S(1)} %collective-permute-done.10.came_ref), channel_id=1, source_target_pairs={{0,8},{8,0},{16,24},{24,16},{32,40},{40,32},{48,56},{56,48},{64,72... | collective-permute-start | bytes 811016 | tf_op jit(solution)/shard_map/ppermute | solution.py:416
  138.9 58.5 %collective-permute-start.12 = (f32[3,4,32]{2,1,0:T(4,128)S(1)}, f32[3,4,32]{2,1,0:T(4,128)S(1)}, u32[]{:S(2)}, u32[]{:S(2)}) collective-permute-start(f32[3,4,32]{2,1,0:T(4,128)S(1)} %get-tuple-element.39), channel_id=1, source_target_pairs={{0,16},{8,24},{48,32},{56,40},{64,80},{72,88},{112,96},{120,104},{... | collective-permute-start | bytes 4616 | tf_op jit(solution)/shard_map/ppermute | solution.py:426

commit v4 on v3

--- a/solution.py
+++ b/solution.py
@@ -88,7 +88,7 @@
     out_ref[2] = right(2) - dot6(b2, w2, TN)
 
 
-def merge_blocks(d, left, right, depth, out_ref, d_ref, x_ref, after):
+def merge_blocks(d, depth, d_ref, x_ref, finish):
     d_ref[...] = d
     x_ref[...], _ = newton(parts(d), first_inverse(d, SQUARINGS[min(depth, len(SQUARINGS) - 1)]), dot3)
 
@@ -102,8 +102,7 @@
 
         x, residual = newton(parts(d_ref[...]), x_ref[...], dot6)
         x_ref[...] = x
-        combine(left, right, x, out_ref)
-        after()
+        finish(x)
         return state[0] + 1, jnp.sum(residual * residual)
 
     lax.while_loop(going, again, (0, F32(1)))
@@ -138,10 +137,8 @@
     sector(0)
     blocks = (a_ref, b_ref, c_ref)
     merge_blocks(
-        c_ref[0] + a_ref[1],
-        lambda i: blocks[i][0],
-        lambda i: blocks[i][1],
-        0, out_ref, d_ref, x_ref, lambda: None,
+        c_ref[0] + a_ref[1], 0, d_ref, x_ref,
+        lambda x: combine(lambda i: blocks[i][0], lambda i: blocks[i][1], x, out_ref),
     )
 
 
@@ -158,13 +155,21 @@
     )(flags, margin, cot, csc, coupling)
 
 
-def merge_refs(upper, own_ref, other_ref, depth, out_ref, d_ref, x_ref, after):
-    merge_blocks(
-        jnp.where(upper, other_ref[2] + own_ref[0], own_ref[2] + other_ref[0]),
+def sides(upper, own_ref, other_ref):
+    return (
         lambda i: jnp.where(upper, other_ref[i], own_ref[i]),
         lambda i: jnp.where(upper, own_ref[i], other_ref[i]),
-        depth, out_ref, d_ref, x_ref, after,
     )
+
+
+def merge_refs(upper, own_ref, other_ref, depth, out_ref, d_ref, x_ref, after):
+    left, right = sides(upper, own_ref, other_ref)
+
+    def finish(x):
+        combine(left, right, x, out_ref)
+        after()
+
+    merge_blocks(left(2) + right(0), depth, d_ref, x_ref, finish)
 
 
 def core_kernel(flags_ref, own_ref, other_ref, out_ref, send_ref, d_ref, x_ref):
@@ -227,30 +232,41 @@
     )(flags, own, came, swapped)
 
 
-def last_kernel(level, flags_ref, own_ref, came_ref, swapped_ref, mine_ref, next_ref, d_ref, x_ref, other_ref, out_ref):
+def last_kernel(level, flags_ref, own_ref, came_ref, swapped_ref, mine_ref, next_ref, d_ref, x_ref, turned_ref, other_ref):
     n = d_ref.shape[0]
     core = flags_ref[2]
     wide, rows = mine_ref.shape[1:]
     active = flags_ref[4 + 2 * level] == 1
-
-    def piece(chip, to_ref):
-        chip_rows = pl.ds(pl.multiple_of(chip * (2 * wide), 2 * wide), 2 * wide)
-        for i in range(3):
-            source = other_ref if i == 1 else out_ref
-            both = source[0 if i == 1 else i, chip_rows, :]
-            moved = pltpu.roll(both, (n - flags_ref[3] * rows) % n, axis=1)[:, :rows]
-            to_ref[i] = jnp.where(core == 0, moved[:wide], moved[wide:])
+    upper = flags_ref[5 + 2 * level] == 1
+    chip = flags_ref[0] // 2
+    block = pl.ds(pl.multiple_of(chip // 2 * (4 * wide), 4 * wide), 4 * wide)
+
+    def cut(wanted, array):
+        moved = pltpu.roll(array, (n - flags_ref[3] * rows) % n, axis=1)[:, :rows]
+        piece = moved[:wide]
+        for i in range(1, 4):
+            piece = jnp.where(wanted == i, moved[i * wide : (i + 1) * wide], piece)
+        return piece
 
     @pl.when(active)
     def _():
         unpack(core, came_ref, swapped_ref, other_ref)
-        merge_refs(
-            flags_ref[5 + 2 * level] == 1, own_ref, other_ref, level + 2, out_ref, d_ref, x_ref, lambda: None
-        )
-        other_ref[0] = out_ref[1].T
-        chip = flags_ref[0] // 2
-        piece(chip, mine_ref)
-        piece(chip + 1 - 2 * (chip % 2), next_ref)
+        left, right = sides(upper, own_ref, other_ref)
+        turned_ref[...] = right(1).T
+
+        def finish(x):
+            x = parts(x)
+            b1, b2 = parts(left(1)), parts(right(1))
+            b1_rows = jnp.where(upper, other_ref[1, block, :], own_ref[1, block, :])
+            w1, w2 = parts(dot6(parts(b1_rows), x)), parts(dot6(parts(turned_ref[block, :]), x))
+            a_rows = jnp.where(upper, other_ref[0, block, :], own_ref[0, block, :])
+            c_rows = jnp.where(upper, own_ref[2, block, :], other_ref[2, block, :])
+            results = (a_rows - dot6(w1, b1, NT), dot6(w2, b1, NT), c_rows - dot6(w2, b2))
+            for i, result in enumerate(results):
+                mine_ref[i] = cut(chip % 2 * 2 + core, result)
+                next_ref[i] = cut((1 - chip % 2) * 2 + core, result)
+
+        merge_blocks(left(2) + right(0), level + 2, d_ref, x_ref, finish)
 
     @pl.when(jnp.logical_not(active))
     def _():
@@ -265,7 +281,7 @@
         out_shape=(jax.ShapeDtypeStruct((3, wide, rows), F32),) * 2,
         in_specs=[SMEM, VMEM, VMEM, VMEM],
         out_specs=(VMEM, VMEM),
-        scratch_shapes=[pltpu.VMEM((n, n), F32)] * 2 + [pltpu.VMEM((3, n, n), F32)] * 2,
+        scratch_shapes=[pltpu.VMEM((n, n), F32)] * 3 + [pltpu.VMEM((3, n, n), F32)],
         compiler_params=PARAMS,
         name="last_merge",
     )(flags, own, came, swapped)
@@ -383,6 +399,9 @@
     count = lax.axis_size("sector")
     position = lax.axis_index("sector")
     plan = levels(count // (2 * YS))
+    cut = surface_functions.reshape(sectors, rows, shards, points // shards)
+    own = exchange(jnp.transpose(cut, (2, 0, 1, 3)))
+    own, position, channel_rates = lax.optimization_barrier((own, position, channel_rates))
     x, y, core = place(position)
     at_end = (y == ENDS[0]) | (y == ENDS[1]) | (y == ENDS[2]) | (y == ENDS[3])
     words = [position, jnp.int32(count), core, lax.axis_index("chan")]
@@ -395,8 +414,6 @@
     cot = channel_rates / jnp.tanh(channel_rates * step)
     csc = channel_rates / jnp.sinh(channel_rates * step)
 
-    cut = surface_functions.reshape(sectors, rows, shards, points // shards)
-    own = exchange(jnp.transpose(cut, (2, 0, 1, 3)))
     before = lax.ppermute(own[:, sectors - 1], "sector", [(i, i + 1) for i in range(count - 1)])
     inner, cot, csc, flags, before = lax.optimization_barrier((inner_parts(own), cot, csc, flags, before))
     partial = exchange(margin_parts(own, before, inner))

time: 199 us -> 199 us (level)
  waiting for transfers between devices: 103 us -> 101 us
where the time goes in v4:
time: 199 us; the launch traced here: 198 us
  waiting for transfers between devices  101 us (51%)
  blocking collectives  38.1 us (19%)
  starting transfers between devices  35.4 us (18%)
  Pallas kernels  19.2 us (10%)
  local copies, waits for them, and re-layouts  2.91 us (1%)
    ppermute x1, waiting for transfers between devices, per_device(): brought = lax.ppermute(for_next, 'sector', pairs)  56.7 us
    all_to_all x2, blocking collectives, exchange(): lax.all_to_all(array, 'chan', split_axis=0, concat_axis=0, tiled=True)  38.1 us
    all_to_all x1, waiting for transfers between devices, exchange(): lax.all_to_all(array, 'chan', split_axis=0, concat_axis=0, tiled=True)  17.5 us
    ppermute x5, waiting for transfers between devices, per_device(): came = lax.ppermute(send, 'sector', pairs)  13.1 us
    all_to_all x1, starting transfers between devices, exchange(): lax.all_to_all(array, 'chan', split_axis=0, concat_axis=0, tiled=True)  10.3 us
    ppermute x5, starting transfers between devices, per_device(): came = lax.ppermute(send, 'sector', pairs)  10 us
    ppermute x5, starting transfers between devices, per_device(): swapped = lax.ppermute(came, 'sector', cores)  9.95 us
    ppermute x5, waiting for transfers between devices, per_device(): swapped = lax.ppermute(came, 'sector', cores)  7.19 us
  transfers between devices with their start and end apart: 14, of which 11 were waited for; matrix products, arithmetic and copies ran while one was open for 0% of the time, Pallas kernels for 0%

profile of v4, /device:TPU:22, one launch (start us, length us, event | category | flops | bytes accessed | tf_op | source)
XLA Modules:
  0.0 198.0 jit_solution(635699253524435309)
XLA Ops:
  0.6 1.2 copy.13
  1.9 1.0 copy.11
  2.9 10.3 %all-to-all-start = ((bf16[8,2,32,512]{3,2,1,0:T(8,128)(2,1)}), bf16[8,2,32,512]{3,2,1,0:T(8,128)(2,1)S(1)}, u32[]{:S(2)}, u32[]{:S(2)}) async-start(bf16[8,2,32,512]{3,2,1,0:T(8,128)(2,1)} %copy.11), calls=%async_computation | async-start | bytes 1048576 | tf_op jit(solution)/shard_map/all_to_all | solution.py:368
  13.2 17.5 %all-to-all-done.own_ref = bf16[8,2,32,512]{3,2,1,0:T(8,128)(2,1)S(1)} async-done(((bf16[8,2,32,512]{3,2,1,0:T(8,128)(2,1)}), bf16[8,2,32,512]{3,2,1,0:T(8,128)(2,1)S(1)}, u32[]{:S(2)}, u32[]{:S(2)}) %all-to-all-start) | async-done | bytes 524320 | tf_op jit(solution)/shard_map/all_to_all | solution.py:368
  30.7 1.9 collective-permute-start
  32.6 0.3 inner_parts.1.inner_ref
  32.9 0.0 copy-start.1
  33.0 0.1 stack.46.flags_ref
  33.0 0.6 copy-done.1
  33.7 4.7 %collective-permute-done.before_ref = bf16[8,32,512]{2,1,0:T(8,128)(2,1)S(1)} collective-permute-done((bf16[8,32,512]{2,1,0:T(8,128)(2,1)S(1)}, bf16[8,32,512]{2,1,0:T(8,128)(2,1)S(1)}, u32[]{:S(2)}, u32[]{:S(2)}) %collective-permute-start) | collective-permute-done | bytes 262176 | tf_op jit(solution)/shard_map/ppermute | solution.py:417
  38.4 0.3 margin_parts.1
  38.6 19.6 %all_to_all.15.partial_ref = f32[8,2,32,256]{3,2,1,0:T(8,128)S(1)} all-to-all(f32[8,2,32,256]{3,2,1,0:T(8,128)S(1)} %margin_parts.1), channel_id=1, replica_groups=mesh['sector'=64,'chan'=8] {'chan'}, dimensions={0} | all-to-all | bytes 1048576 | tf_op jit(solution)/shard_map/all_to_all | solution.py:368
  58.3 0.0 copy-start
  58.3 18.6 %all_to_all.16.margin_ref = f32[8,2,32,256]{3,2,1,0:T(8,128)S(1)} all-to-all(f32[8,2,32,256]{3,2,1,0:T(8,128)S(1)} %total_for_all.1), channel_id=1, replica_groups=mesh['sector'=64,'chan'=8] {'chan'}, dimensions={0} | all-to-all | bytes 1048576 | tf_op jit(solution)/shard_map/all_to_all | solution.py:368
  76.8 0.0 copy-done
  76.9 5.4 %leaf.1.own_ref = f32[3,256,256]{2,1,0:T(8,128)S(1)} custom-call(s32[14]{0:T(128)S(1)} %stack.46.flags_ref, f32[8,2,32,256]{3,2,1,0:T(8,128)S(1)} %all_to_all.16.margin_ref, f32[2,256]{1,0:T(2,128)S(1)} %get-tuple-element.32.cot_ref, f32[2,256]{1,0:T(2,128)S(1)} %get-tuple-element.33.csc_ref, bf16[2,256,256]{2,1,0:T(8,128)(2,1)S(1)} %copy-done), custom_call_target="tpu_custom_call" | custom-call | tf_op jit(solution)/shard_map/leaf/pallas_call | solution.py:147
  82.3 1.9 collective-permute-start.1
  84.2 2.3 %collective-permute-done.1.other_ref = f32[3,256,256]{2,1,0:T(8,128)S(1)} collective-permute-done((f32[3,256,256]{2,1,0:T(8,128)S(1)}, f32[3,256,256]{2,1,0:T(8,128)S(1)}, u32[]{:S(2)}, u32[]{:S(2)}) %collective-permute-start.1) | collective-permute-done | bytes 786464 | tf_op jit(solution)/shard_map/ppermute | solution.py:424
  86.4 4.5 %core_merge.1 = (f32[3,256,256]{2,1,0:T(8,128)S(1)}, f32[264,256]{1,0:T(8,128)S(1)}) custom-call(s32[14]{0:T(128)S(1)} %stack.46.flags_ref, f32[3,256,256]{2,1,0:T(8,128)S(1)} %leaf.1.own_ref, f32[3,256,256]{2,1,0:T(8,128)S(1)} %collective-permute-done.1.other_ref), custom_call_target="tpu_custom_call" | custom-call | tf_op jit(solution)/shard_map/core_merge/pallas_call | solution.py:182
  91.0 6.7 %collective-permute-start.2 = (f32[264,256]{1,0:T(8,128)S(1)}, f32[264,256]{1,0:T(8,128)S(1)}, u32[]{:S(2)}, u32[]{:S(2)}) collective-permute-start(f32[264,256]{1,0:T(8,128)S(1)} %get-tuple-element.35), channel_id=1, source_target_pairs={{16,0},{24,8},{0,16},{8,24},{48,32},{56,40},{32,48},{40,56},{80,64... | collective-permute-start | bytes 811016 | tf_op jit(solution)/shard_map/ppermute | solution.py:432
  97.7 6.8 %collective-permute-done.2.came_ref = f32[264,256]{1,0:T(8,128)S(1)} collective-permute-done((f32[264,256]{1,0:T(8,128)S(1)}, f32[264,256]{1,0:T(8,128)S(1)}, u32[]{:S(2)}, u32[]{:S(2)}) %collective-permute-start.2) | collective-permute-done | bytes 270368 | tf_op jit(solution)/shard_map/ppermute | solution.py:432
  104.4 1.9 collective-permute-start.3
  106.3 1.5 collective-permute-done.3.swapped_ref
  107.8 4.8 %chip_merge.4 = (f32[3,256,256]{2,1,0:T(8,128)S(1)}, f32[264,256]{1,0:T(8,128)S(1)}) custom-call(s32[14]{0:T(128)S(1)} %stack.46.flags_ref, f32[3,256,256]{2,1,0:T(8,128)S(1)} %get-tuple-element.34.own_ref, f32[264,256]{1,0:T(8,128)S(1)} %collective-permute-done.2.came_ref, f32[264,256]{1,0:T(8,128)S(1)} %collective-permute-done.3.swapped_ref), custom_call_target="tpu_custom_call" | custom-call | tf_op jit(solution)/shard_map/chip_merge/pallas_call | solution.py:224
  112.6 1.3 collective-permute-start.4
  113.9 6.3 %collective-permute-done.4.came_ref = f32[264,256]{1,0:T(8,128)S(1)} collective-permute-done((f32[264,256]{1,0:T(8,128)S(1)}, f32[264,256]{1,0:T(8,128)S(1)}, u32[]{:S(2)}, u32[]{:S(2)}) %collective-permute-start.4) | collective-permute-done | bytes 270368 | tf_op jit(solution)/shard_map/ppermute | solution.py:432
  120.2 1.9 collective-permute-start.5
  122.1 1.5 collective-permute-done.5.swapped_ref
  123.7 0.8 chip_merge.5
  124.5 0.7 collective-permute-start.6
  125.1 0.0 collective-permute-done.6.came_ref
  125.2 2.0 %collective-permute-start.7 = (f32[264,256]{1,0:T(8,128)S(1)}, f32[264,256]{1,0:T(8,128)S(1)}, u32[]{:S(2)}, u32[]{:S(2)}) collective-permute-start(f32[264,256]{1,0:T(8,128)S(1)} %collective-permute-done.6.came_ref), channel_id=1, source_target_pairs={{0,8},{8,0},{16,24},{24,16},{32,40},{40,32},{48,56},{56,48},{64,72... | collective-permute-start | bytes 811016 | tf_op jit(solution)/shard_map/ppermute | solution.py:433
  127.2 1.4 collective-permute-done.7.swapped_ref
  128.6 0.6 chip_merge.6
  129.2 0.7 collective-permute-start.8
  129.9 0.0 collective-permute-done.8.came_ref
  129.9 2.0 %collective-permute-start.9 = (f32[264,256]{1,0:T(8,128)S(1)}, f32[264,256]{1,0:T(8,128)S(1)}, u32[]{:S(2)}, u32[]{:S(2)}) collective-permute-start(f32[264,256]{1,0:T(8,128)S(1)} %collective-permute-done.8.came_ref), channel_id=1, source_target_pairs={{0,8},{8,0},{16,24},{24,16},{32,40},{40,32},{48,56},{56,48},{64,72... | collective-permute-start | bytes 811016 | tf_op jit(solution)/shard_map/ppermute | solution.py:433
  132.0 1.4 collective-permute-done.9.swapped_ref
  133.4 0.6 chip_merge.7
  134.0 0.7 collective-permute-start.10
  134.7 0.0 collective-permute-done.10.came_ref
  134.7 2.0 %collective-permute-start.11 = (f32[264,256]{1,0:T(8,128)S(1)}, f32[264,256]{1,0:T(8,128)S(1)}, u32[]{:S(2)}, u32[]{:S(2)}) collective-permute-start(f32[264,256]{1,0:T(8,128)S(1)} %collective-permute-done.10.came_ref), channel_id=1, source_target_pairs={{0,8},{8,0},{16,24},{24,16},{32,40},{40,32},{48,56},{56,48},{64,72... | collective-permute-start | bytes 811016 | tf_op jit(solution)/shard_map/ppermute | solution.py:433
  136.7 1.4 collective-permute-done.11.swapped_ref
  138.1 0.8 last_merge.1
  138.9 1.3 collective-permute-start.12
  140.2 56.7 %collective-permute-done.12.brought_ref = f32[3,4,32]{2,1,0:T(4,128)S(1)} collective-permute-done((f32[3,4,32]{2,1,0:T(4,128)S(1)}, f32[3,4,32]{2,1,0:T(4,128)S(1)}, u32[]{:S(2)}, u32[]{:S(2)}) %collective-permute-start.12) | collective-permute-done | bytes 1568 | tf_op jit(solution)/shard_map/ppermute | solution.py:443
  196.9 1.1 pick.1
  (4 shorter events, 0.1 us)
Async XLA Ops:
  2.9 27.8 %all-to-all-start = ((bf16[8,2,32,512]{3,2,1,0:T(8,128)(2,1)}), bf16[8,2,32,512]{3,2,1,0:T(8,128)(2,1)S(1)}, u32[]{:S(2)}, u32[]{:S(2)}) async-start(bf16[8,2,32,512]{3,2,1,0:T(8,128)(2,1)} %copy.11), calls=%async_computation | async-start | bytes 1048576 | tf_op jit(solution)/shard_map/all_to_all | solution.py:368
  30.7 7.7 %collective-permute-start = (bf16[8,32,512]{2,1,0:T(8,128)(2,1)S(1)}, bf16[8,32,512]{2,1,0:T(8,128)(2,1)S(1)}, u32[]{:S(2)}, u32[]{:S(2)}) collective-permute-start(bf16[8,32,512]{2,1,0:T(8,128)(2,1)S(1)} %slice_bitcast_fusion), channel_id=1, source_target_pairs={{0,8},{8,16},{16,24},{24,32},{32,40},{40,48},{48,56},{56,64},{64,7... | collective-permute-start | bytes 786440 | tf_op jit(solution)/shard_map/ppermute | solution.py:417
  32.9 0.7 copy-start.1
  58.3 18.6 %copy-start = (bf16[2,256,256]{2,1,0:T(8,128)(2,1)S(1)}, bf16[2,256,256]{2,1,0:T(8,128)(2,1)}, u32[]{:S(2)}) copy-start(bf16[2,256,256]{2,1,0:T(8,128)(2,1)} %coupling_ref.1) | copy-start | bytes 786436
  82.3 4.2 %collective-permute-start.1 = (f32[3,256,256]{2,1,0:T(8,128)S(1)}, f32[3,256,256]{2,1,0:T(8,128)S(1)}, u32[]{:S(2)}, u32[]{:S(2)}) collective-permute-start(f32[3,256,256]{2,1,0:T(8,128)S(1)} %leaf.1.own_ref), channel_id=1, source_target_pairs={{0,8},{8,0},{16,24},{24,16},{32,40},{40,32},{48,56},{56,48},{64,72... | collective-permute-start | bytes 2359304 | tf_op jit(solution)/shard_map/ppermute | solution.py:424
  91.0 13.4 %collective-permute-start.2 = (f32[264,256]{1,0:T(8,128)S(1)}, f32[264,256]{1,0:T(8,128)S(1)}, u32[]{:S(2)}, u32[]{:S(2)}) collective-permute-start(f32[264,256]{1,0:T(8,128)S(1)} %get-tuple-element.35), channel_id=1, source_target_pairs={{16,0},{24,8},{0,16},{8,24},{48,32},{56,40},{32,48},{40,56},{80,64... | collective-permute-start | bytes 811016 | tf_op jit(solution)/shard_map/ppermute | solution.py:432
  104.4 3.4 %collective-permute-start.3 = (f32[264,256]{1,0:T(8,128)S(1)}, f32[264,256]{1,0:T(8,128)S(1)}, u32[]{:S(2)}, u32[]{:S(2)}) collective-permute-start(f32[264,256]{1,0:T(8,128)S(1)} %collective-permute-done.2.came_ref), channel_id=1, source_target_pairs={{0,8},{8,0},{16,24},{24,16},{32,40},{40,32},{48,56},{56,48},{64,72... | collective-permute-start | bytes 811016 | tf_op jit(solution)/shard_map/ppermute | solution.py:433
  112.6 7.6 %collective-permute-start.4 = (f32[264,256]{1,0:T(8,128)S(1)}, f32[264,256]{1,0:T(8,128)S(1)}, u32[]{:S(2)}, u32[]{:S(2)}) collective-permute-start(f32[264,256]{1,0:T(8,128)S(1)} %get-tuple-element.37), channel_id=1, source_target_pairs={{32,0},{40,8},{16,48},{24,56},{96,64},{104,72},{80,112},{88,120},{... | collective-permute-start | bytes 811016 | tf_op jit(solution)/shard_map/ppermute | solution.py:432
  120.2 3.4 %collective-permute-start.5 = (f32[264,256]{1,0:T(8,128)S(1)}, f32[264,256]{1,0:T(8,128)S(1)}, u32[]{:S(2)}, u32[]{:S(2)}) collective-permute-start(f32[264,256]{1,0:T(8,128)S(1)} %collective-permute-done.4.came_ref), channel_id=1, source_target_pairs={{0,8},{8,0},{16,24},{24,16},{32,40},{40,32},{48,56},{56,48},{64,72... | collective-permute-start | bytes 811016 | tf_op jit(solution)/shard_map/ppermute | solution.py:433
  124.5 0.7 collective-permute-start.6
  125.2 3.4 %collective-permute-start.7 = (f32[264,256]{1,0:T(8,128)S(1)}, f32[264,256]{1,0:T(8,128)S(1)}, u32[]{:S(2)}, u32[]{:S(2)}) collective-permute-start(f32[264,256]{1,0:T(8,128)S(1)} %collective-permute-done.6.came_ref), channel_id=1, source_target_pairs={{0,8},{8,0},{16,24},{24,16},{32,40},{40,32},{48,56},{56,48},{64,72... | collective-permute-start | bytes 811016 | tf_op jit(solution)/shard_map/ppermute | solution.py:433
  129.2 0.7 collective-permute-start.8
  129.9 3.4 %collective-permute-start.9 = (f32[264,256]{1,0:T(8,128)S(1)}, f32[264,256]{1,0:T(8,128)S(1)}, u32[]{:S(2)}, u32[]{:S(2)}) collective-permute-start(f32[264,256]{1,0:T(8,128)S(1)} %collective-permute-done.8.came_ref), channel_id=1, source_target_pairs={{0,8},{8,0},{16,24},{24,16},{32,40},{40,32},{48,56},{56,48},{64,72... | collective-permute-start | bytes 811016 | tf_op jit(solution)/shard_map/ppermute | solution.py:433
  134.0 0.7 collective-permute-start.10
  134.7 3.4 %collective-permute-start.11 = (f32[264,256]{1,0:T(8,128)S(1)}, f32[264,256]{1,0:T(8,128)S(1)}, u32[]{:S(2)}, u32[]{:S(2)}) collective-permute-start(f32[264,256]{1,0:T(8,128)S(1)} %collective-permute-done.10.came_ref), channel_id=1, source_target_pairs={{0,8},{8,0},{16,24},{24,16},{32,40},{40,32},{48,56},{56,48},{64,72... | collective-permute-start | bytes 811016 | tf_op jit(solution)/shard_map/ppermute | solution.py:433
  138.9 58.0 %collective-permute-start.12 = (f32[3,4,32]{2,1,0:T(4,128)S(1)}, f32[3,4,32]{2,1,0:T(4,128)S(1)}, u32[]{:S(2)}, u32[]{:S(2)}) collective-permute-start(f32[3,4,32]{2,1,0:T(4,128)S(1)} %get-tuple-element.45), channel_id=1, source_target_pairs={{0,16},{8,24},{48,32},{56,40},{64,80},{72,88},{112,96},{120,104},{... | collective-permute-start | bytes 4616 | tf_op jit(solution)/shard_map/ppermute | solution.py:443

commit v5 on v4

--- a/solution.py
+++ b/solution.py
@@ -303,6 +303,24 @@
     )(flags, mine, brought)
 
 
+def shares_kernel(whole_ref, out_ref):
+    depth = out_ref.shape[-1]
+    for shard in range(out_ref.shape[0]):
+        out_ref[shard] = whole_ref[:, :, shard * depth : (shard + 1) * depth]
+
+
+def shares(surface_functions, shards):
+    sectors, rows, points = surface_functions.shape
+    return pl.pallas_call(
+        shares_kernel,
+        out_shape=jax.ShapeDtypeStruct((shards, sectors, rows, points // shards), BF16),
+        in_specs=[VMEM],
+        out_specs=VMEM,
+        compiler_params=PARAMS,
+        name="shares",
+    )(surface_functions)
+
+
 def inner_kernel(own_ref, out_ref):
     shards, _, rows, depth = own_ref.shape
     n = shards * rows
@@ -399,12 +417,13 @@
     count = lax.axis_size("sector")
     position = lax.axis_index("sector")
     plan = levels(count // (2 * YS))
-    cut = surface_functions.reshape(sectors, rows, shards, points // shards)
-    own = exchange(jnp.transpose(cut, (2, 0, 1, 3)))
-    own, position, channel_rates = lax.optimization_barrier((own, position, channel_rates))
+    own = exchange(shares(surface_functions, shards))
+    own, position, shard, channel_rates = lax.optimization_barrier(
+        (own, position, lax.axis_index("chan"), channel_rates)
+    )
     x, y, core = place(position)
     at_end = (y == ENDS[0]) | (y == ENDS[1]) | (y == ENDS[2]) | (y == ENDS[3])
-    words = [position, jnp.int32(count), core, lax.axis_index("chan")]
+    words = [position, jnp.int32(count), core, shard]
     for _, takers, (axis, bit) in plan:
         words.append(jnp.int32(1) if len(takers) == YS else at_end.astype(jnp.int32))
         words.append((x if axis == "x" else y) >> bit & 1)

time: 199 us -> 198 us (level)
  no operation moved by 1% of the time
where the time goes in v5:
time: 198 us
  waiting for transfers between devices  101 us (51%)
  blocking collectives  38.1 us (19%)
  starting transfers between devices  35.4 us (18%)
  Pallas kernels  20 us (10%)
    ppermute x1, waiting for transfers between devices, per_device(): brought = lax.ppermute(for_next, 'sector', pairs)  56.7 us
    all_to_all x2, blocking collectives, exchange(): lax.all_to_all(array, 'chan', split_axis=0, concat_axis=0, tiled=True)  38.1 us
    all_to_all x1, waiting for transfers between devices, exchange(): lax.all_to_all(array, 'chan', split_axis=0, concat_axis=0, tiled=True)  17.5 us
    ppermute x5, waiting for transfers between devices, per_device(): came = lax.ppermute(send, 'sector', pairs)  13.1 us
    all_to_all x1, starting transfers between devices, exchange(): lax.all_to_all(array, 'chan', split_axis=0, concat_axis=0, tiled=True)  10.3 us
    ppermute x5, starting transfers between devices, per_device(): came = lax.ppermute(send, 'sector', pairs)  10 us
    ppermute x5, starting transfers between devices, per_device(): swapped = lax.ppermute(came, 'sector', cores)  9.95 us
    ppermute x5, waiting for transfers between devices, per_device(): swapped = lax.ppermute(came, 'sector', cores)  7.19 us
  transfers between devices with their start and end apart: 14, of which 11 were waited for; matrix products, arithmetic and copies ran while one was open for 0% of the time, Pallas kernels for 0%

profile of v5, /device:TPU:22, one launch (start us, length us, event | category | flops | bytes accessed | tf_op | source)
XLA Modules:
  0.0 197.7 jit_solution(11932242839015616897)
XLA Ops:
  0.6 0.0 copy-start
  0.6 1.0 copy-done
  1.7 0.8 shares.1
  2.5 10.3 %all-to-all-start = ((bf16[8,2,32,512]{3,2,1,0:T(8,128)(2,1)}), bf16[8,2,32,512]{3,2,1,0:T(8,128)(2,1)S(1)}, u32[]{:S(2)}, u32[]{:S(2)}) async-start(bf16[8,2,32,512]{3,2,1,0:T(8,128)(2,1)} %shares.1), calls=%async_computation | async-start | bytes 1048576 | tf_op jit(solution)/shard_map/all_to_all | solution.py:386
  12.8 17.5 %all-to-all-done.own_ref = bf16[8,2,32,512]{3,2,1,0:T(8,128)(2,1)S(1)} async-done(((bf16[8,2,32,512]{3,2,1,0:T(8,128)(2,1)}), bf16[8,2,32,512]{3,2,1,0:T(8,128)(2,1)S(1)}, u32[]{:S(2)}, u32[]{:S(2)}) %all-to-all-start) | async-done | bytes 524320 | tf_op jit(solution)/shard_map/all_to_all | solution.py:386
  30.3 1.9 collective-permute-start
  32.3 0.3 inner_parts.1.inner_ref
  32.6 0.0 copy-start.2
  32.6 0.1 stack.46.flags_ref
  32.7 0.6 copy-done.2
  33.3 4.7 %collective-permute-done.before_ref = bf16[8,32,512]{2,1,0:T(8,128)(2,1)S(1)} collective-permute-done((bf16[8,32,512]{2,1,0:T(8,128)(2,1)S(1)}, bf16[8,32,512]{2,1,0:T(8,128)(2,1)S(1)}, u32[]{:S(2)}, u32[]{:S(2)}) %collective-permute-start) | collective-permute-done | bytes 262176 | tf_op jit(solution)/shard_map/ppermute | solution.py:436
  38.0 0.3 margin_parts.1
  38.3 19.6 %all_to_all.15.partial_ref = f32[8,2,32,256]{3,2,1,0:T(8,128)S(1)} all-to-all(f32[8,2,32,256]{3,2,1,0:T(8,128)S(1)} %margin_parts.1), channel_id=1, replica_groups=mesh['sector'=64,'chan'=8] {'chan'}, dimensions={0} | all-to-all | bytes 1048576 | tf_op jit(solution)/shard_map/all_to_all | solution.py:386
  57.9 0.0 copy-start.1
  57.9 18.6 %all_to_all.16.margin_ref = f32[8,2,32,256]{3,2,1,0:T(8,128)S(1)} all-to-all(f32[8,2,32,256]{3,2,1,0:T(8,128)S(1)} %total_for_all.1), channel_id=1, replica_groups=mesh['sector'=64,'chan'=8] {'chan'}, dimensions={0} | all-to-all | bytes 1048576 | tf_op jit(solution)/shard_map/all_to_all | solution.py:386
  76.5 0.0 copy-done.1
  76.5 5.4 %leaf.1.own_ref = f32[3,256,256]{2,1,0:T(8,128)S(1)} custom-call(s32[14]{0:T(128)S(1)} %stack.46.flags_ref, f32[8,2,32,256]{3,2,1,0:T(8,128)S(1)} %all_to_all.16.margin_ref, f32[2,256]{1,0:T(2,128)S(1)} %get-tuple-element.34.cot_ref, f32[2,256]{1,0:T(2,128)S(1)} %get-tuple-element.35.csc_ref, bf16[2,256,256]{2,1,0:T(8,128)(2,1)S(1)} %copy-done.1), custom_call_target="tpu_custom_call" | custom-call | tf_op jit(solution)/shard_map/leaf/pallas_call | solution.py:147
  81.9 1.9 collective-permute-start.1
  83.8 2.3 %collective-permute-done.1.other_ref = f32[3,256,256]{2,1,0:T(8,128)S(1)} collective-permute-done((f32[3,256,256]{2,1,0:T(8,128)S(1)}, f32[3,256,256]{2,1,0:T(8,128)S(1)}, u32[]{:S(2)}, u32[]{:S(2)}) %collective-permute-start.1) | collective-permute-done | bytes 786464 | tf_op jit(solution)/shard_map/ppermute | solution.py:443
  86.1 4.5 %core_merge.1 = (f32[3,256,256]{2,1,0:T(8,128)S(1)}, f32[264,256]{1,0:T(8,128)S(1)}) custom-call(s32[14]{0:T(128)S(1)} %stack.46.flags_ref, f32[3,256,256]{2,1,0:T(8,128)S(1)} %leaf.1.own_ref, f32[3,256,256]{2,1,0:T(8,128)S(1)} %collective-permute-done.1.other_ref), custom_call_target="tpu_custom_call" | custom-call | tf_op jit(solution)/shard_map/core_merge/pallas_call | solution.py:182
  90.6 6.7 %collective-permute-start.2 = (f32[264,256]{1,0:T(8,128)S(1)}, f32[264,256]{1,0:T(8,128)S(1)}, u32[]{:S(2)}, u32[]{:S(2)}) collective-permute-start(f32[264,256]{1,0:T(8,128)S(1)} %get-tuple-element.37), channel_id=1, source_target_pairs={{16,0},{24,8},{0,16},{8,24},{48,32},{56,40},{32,48},{40,56},{80,64... | collective-permute-start | bytes 811016 | tf_op jit(solution)/shard_map/ppermute | solution.py:451
  97.3 6.8 %collective-permute-done.2.came_ref = f32[264,256]{1,0:T(8,128)S(1)} collective-permute-done((f32[264,256]{1,0:T(8,128)S(1)}, f32[264,256]{1,0:T(8,128)S(1)}, u32[]{:S(2)}, u32[]{:S(2)}) %collective-permute-start.2) | collective-permute-done | bytes 270368 | tf_op jit(solution)/shard_map/ppermute | solution.py:451
  104.1 1.9 collective-permute-start.3
  106.0 1.5 collective-permute-done.3.swapped_ref
  107.5 4.8 %chip_merge.4 = (f32[3,256,256]{2,1,0:T(8,128)S(1)}, f32[264,256]{1,0:T(8,128)S(1)}) custom-call(s32[14]{0:T(128)S(1)} %stack.46.flags_ref, f32[3,256,256]{2,1,0:T(8,128)S(1)} %get-tuple-element.36.own_ref, f32[264,256]{1,0:T(8,128)S(1)} %collective-permute-done.2.came_ref, f32[264,256]{1,0:T(8,128)S(1)} %collective-permute-done.3.swapped_ref), custom_call_target="tpu_custom_call" | custom-call | tf_op jit(solution)/shard_map/chip_merge/pallas_call | solution.py:224
  112.3 1.3 collective-permute-start.4
  113.6 6.3 %collective-permute-done.4.came_ref = f32[264,256]{1,0:T(8,128)S(1)} collective-permute-done((f32[264,256]{1,0:T(8,128)S(1)}, f32[264,256]{1,0:T(8,128)S(1)}, u32[]{:S(2)}, u32[]{:S(2)}) %collective-permute-start.4) | collective-permute-done | bytes 270368 | tf_op jit(solution)/shard_map/ppermute | solution.py:451
  119.9 1.9 collective-permute-start.5
  121.8 1.5 collective-permute-done.5.swapped_ref
  123.3 0.8 chip_merge.5
  124.1 0.7 collective-permute-start.6
  124.8 0.0 collective-permute-done.6.came_ref
  124.8 2.0 %collective-permute-start.7 = (f32[264,256]{1,0:T(8,128)S(1)}, f32[264,256]{1,0:T(8,128)S(1)}, u32[]{:S(2)}, u32[]{:S(2)}) collective-permute-start(f32[264,256]{1,0:T(8,128)S(1)} %collective-permute-done.6.came_ref), channel_id=1, source_target_pairs={{0,8},{8,0},{16,24},{24,16},{32,40},{40,32},{48,56},{56,48},{64,72... | collective-permute-start | bytes 811016 | tf_op jit(solution)/shard_map/ppermute | solution.py:452
  126.9 1.4 collective-permute-done.7.swapped_ref
  128.3 0.6 chip_merge.6
  128.9 0.7 collective-permute-start.8
  129.6 0.0 collective-permute-done.8.came_ref
  129.6 2.0 %collective-permute-start.9 = (f32[264,256]{1,0:T(8,128)S(1)}, f32[264,256]{1,0:T(8,128)S(1)}, u32[]{:S(2)}, u32[]{:S(2)}) collective-permute-start(f32[264,256]{1,0:T(8,128)S(1)} %collective-permute-done.8.came_ref), channel_id=1, source_target_pairs={{0,8},{8,0},{16,24},{24,16},{32,40},{40,32},{48,56},{56,48},{64,72... | collective-permute-start | bytes 811016 | tf_op jit(solution)/shard_map/ppermute | solution.py:452
  131.6 1.4 collective-permute-done.9.swapped_ref
  133.0 0.6 chip_merge.7
  133.6 0.7 collective-permute-start.10
  134.3 0.0 collective-permute-done.10.came_ref
  134.3 2.0 %collective-permute-start.11 = (f32[264,256]{1,0:T(8,128)S(1)}, f32[264,256]{1,0:T(8,128)S(1)}, u32[]{:S(2)}, u32[]{:S(2)}) collective-permute-start(f32[264,256]{1,0:T(8,128)S(1)} %collective-permute-done.10.came_ref), channel_id=1, source_target_pairs={{0,8},{8,0},{16,24},{24,16},{32,40},{40,32},{48,56},{56,48},{64,72... | collective-permute-start | bytes 811016 | tf_op jit(solution)/shard_map/ppermute | solution.py:452
  136.4 1.4 collective-permute-done.11.swapped_ref
  137.8 0.8 last_merge.1
  138.6 1.3 collective-permute-start.12
  139.9 56.7 %collective-permute-done.12.brought_ref = f32[3,4,32]{2,1,0:T(4,128)S(1)} collective-permute-done((f32[3,4,32]{2,1,0:T(4,128)S(1)}, f32[3,4,32]{2,1,0:T(4,128)S(1)}, u32[]{:S(2)}, u32[]{:S(2)}) %collective-permute-start.12) | collective-permute-done | bytes 1568 | tf_op jit(solution)/shard_map/ppermute | solution.py:462
  196.5 1.1 pick.1
  (3 shorter events, 0.1 us)
Async XLA Ops:
  0.6 1.0 copy-start
  2.5 27.8 %all-to-all-start = ((bf16[8,2,32,512]{3,2,1,0:T(8,128)(2,1)}), bf16[8,2,32,512]{3,2,1,0:T(8,128)(2,1)S(1)}, u32[]{:S(2)}, u32[]{:S(2)}) async-start(bf16[8,2,32,512]{3,2,1,0:T(8,128)(2,1)} %shares.1), calls=%async_computation | async-start | bytes 1048576 | tf_op jit(solution)/shard_map/all_to_all | solution.py:386
  30.3 7.7 %collective-permute-start = (bf16[8,32,512]{2,1,0:T(8,128)(2,1)S(1)}, bf16[8,32,512]{2,1,0:T(8,128)(2,1)S(1)}, u32[]{:S(2)}, u32[]{:S(2)}) collective-permute-start(bf16[8,32,512]{2,1,0:T(8,128)(2,1)S(1)} %slice_bitcast_fusion), channel_id=1, source_target_pairs={{0,8},{8,16},{16,24},{24,32},{32,40},{40,48},{48,56},{56,64},{64,7... | collective-permute-start | bytes 786440 | tf_op jit(solution)/shard_map/ppermute | solution.py:436
  32.6 0.7 copy-start.2
  57.9 18.6 %copy-start.1 = (bf16[2,256,256]{2,1,0:T(8,128)(2,1)S(1)}, bf16[2,256,256]{2,1,0:T(8,128)(2,1)}, u32[]{:S(2)}) copy-start(bf16[2,256,256]{2,1,0:T(8,128)(2,1)} %coupling_ref.1) | copy-start | bytes 786436
  81.9 4.2 %collective-permute-start.1 = (f32[3,256,256]{2,1,0:T(8,128)S(1)}, f32[3,256,256]{2,1,0:T(8,128)S(1)}, u32[]{:S(2)}, u32[]{:S(2)}) collective-permute-start(f32[3,256,256]{2,1,0:T(8,128)S(1)} %leaf.1.own_ref), channel_id=1, source_target_pairs={{0,8},{8,0},{16,24},{24,16},{32,40},{40,32},{48,56},{56,48},{64,72... | collective-permute-start | bytes 2359304 | tf_op jit(solution)/shard_map/ppermute | solution.py:443
  90.6 13.4 %collective-permute-start.2 = (f32[264,256]{1,0:T(8,128)S(1)}, f32[264,256]{1,0:T(8,128)S(1)}, u32[]{:S(2)}, u32[]{:S(2)}) collective-permute-start(f32[264,256]{1,0:T(8,128)S(1)} %get-tuple-element.37), channel_id=1, source_target_pairs={{16,0},{24,8},{0,16},{8,24},{48,32},{56,40},{32,48},{40,56},{80,64... | collective-permute-start | bytes 811016 | tf_op jit(solution)/shard_map/ppermute | solution.py:451
  104.1 3.4 %collective-permute-start.3 = (f32[264,256]{1,0:T(8,128)S(1)}, f32[264,256]{1,0:T(8,128)S(1)}, u32[]{:S(2)}, u32[]{:S(2)}) collective-permute-start(f32[264,256]{1,0:T(8,128)S(1)} %collective-permute-done.2.came_ref), channel_id=1, source_target_pairs={{0,8},{8,0},{16,24},{24,16},{32,40},{40,32},{48,56},{56,48},{64,72... | collective-permute-start | bytes 811016 | tf_op jit(solution)/shard_map/ppermute | solution.py:452
  112.3 7.6 %collective-permute-start.4 = (f32[264,256]{1,0:T(8,128)S(1)}, f32[264,256]{1,0:T(8,128)S(1)}, u32[]{:S(2)}, u32[]{:S(2)}) collective-permute-start(f32[264,256]{1,0:T(8,128)S(1)} %get-tuple-element.39), channel_id=1, source_target_pairs={{32,0},{40,8},{16,48},{24,56},{96,64},{104,72},{80,112},{88,120},{... | collective-permute-start | bytes 811016 | tf_op jit(solution)/shard_map/ppermute | solution.py:451
  119.9 3.4 %collective-permute-start.5 = (f32[264,256]{1,0:T(8,128)S(1)}, f32[264,256]{1,0:T(8,128)S(1)}, u32[]{:S(2)}, u32[]{:S(2)}) collective-permute-start(f32[264,256]{1,0:T(8,128)S(1)} %collective-permute-done.4.came_ref), channel_id=1, source_target_pairs={{0,8},{8,0},{16,24},{24,16},{32,40},{40,32},{48,56},{56,48},{64,72... | collective-permute-start | bytes 811016 | tf_op jit(solution)/shard_map/ppermute | solution.py:452
  124.1 0.7 collective-permute-start.6
  124.8 3.4 %collective-permute-start.7 = (f32[264,256]{1,0:T(8,128)S(1)}, f32[264,256]{1,0:T(8,128)S(1)}, u32[]{:S(2)}, u32[]{:S(2)}) collective-permute-start(f32[264,256]{1,0:T(8,128)S(1)} %collective-permute-done.6.came_ref), channel_id=1, source_target_pairs={{0,8},{8,0},{16,24},{24,16},{32,40},{40,32},{48,56},{56,48},{64,72... | collective-permute-start | bytes 811016 | tf_op jit(solution)/shard_map/ppermute | solution.py:452
  128.9 0.7 collective-permute-start.8
  129.6 3.4 %collective-permute-start.9 = (f32[264,256]{1,0:T(8,128)S(1)}, f32[264,256]{1,0:T(8,128)S(1)}, u32[]{:S(2)}, u32[]{:S(2)}) collective-permute-start(f32[264,256]{1,0:T(8,128)S(1)} %collective-permute-done.8.came_ref), channel_id=1, source_target_pairs={{0,8},{8,0},{16,24},{24,16},{32,40},{40,32},{48,56},{56,48},{64,72... | collective-permute-start | bytes 811016 | tf_op jit(solution)/shard_map/ppermute | solution.py:452
  133.6 0.7 collective-permute-start.10
  134.3 3.4 %collective-permute-start.11 = (f32[264,256]{1,0:T(8,128)S(1)}, f32[264,256]{1,0:T(8,128)S(1)}, u32[]{:S(2)}, u32[]{:S(2)}) collective-permute-start(f32[264,256]{1,0:T(8,128)S(1)} %collective-permute-done.10.came_ref), channel_id=1, source_target_pairs={{0,8},{8,0},{16,24},{24,16},{32,40},{40,32},{48,56},{56,48},{64,72... | collective-permute-start | bytes 811016 | tf_op jit(solution)/shard_map/ppermute | solution.py:452
  138.6 58.0 %collective-permute-start.12 = (f32[3,4,32]{2,1,0:T(4,128)S(1)}, f32[3,4,32]{2,1,0:T(4,128)S(1)}, u32[]{:S(2)}, u32[]{:S(2)}) collective-permute-start(f32[3,4,32]{2,1,0:T(4,128)S(1)} %get-tuple-element.47), channel_id=1, source_target_pairs={{0,16},{8,24},{48,32},{56,40},{64,80},{72,88},{112,96},{120,104},{... | collective-permute-start | bytes 4616 | tf_op jit(solution)/shard_map/ppermute | solution.py:462

commit v6 on v5

--- a/solution.py
+++ b/solution.py
@@ -201,16 +201,36 @@
     other_ref[2] = jnp.where(row == column, diagonal, jnp.where(row < column, both, turned))
 
 
-def chip_kernel(level, flags_ref, own_ref, came_ref, swapped_ref, out_ref, send_ref, d_ref, x_ref, other_ref):
+def pack_for_last(flags_ref, level, rows, block, out_ref, send_ref, turned_ref):
+    n = out_ref.shape[-1]
+    half = n // 2
+    row, column = grid_of(n)
+    both = jnp.where(row >= column, out_ref[0], out_ref[2])
+    send_ref[0:half] = jnp.where(flags_ref[2] == 0, both[:half], both[half:])
+    diagonal = jnp.sum(jnp.where(row == column, out_ref[2], F32(0)), axis=0, keepdims=True)
+    send_ref[half : half + 8] = jnp.broadcast_to(diagonal, (8, n))
+    turned_ref[...] = jnp.where(flags_ref[5 + 2 * level] == 1, out_ref[1].T, out_ref[1])
+    first = flags_ref[4 + 2 * (level + 1)]
+    send_ref[half + 8 : half + 8 + block] = turned_ref[pl.ds(pl.multiple_of(first * block, block), block), :]
+    mine = pl.ds(pl.multiple_of(flags_ref[3] * rows, rows), rows)
+    send_ref[half + 8 + block : half + 8 + block + rows] = turned_ref[mine, :]
+
+
+def chip_kernel(level, last, flags_ref, own_ref, came_ref, swapped_ref, out_ref, send_ref, d_ref, x_ref, other_ref, turned_ref):
     core = flags_ref[2]
     active = flags_ref[4 + 2 * level] == 1
+
+    def send_off():
+        if last is None:
+            pack(core, out_ref, send_ref)
+        else:
+            pack_for_last(flags_ref, level + 1, *last, out_ref, send_ref, turned_ref)
 
     @pl.when(active)
     def _():
         unpack(core, came_ref, swapped_ref, other_ref)
         merge_refs(
-            flags_ref[5 + 2 * level] == 1, own_ref, other_ref, level + 2, out_ref, d_ref, x_ref,
-            lambda: pack(core, out_ref, send_ref),
+            flags_ref[5 + 2 * level] == 1, own_ref, other_ref, level + 2, out_ref, d_ref, x_ref, send_off
         )
 
     @pl.when(jnp.logical_not(active))
@@ -219,14 +239,15 @@
         send_ref[...] = jnp.zeros_like(send_ref)
 
 
-def chip_merge(level, flags, own, came, swapped):
+def chip_merge(level, last, flags, own, came, swapped):
     n = own.shape[-1]
-    return pl.pallas_call(
-        functools.partial(chip_kernel, level),
-        out_shape=(jax.ShapeDtypeStruct((3, n, n), F32), jax.ShapeDtypeStruct((n + 8, n), F32)),
+    sent = n + 8 if last is None else n // 2 + 8 + sum(last)
+    return pl.pallas_call(
+        functools.partial(chip_kernel, level, last),
+        out_shape=(jax.ShapeDtypeStruct((3, n, n), F32), jax.ShapeDtypeStruct((sent, n), F32)),
         in_specs=[SMEM, VMEM, VMEM, VMEM],
         out_specs=(VMEM, VMEM),
-        scratch_shapes=[pltpu.VMEM((n, n), F32)] * 2 + [pltpu.VMEM((3, n, n), F32)],
+        scratch_shapes=[pltpu.VMEM((n, n), F32)] * 2 + [pltpu.VMEM((3, n, n), F32), pltpu.VMEM((n, n), F32)],
         compiler_params=PARAMS,
         name="chip_merge",
     )(flags, own, came, swapped)
@@ -239,34 +260,49 @@
     active = flags_ref[4 + 2 * level] == 1
     upper = flags_ref[5 + 2 * level] == 1
     chip = flags_ref[0] // 2
-    block = pl.ds(pl.multiple_of(chip // 2 * (4 * wide), 4 * wide), 4 * wide)
+    depth = 4 * wide
+    block = pl.ds(pl.multiple_of(chip // 2 * depth, depth), depth)
+    mine = pl.ds(pl.multiple_of(flags_ref[3] * rows, rows), rows)
+    half = n // 2
 
     def cut(wanted, array):
-        moved = pltpu.roll(array, (n - flags_ref[3] * rows) % n, axis=1)[:, :rows]
-        piece = moved[:wide]
+        piece = array[:wide]
         for i in range(1, 4):
-            piece = jnp.where(wanted == i, moved[i * wide : (i + 1) * wide], piece)
+            piece = jnp.where(wanted == i, array[i * wide : (i + 1) * wide], piece)
         return piece
+
+    def at_mine(array):
+        return pltpu.roll(array, (n - flags_ref[3] * rows) % n, axis=1)[:, :rows]
 
     @pl.when(active)
     def _():
-        unpack(core, came_ref, swapped_ref, other_ref)
-        left, right = sides(upper, own_ref, other_ref)
-        turned_ref[...] = right(1).T
+        row, column = grid_of(n)
+        x_ref[0:half] = jnp.where(core == 0, came_ref[0:half], swapped_ref[0:half])
+        x_ref[half:n] = jnp.where(core == 0, swapped_ref[0:half], came_ref[0:half])
+        both = x_ref[...]
+        turned = both.T
+        other_ref[0] = jnp.where(row >= column, both, turned)
+        other_ref[1] = jnp.where(row == column, came_ref[half : half + 1], jnp.where(row < column, both, turned))
+        turned_ref[...] = jnp.where(upper, own_ref[1].T, own_ref[1])
+        d = jnp.where(upper, other_ref[1] + own_ref[0], own_ref[2] + other_ref[0])
 
         def finish(x):
             x = parts(x)
-            b1, b2 = parts(left(1)), parts(right(1))
-            b1_rows = jnp.where(upper, other_ref[1, block, :], own_ref[1, block, :])
-            w1, w2 = parts(dot6(parts(b1_rows), x)), parts(dot6(parts(turned_ref[block, :]), x))
+            came_block = came_ref[half + 8 : half + 8 + depth]
+            came_mine = came_ref[half + 8 + depth : half + 8 + depth + rows]
+            own_block, own_mine = turned_ref[block, :], turned_ref[mine, :]
+            b1_block, b2_block = jnp.where(upper, came_block, own_block), jnp.where(upper, own_block, came_block)
+            b1 = parts(jnp.where(upper, came_mine, own_mine))
+            b2 = parts(jnp.where(upper, own_mine, came_mine))
+            w1, w2 = parts(dot6(parts(b1_block), x)), parts(dot6(parts(b2_block), x))
             a_rows = jnp.where(upper, other_ref[0, block, :], own_ref[0, block, :])
-            c_rows = jnp.where(upper, own_ref[2, block, :], other_ref[2, block, :])
-            results = (a_rows - dot6(w1, b1, NT), dot6(w2, b1, NT), c_rows - dot6(w2, b2))
+            c_rows = jnp.where(upper, own_ref[2, block, :], other_ref[1, block, :])
+            results = (at_mine(a_rows) - dot6(w1, b1, NT), dot6(w2, b1, NT), at_mine(c_rows) - dot6(w2, b2, NT))
             for i, result in enumerate(results):
                 mine_ref[i] = cut(chip % 2 * 2 + core, result)
                 next_ref[i] = cut((1 - chip % 2) * 2 + core, result)
 
-        merge_blocks(left(2) + right(0), level + 2, d_ref, x_ref, finish)
+        merge_blocks(d, level + 2, d_ref, x_ref, finish)
 
     @pl.when(jnp.logical_not(active))
     def _():
@@ -281,7 +317,7 @@
         out_shape=(jax.ShapeDtypeStruct((3, wide, rows), F32),) * 2,
         in_specs=[SMEM, VMEM, VMEM, VMEM],
         out_specs=(VMEM, VMEM),
-        scratch_shapes=[pltpu.VMEM((n, n), F32)] * 3 + [pltpu.VMEM((3, n, n), F32)],
+        scratch_shapes=[pltpu.VMEM((n, n), F32)] * 3 + [pltpu.VMEM((2, n, n), F32)],
         compiler_params=PARAMS,
         name="last_merge",
     )(flags, own, came, swapped)
@@ -427,6 +463,8 @@
     for _, takers, (axis, bit) in plan:
         words.append(jnp.int32(1) if len(takers) == YS else at_end.astype(jnp.int32))
         words.append((x if axis == "x" else y) >> bit & 1)
+    across, along = plan[-1][0](x, y)
+    words.append((across * YS + along) // 2)
     flags = jnp.stack([jnp.asarray(word, jnp.int32) for word in words])
 
     step = 1.0 / (sectors * count)
@@ -451,7 +489,8 @@
         came = lax.ppermute(send, "sector", pairs)
         swapped = lax.ppermute(came, "sector", cores)
         if level < len(plan) - 1:
-            packed, send = chip_merge(level, flags, packed, came, swapped)
+            last = (rows, 4 * wide) if level == len(plan) - 2 else None
+            packed, send = chip_merge(level, last, flags, packed, came, swapped)
         else:
             mine, for_next = last_merge(level, flags, packed, came, swapped, wide, rows)
     pairs = []

time: 198 us -> 196 us (0.990)
  waiting for transfers between devices: 101 us -> 99 us
    ppermute x1, waiting for transfers between devices: 56.7 us -> 54.4 us  [per_device(): brought = lax.ppermute(for_next, 'sector', pairs)]
where the time goes in v6:
time: 196 us; the launch traced here: 195 us
  waiting for transfers between devices  99 us (51%)
  blocking collectives  38.1 us (19%)
  starting transfers between devices  35.4 us (18%)
  Pallas kernels  19.8 us (10%)
    ppermute x1, waiting for transfers between devices, per_device(): brought = lax.ppermute(for_next, 'sector', pairs)  54.4 us
    all_to_all x2, blocking collectives, exchange(): lax.all_to_all(array, 'chan', split_axis=0, concat_axis=0, tiled=True)  38.1 us
    all_to_all x1, waiting for transfers between devices, exchange(): lax.all_to_all(array, 'chan', split_axis=0, concat_axis=0, tiled=True)  17.5 us
    ppermute x5, waiting for transfers between devices, per_device(): came = lax.ppermute(send, 'sector', pairs)  13.1 us
    all_to_all x1, starting transfers between devices, exchange(): lax.all_to_all(array, 'chan', split_axis=0, concat_axis=0, tiled=True)  10.3 us
    ppermute x5, starting transfers between devices, per_device(): came = lax.ppermute(send, 'sector', pairs)  10 us
    ppermute x5, starting transfers between devices, per_device(): swapped = lax.ppermute(came, 'sector', cores)  9.95 us
    ppermute x5, waiting for transfers between devices, per_device(): swapped = lax.ppermute(came, 'sector', cores)  7.07 us
  transfers between devices with their start and end apart: 14, of which 11 were waited for; matrix products, arithmetic and copies ran while one was open for 0% of the time, Pallas kernels for 0%

profile of v6, /device:TPU:22, one launch (start us, length us, event | category | flops | bytes accessed | tf_op | source)
XLA Modules:
  0.0 195.1 jit_solution(4290017964014335055)
XLA Ops:
  0.6 0.0 copy-start
  0.6 1.0 copy-done
  1.7 0.8 shares.1
  2.5 10.3 %all-to-all-start = ((bf16[8,2,32,512]{3,2,1,0:T(8,128)(2,1)}), bf16[8,2,32,512]{3,2,1,0:T(8,128)(2,1)S(1)}, u32[]{:S(2)}, u32[]{:S(2)}) async-start(bf16[8,2,32,512]{3,2,1,0:T(8,128)(2,1)} %shares.1), calls=%async_computation | async-start | bytes 1048576 | tf_op jit(solution)/shard_map/all_to_all | solution.py:422
  12.8 17.5 %all-to-all-done.own_ref = bf16[8,2,32,512]{3,2,1,0:T(8,128)(2,1)S(1)} async-done(((bf16[8,2,32,512]{3,2,1,0:T(8,128)(2,1)}), bf16[8,2,32,512]{3,2,1,0:T(8,128)(2,1)S(1)}, u32[]{:S(2)}, u32[]{:S(2)}) %all-to-all-start) | async-done | bytes 524320 | tf_op jit(solution)/shard_map/all_to_all | solution.py:422
  30.3 1.9 collective-permute-start
  32.3 0.3 inner_parts.1.inner_ref
  32.6 0.0 copy-start.2
  32.6 0.1 stack.50.flags_ref
  32.7 0.6 copy-done.2
  33.3 4.7 %collective-permute-done.before_ref = bf16[8,32,512]{2,1,0:T(8,128)(2,1)S(1)} collective-permute-done((bf16[8,32,512]{2,1,0:T(8,128)(2,1)S(1)}, bf16[8,32,512]{2,1,0:T(8,128)(2,1)S(1)}, u32[]{:S(2)}, u32[]{:S(2)}) %collective-permute-start) | collective-permute-done | bytes 262176 | tf_op jit(solution)/shard_map/ppermute | solution.py:474
  38.0 0.3 margin_parts.1
  38.3 19.6 %all_to_all.15.partial_ref = f32[8,2,32,256]{3,2,1,0:T(8,128)S(1)} all-to-all(f32[8,2,32,256]{3,2,1,0:T(8,128)S(1)} %margin_parts.1), channel_id=1, replica_groups=mesh['sector'=64,'chan'=8] {'chan'}, dimensions={0} | all-to-all | bytes 1048576 | tf_op jit(solution)/shard_map/all_to_all | solution.py:422
  57.9 0.0 copy-start.1
  57.9 18.6 %all_to_all.16.margin_ref = f32[8,2,32,256]{3,2,1,0:T(8,128)S(1)} all-to-all(f32[8,2,32,256]{3,2,1,0:T(8,128)S(1)} %total_for_all.1), channel_id=1, replica_groups=mesh['sector'=64,'chan'=8] {'chan'}, dimensions={0} | all-to-all | bytes 1048576 | tf_op jit(solution)/shard_map/all_to_all | solution.py:422
  76.5 0.0 copy-done.1
  76.5 5.4 %leaf.1.own_ref = f32[3,256,256]{2,1,0:T(8,128)S(1)} custom-call(s32[15]{0:T(128)S(1)} %stack.50.flags_ref, f32[8,2,32,256]{3,2,1,0:T(8,128)S(1)} %all_to_all.16.margin_ref, f32[2,256]{1,0:T(2,128)S(1)} %get-tuple-element.34.cot_ref, f32[2,256]{1,0:T(2,128)S(1)} %get-tuple-element.35.csc_ref, bf16[2,256,256]{2,1,0:T(8,128)(2,1)S(1)} %copy-done.1), custom_call_target="tpu_custom_call" | custom-call | tf_op jit(solution)/shard_map/leaf/pallas_call | solution.py:147
  81.9 1.9 collective-permute-start.1
  83.8 2.3 %collective-permute-done.1.other_ref = f32[3,256,256]{2,1,0:T(8,128)S(1)} collective-permute-done((f32[3,256,256]{2,1,0:T(8,128)S(1)}, f32[3,256,256]{2,1,0:T(8,128)S(1)}, u32[]{:S(2)}, u32[]{:S(2)}) %collective-permute-start.1) | collective-permute-done | bytes 786464 | tf_op jit(solution)/shard_map/ppermute | solution.py:481
  86.1 4.5 %core_merge.1 = (f32[3,256,256]{2,1,0:T(8,128)S(1)}, f32[264,256]{1,0:T(8,128)S(1)}) custom-call(s32[15]{0:T(128)S(1)} %stack.50.flags_ref, f32[3,256,256]{2,1,0:T(8,128)S(1)} %leaf.1.own_ref, f32[3,256,256]{2,1,0:T(8,128)S(1)} %collective-permute-done.1.other_ref), custom_call_target="tpu_custom_call" | custom-call | tf_op jit(solution)/shard_map/core_merge/pallas_call | solution.py:182
  90.6 6.7 %collective-permute-start.2 = (f32[264,256]{1,0:T(8,128)S(1)}, f32[264,256]{1,0:T(8,128)S(1)}, u32[]{:S(2)}, u32[]{:S(2)}) collective-permute-start(f32[264,256]{1,0:T(8,128)S(1)} %get-tuple-element.37), channel_id=1, source_target_pairs={{16,0},{24,8},{0,16},{8,24},{48,32},{56,40},{32,48},{40,56},{80,64... | collective-permute-start | bytes 811016 | tf_op jit(solution)/shard_map/ppermute | solution.py:489
  97.3 6.8 %collective-permute-done.2.came_ref = f32[264,256]{1,0:T(8,128)S(1)} collective-permute-done((f32[264,256]{1,0:T(8,128)S(1)}, f32[264,256]{1,0:T(8,128)S(1)}, u32[]{:S(2)}, u32[]{:S(2)}) %collective-permute-start.2) | collective-permute-done | bytes 270368 | tf_op jit(solution)/shard_map/ppermute | solution.py:489
  104.1 1.9 collective-permute-start.3
  106.0 1.5 collective-permute-done.3.swapped_ref
  107.5 4.8 %chip_merge.4 = (f32[3,256,256]{2,1,0:T(8,128)S(1)}, f32[264,256]{1,0:T(8,128)S(1)}) custom-call(s32[15]{0:T(128)S(1)} %stack.50.flags_ref, f32[3,256,256]{2,1,0:T(8,128)S(1)} %get-tuple-element.36.own_ref, f32[264,256]{1,0:T(8,128)S(1)} %collective-permute-done.2.came_ref, f32[264,256]{1,0:T(8,128)S(1)} %collective-permute-done.3.swapped_ref), custom_call_target="tpu_custom_call" | custom-call | tf_op jit(solution)/shard_map/chip_merge/pallas_call | solution.py:245
  112.3 1.3 collective-permute-start.4
  113.6 6.3 %collective-permute-done.4.came_ref = f32[264,256]{1,0:T(8,128)S(1)} collective-permute-done((f32[264,256]{1,0:T(8,128)S(1)}, f32[264,256]{1,0:T(8,128)S(1)}, u32[]{:S(2)}, u32[]{:S(2)}) %collective-permute-start.4) | collective-permute-done | bytes 270368 | tf_op jit(solution)/shard_map/ppermute | solution.py:489
  119.9 1.9 collective-permute-start.5
  121.8 1.5 collective-permute-done.5.swapped_ref
  123.3 0.8 chip_merge.5
  124.1 0.7 collective-permute-start.6
  124.8 0.0 collective-permute-done.6.came_ref
  124.8 2.0 %collective-permute-start.7 = (f32[264,256]{1,0:T(8,128)S(1)}, f32[264,256]{1,0:T(8,128)S(1)}, u32[]{:S(2)}, u32[]{:S(2)}) collective-permute-start(f32[264,256]{1,0:T(8,128)S(1)} %collective-permute-done.6.came_ref), channel_id=1, source_target_pairs={{0,8},{8,0},{16,24},{24,16},{32,40},{40,32},{48,56},{56,48},{64,72... | collective-permute-start | bytes 811016 | tf_op jit(solution)/shard_map/ppermute | solution.py:490
  126.9 1.4 collective-permute-done.7.swapped_ref
  128.3 0.6 chip_merge.6
  128.9 0.7 collective-permute-start.8
  129.6 0.0 collective-permute-done.8.came_ref
  129.6 2.0 %collective-permute-start.9 = (f32[264,256]{1,0:T(8,128)S(1)}, f32[264,256]{1,0:T(8,128)S(1)}, u32[]{:S(2)}, u32[]{:S(2)}) collective-permute-start(f32[264,256]{1,0:T(8,128)S(1)} %collective-permute-done.8.came_ref), channel_id=1, source_target_pairs={{0,8},{8,0},{16,24},{24,16},{32,40},{40,32},{48,56},{56,48},{64,72... | collective-permute-start | bytes 811016 | tf_op jit(solution)/shard_map/ppermute | solution.py:490
  131.6 1.4 collective-permute-done.9.swapped_ref
  133.0 0.6 chip_merge.7
  133.6 0.7 collective-permute-start.10
  134.3 0.0 collective-permute-done.10.came_ref
  134.3 2.0 %collective-permute-start.11 = (f32[184,256]{1,0:T(8,128)S(1)}, f32[184,256]{1,0:T(8,128)S(1)}, u32[]{:S(2)}, u32[]{:S(2)}) collective-permute-start(f32[184,256]{1,0:T(8,128)S(1)} %collective-permute-done.10.came_ref), channel_id=1, source_target_pairs={{0,8},{8,0},{16,24},{24,16},{32,40},{40,32},{48,56},{56,48},{64,72... | collective-permute-start | bytes 565256 | tf_op jit(solution)/shard_map/ppermute | solution.py:490
  136.4 1.3 collective-permute-done.11.swapped_ref
  137.6 0.6 last_merge.1
  138.2 1.3 collective-permute-start.12
  139.5 54.4 %collective-permute-done.12.brought_ref = f32[3,4,32]{2,1,0:T(4,128)S(1)} collective-permute-done((f32[3,4,32]{2,1,0:T(4,128)S(1)}, f32[3,4,32]{2,1,0:T(4,128)S(1)}, u32[]{:S(2)}, u32[]{:S(2)}) %collective-permute-start.12) | collective-permute-done | bytes 1568 | tf_op jit(solution)/shard_map/ppermute | solution.py:501
  193.9 1.1 pick.1
  (3 shorter events, 0.1 us)
Async XLA Ops:
  0.6 1.0 copy-start
  2.5 27.8 %all-to-all-start = ((bf16[8,2,32,512]{3,2,1,0:T(8,128)(2,1)}), bf16[8,2,32,512]{3,2,1,0:T(8,128)(2,1)S(1)}, u32[]{:S(2)}, u32[]{:S(2)}) async-start(bf16[8,2,32,512]{3,2,1,0:T(8,128)(2,1)} %shares.1), calls=%async_computation | async-start | bytes 1048576 | tf_op jit(solution)/shard_map/all_to_all | solution.py:422
  30.3 7.7 %collective-permute-start = (bf16[8,32,512]{2,1,0:T(8,128)(2,1)S(1)}, bf16[8,32,512]{2,1,0:T(8,128)(2,1)S(1)}, u32[]{:S(2)}, u32[]{:S(2)}) collective-permute-start(bf16[8,32,512]{2,1,0:T(8,128)(2,1)S(1)} %slice_bitcast_fusion), channel_id=1, source_target_pairs={{0,8},{8,16},{16,24},{24,32},{32,40},{40,48},{48,56},{56,64},{64,7... | collective-permute-start | bytes 786440 | tf_op jit(solution)/shard_map/ppermute | solution.py:474
  32.6 0.7 copy-start.2
  57.9 18.6 %copy-start.1 = (bf16[2,256,256]{2,1,0:T(8,128)(2,1)S(1)}, bf16[2,256,256]{2,1,0:T(8,128)(2,1)}, u32[]{:S(2)}) copy-start(bf16[2,256,256]{2,1,0:T(8,128)(2,1)} %coupling_ref.1) | copy-start | bytes 786436
  81.9 4.2 %collective-permute-start.1 = (f32[3,256,256]{2,1,0:T(8,128)S(1)}, f32[3,256,256]{2,1,0:T(8,128)S(1)}, u32[]{:S(2)}, u32[]{:S(2)}) collective-permute-start(f32[3,256,256]{2,1,0:T(8,128)S(1)} %leaf.1.own_ref), channel_id=1, source_target_pairs={{0,8},{8,0},{16,24},{24,16},{32,40},{40,32},{48,56},{56,48},{64,72... | collective-permute-start | bytes 2359304 | tf_op jit(solution)/shard_map/ppermute | solution.py:481
  90.6 13.4 %collective-permute-start.2 = (f32[264,256]{1,0:T(8,128)S(1)}, f32[264,256]{1,0:T(8,128)S(1)}, u32[]{:S(2)}, u32[]{:S(2)}) collective-permute-start(f32[264,256]{1,0:T(8,128)S(1)} %get-tuple-element.37), channel_id=1, source_target_pairs={{16,0},{24,8},{0,16},{8,24},{48,32},{56,40},{32,48},{40,56},{80,64... | collective-permute-start | bytes 811016 | tf_op jit(solution)/shard_map/ppermute | solution.py:489
  104.1 3.4 %collective-permute-start.3 = (f32[264,256]{1,0:T(8,128)S(1)}, f32[264,256]{1,0:T(8,128)S(1)}, u32[]{:S(2)}, u32[]{:S(2)}) collective-permute-start(f32[264,256]{1,0:T(8,128)S(1)} %collective-permute-done.2.came_ref), channel_id=1, source_target_pairs={{0,8},{8,0},{16,24},{24,16},{32,40},{40,32},{48,56},{56,48},{64,72... | collective-permute-start | bytes 811016 | tf_op jit(solution)/shard_map/ppermute | solution.py:490
  112.3 7.6 %collective-permute-start.4 = (f32[264,256]{1,0:T(8,128)S(1)}, f32[264,256]{1,0:T(8,128)S(1)}, u32[]{:S(2)}, u32[]{:S(2)}) collective-permute-start(f32[264,256]{1,0:T(8,128)S(1)} %get-tuple-element.39), channel_id=1, source_target_pairs={{32,0},{40,8},{16,48},{24,56},{96,64},{104,72},{80,112},{88,120},{... | collective-permute-start | bytes 811016 | tf_op jit(solution)/shard_map/ppermute | solution.py:489
  119.9 3.4 %collective-permute-start.5 = (f32[264,256]{1,0:T(8,128)S(1)}, f32[264,256]{1,0:T(8,128)S(1)}, u32[]{:S(2)}, u32[]{:S(2)}) collective-permute-start(f32[264,256]{1,0:T(8,128)S(1)} %collective-permute-done.4.came_ref), channel_id=1, source_target_pairs={{0,8},{8,0},{16,24},{24,16},{32,40},{40,32},{48,56},{56,48},{64,72... | collective-permute-start | bytes 811016 | tf_op jit(solution)/shard_map/ppermute | solution.py:490
  124.1 0.7 collective-permute-start.6
  124.8 3.4 %collective-permute-start.7 = (f32[264,256]{1,0:T(8,128)S(1)}, f32[264,256]{1,0:T(8,128)S(1)}, u32[]{:S(2)}, u32[]{:S(2)}) collective-permute-start(f32[264,256]{1,0:T(8,128)S(1)} %collective-permute-done.6.came_ref), channel_id=1, source_target_pairs={{0,8},{8,0},{16,24},{24,16},{32,40},{40,32},{48,56},{56,48},{64,72... | collective-permute-start | bytes 811016 | tf_op jit(solution)/shard_map/ppermute | solution.py:490
  128.9 0.7 collective-permute-start.8
  129.6 3.4 %collective-permute-start.9 = (f32[264,256]{1,0:T(8,128)S(1)}, f32[264,256]{1,0:T(8,128)S(1)}, u32[]{:S(2)}, u32[]{:S(2)}) collective-permute-start(f32[264,256]{1,0:T(8,128)S(1)} %collective-permute-done.8.came_ref), channel_id=1, source_target_pairs={{0,8},{8,0},{16,24},{24,16},{32,40},{40,32},{48,56},{56,48},{64,72... | collective-permute-start | bytes 811016 | tf_op jit(solution)/shard_map/ppermute | solution.py:490
  133.6 0.7 collective-permute-start.10
  134.3 3.3 %collective-permute-start.11 = (f32[184,256]{1,0:T(8,128)S(1)}, f32[184,256]{1,0:T(8,128)S(1)}, u32[]{:S(2)}, u32[]{:S(2)}) collective-permute-start(f32[184,256]{1,0:T(8,128)S(1)} %collective-permute-done.10.came_ref), channel_id=1, source_target_pairs={{0,8},{8,0},{16,24},{24,16},{32,40},{40,32},{48,56},{56,48},{64,72... | collective-permute-start | bytes 565256 | tf_op jit(solution)/shard_map/ppermute | solution.py:490
  138.2 55.7 %collective-permute-start.12 = (f32[3,4,32]{2,1,0:T(4,128)S(1)}, f32[3,4,32]{2,1,0:T(4,128)S(1)}, u32[]{:S(2)}, u32[]{:S(2)}) collective-permute-start(f32[3,4,32]{2,1,0:T(4,128)S(1)} %get-tuple-element.47), channel_id=1, source_target_pairs={{0,16},{8,24},{48,32},{56,40},{64,80},{72,88},{112,96},{120,104},{... | collective-permute-start | bytes 4616 | tf_op jit(solution)/shard_map/ppermute | solution.py:501

commit v7 on v6

--- a/solution.py
+++ b/solution.py
@@ -118,28 +118,30 @@
     send_ref[n : n + 8] = jnp.broadcast_to(diagonal, (8, n))
 
 
-def leaf_kernel(flags_ref, margin_ref, cot_ref, csc_ref, coupling_ref, out_ref, d_ref, x_ref, a_ref, b_ref, c_ref):
+def leaf_kernel(flags_ref, margin_ref, cot_ref, csc_ref, coupling_ref, out_ref, d_ref, x_ref):
     n = d_ref.shape[0]
     row, column = grid_of(n)
     half_step = 0.5 / (2 * flags_ref[1]).astype(F32)
 
-    def sector(s):
-        margin = margin_ref[:, s].reshape(n, n)
-        if s == 0:
-            margin = jnp.where(flags_ref[0] == 0, unit(n), margin)
-        inner = jnp.where(row == column, cot_ref[s : s + 1, :], F32(0)) + half_step * coupling_ref[s].astype(F32)
-        m = parts(margin)
-        a_ref[s] = dot6(parts(dot6(m, parts(inner))), m, NT)
-        b_ref[s] = margin * csc_ref[s : s + 1, :]
-        c_ref[s] = inner
-
-    sector(1)
-    sector(0)
-    blocks = (a_ref, b_ref, c_ref)
-    merge_blocks(
-        c_ref[0] + a_ref[1], 0, d_ref, x_ref,
-        lambda x: combine(lambda i: blocks[i][0], lambda i: blocks[i][1], x, out_ref),
-    )
+    def inner(s):
+        diagonal = jnp.where(row == column, cot_ref[s : s + 1, :], F32(0))
+        return diagonal + half_step * coupling_ref[s].astype(F32)
+
+    second = margin_ref[:, 1].reshape(n, n)
+    m1 = parts(second)
+    a1 = dot6(parts(dot6(m1, parts(inner(1)))), m1, NT)
+
+    def finish(x):
+        m0 = parts(jnp.where(flags_ref[0] == 0, unit(n), margin_ref[:, 0].reshape(n, n)))
+        csc = csc_ref[0:1, :]
+        csc_down = jnp.sum(jnp.where(row == column, csc, F32(0)), axis=1, keepdims=True)
+        b2 = parts(margin_ref[:, 1].reshape(n, n) * csc_ref[1:2, :])
+        w2 = dot6(parts(x), b2)
+        out_ref[0] = dot6(parts(dot6(m0, parts(inner(0) - csc_down * x * csc))), m0, NT)
+        out_ref[1] = dot6(m0, parts(csc_down * w2))
+        out_ref[2] = inner(1) - dot6(b2, parts(w2), TN)
+
+    merge_blocks(inner(0) + a1, 0, d_ref, x_ref, finish)
 
 
 def leaf(flags, margin, cot, csc, coupling):
@@ -149,7 +151,7 @@
         out_shape=jax.ShapeDtypeStruct((3, n, n), F32),
         in_specs=[SMEM, VMEM, VMEM, VMEM, VMEM],
         out_specs=VMEM,
-        scratch_shapes=[pltpu.VMEM((n, n), F32)] * 2 + [pltpu.VMEM((2, n, n), F32)] * 3,
+        scratch_shapes=[pltpu.VMEM((n, n), F32)] * 2,
         compiler_params=PARAMS,
         name="leaf",
     )(flags, margin, cot, csc, coupling)

time: 196 us -> 196 us (level)
  no operation moved by 1% of the time
where the time goes in v7:
time: 196 us; the launch traced here: 195 us
  waiting for transfers between devices  99 us (51%)
  blocking collectives  38.1 us (19%)
  starting transfers between devices  35.4 us (18%)
  Pallas kernels  19.9 us (10%)
    ppermute x1, waiting for transfers between devices, per_device(): brought = lax.ppermute(for_next, 'sector', pairs)  54.4 us
    all_to_all x2, blocking collectives, exchange(): lax.all_to_all(array, 'chan', split_axis=0, concat_axis=0, tiled=True)  38.1 us
    all_to_all x1, waiting for transfers between devices, exchange(): lax.all_to_all(array, 'chan', split_axis=0, concat_axis=0, tiled=True)  17.5 us
    ppermute x5, waiting for transfers between devices, per_device(): came = lax.ppermute(send, 'sector', pairs)  13.1 us
    all_to_all x1, starting transfers between devices, exchange(): lax.all_to_all(array, 'chan', split_axis=0, concat_axis=0, tiled=True)  10.3 us
    ppermute x5, starting transfers between devices, per_device(): came = lax.ppermute(send, 'sector', pairs)  10 us
    ppermute x5, starting transfers between devices, per_device(): swapped = lax.ppermute(came, 'sector', cores)  9.95 us
    ppermute x5, waiting for transfers between devices, per_device(): swapped = lax.ppermute(came, 'sector', cores)  7.07 us
  transfers between devices with their start and end apart: 14, of which 11 were waited for; matrix products, arithmetic and copies ran while one was open for 0% of the time, Pallas kernels for 0%

profile of v7, /device:TPU:22, one launch (start us, length us, event | category | flops | bytes accessed | tf_op | source)
XLA Modules:
  0.0 195.1 jit_solution(581953865864730927)
XLA Ops:
  0.6 0.0 copy-start
  0.6 1.0 copy-done
  1.7 0.8 shares.1
  2.5 10.3 %all-to-all-start = ((bf16[8,2,32,512]{3,2,1,0:T(8,128)(2,1)}), bf16[8,2,32,512]{3,2,1,0:T(8,128)(2,1)S(1)}, u32[]{:S(2)}, u32[]{:S(2)}) async-start(bf16[8,2,32,512]{3,2,1,0:T(8,128)(2,1)} %shares.1), calls=%async_computation | async-start | bytes 1048576 | tf_op jit(solution)/shard_map/all_to_all | solution.py:424
  12.8 17.5 %all-to-all-done.own_ref = bf16[8,2,32,512]{3,2,1,0:T(8,128)(2,1)S(1)} async-done(((bf16[8,2,32,512]{3,2,1,0:T(8,128)(2,1)}), bf16[8,2,32,512]{3,2,1,0:T(8,128)(2,1)S(1)}, u32[]{:S(2)}, u32[]{:S(2)}) %all-to-all-start) | async-done | bytes 524320 | tf_op jit(solution)/shard_map/all_to_all | solution.py:424
  30.3 1.9 collective-permute-start
  32.3 0.3 inner_parts.1.inner_ref
  32.6 0.0 copy-start.2
  32.6 0.1 stack.50.flags_ref
  32.7 0.6 copy-done.2
  33.3 4.7 %collective-permute-done.before_ref = bf16[8,32,512]{2,1,0:T(8,128)(2,1)S(1)} collective-permute-done((bf16[8,32,512]{2,1,0:T(8,128)(2,1)S(1)}, bf16[8,32,512]{2,1,0:T(8,128)(2,1)S(1)}, u32[]{:S(2)}, u32[]{:S(2)}) %collective-permute-start) | collective-permute-done | bytes 262176 | tf_op jit(solution)/shard_map/ppermute | solution.py:476
  38.0 0.3 margin_parts.1
  38.3 19.6 %all_to_all.15.partial_ref = f32[8,2,32,256]{3,2,1,0:T(8,128)S(1)} all-to-all(f32[8,2,32,256]{3,2,1,0:T(8,128)S(1)} %margin_parts.1), channel_id=1, replica_groups=mesh['sector'=64,'chan'=8] {'chan'}, dimensions={0} | all-to-all | bytes 1048576 | tf_op jit(solution)/shard_map/all_to_all | solution.py:424
  57.9 0.0 copy-start.1
  57.9 18.6 %all_to_all.16.margin_ref = f32[8,2,32,256]{3,2,1,0:T(8,128)S(1)} all-to-all(f32[8,2,32,256]{3,2,1,0:T(8,128)S(1)} %total_for_all.1), channel_id=1, replica_groups=mesh['sector'=64,'chan'=8] {'chan'}, dimensions={0} | all-to-all | bytes 1048576 | tf_op jit(solution)/shard_map/all_to_all | solution.py:424
  76.5 0.0 copy-done.1
  76.5 5.5 %leaf.1.own_ref = f32[3,256,256]{2,1,0:T(8,128)S(1)} custom-call(s32[15]{0:T(128)S(1)} %stack.50.flags_ref, f32[8,2,32,256]{3,2,1,0:T(8,128)S(1)} %all_to_all.16.margin_ref, f32[2,256]{1,0:T(2,128)S(1)} %get-tuple-element.34.cot_ref, f32[2,256]{1,0:T(2,128)S(1)} %get-tuple-element.35.csc_ref, bf16[2,256,256]{2,1,0:T(8,128)(2,1)S(1)} %copy-done.1), custom_call_target="tpu_custom_call" | custom-call | tf_op jit(solution)/shard_map/leaf/pallas_call | solution.py:149
  82.0 1.9 collective-permute-start.1
  83.9 2.3 %collective-permute-done.1.other_ref = f32[3,256,256]{2,1,0:T(8,128)S(1)} collective-permute-done((f32[3,256,256]{2,1,0:T(8,128)S(1)}, f32[3,256,256]{2,1,0:T(8,128)S(1)}, u32[]{:S(2)}, u32[]{:S(2)}) %collective-permute-start.1) | collective-permute-done | bytes 786464 | tf_op jit(solution)/shard_map/ppermute | solution.py:483
  86.2 4.5 %core_merge.1 = (f32[3,256,256]{2,1,0:T(8,128)S(1)}, f32[264,256]{1,0:T(8,128)S(1)}) custom-call(s32[15]{0:T(128)S(1)} %stack.50.flags_ref, f32[3,256,256]{2,1,0:T(8,128)S(1)} %leaf.1.own_ref, f32[3,256,256]{2,1,0:T(8,128)S(1)} %collective-permute-done.1.other_ref), custom_call_target="tpu_custom_call" | custom-call | tf_op jit(solution)/shard_map/core_merge/pallas_call | solution.py:184
  90.7 6.7 %collective-permute-start.2 = (f32[264,256]{1,0:T(8,128)S(1)}, f32[264,256]{1,0:T(8,128)S(1)}, u32[]{:S(2)}, u32[]{:S(2)}) collective-permute-start(f32[264,256]{1,0:T(8,128)S(1)} %get-tuple-element.37), channel_id=1, source_target_pairs={{16,0},{24,8},{0,16},{8,24},{48,32},{56,40},{32,48},{40,56},{80,64... | collective-permute-start | bytes 811016 | tf_op jit(solution)/shard_map/ppermute | solution.py:491
  97.4 6.8 %collective-permute-done.2.came_ref = f32[264,256]{1,0:T(8,128)S(1)} collective-permute-done((f32[264,256]{1,0:T(8,128)S(1)}, f32[264,256]{1,0:T(8,128)S(1)}, u32[]{:S(2)}, u32[]{:S(2)}) %collective-permute-start.2) | collective-permute-done | bytes 270368 | tf_op jit(solution)/shard_map/ppermute | solution.py:491
  104.1 1.9 collective-permute-start.3
  106.0 1.5 collective-permute-done.3.swapped_ref
  107.6 4.8 %chip_merge.4 = (f32[3,256,256]{2,1,0:T(8,128)S(1)}, f32[264,256]{1,0:T(8,128)S(1)}) custom-call(s32[15]{0:T(128)S(1)} %stack.50.flags_ref, f32[3,256,256]{2,1,0:T(8,128)S(1)} %get-tuple-element.36.own_ref, f32[264,256]{1,0:T(8,128)S(1)} %collective-permute-done.2.came_ref, f32[264,256]{1,0:T(8,128)S(1)} %collective-permute-done.3.swapped_ref), custom_call_target="tpu_custom_call" | custom-call | tf_op jit(solution)/shard_map/chip_merge/pallas_call | solution.py:247
  112.3 1.3 collective-permute-start.4
  113.6 6.3 %collective-permute-done.4.came_ref = f32[264,256]{1,0:T(8,128)S(1)} collective-permute-done((f32[264,256]{1,0:T(8,128)S(1)}, f32[264,256]{1,0:T(8,128)S(1)}, u32[]{:S(2)}, u32[]{:S(2)}) %collective-permute-start.4) | collective-permute-done | bytes 270368 | tf_op jit(solution)/shard_map/ppermute | solution.py:491
  119.9 1.9 collective-permute-start.5
  121.8 1.5 collective-permute-done.5.swapped_ref
  123.4 0.8 chip_merge.5
  124.2 0.7 collective-permute-start.6
  124.8 0.0 collective-permute-done.6.came_ref
  124.9 2.0 %collective-permute-start.7 = (f32[264,256]{1,0:T(8,128)S(1)}, f32[264,256]{1,0:T(8,128)S(1)}, u32[]{:S(2)}, u32[]{:S(2)}) collective-permute-start(f32[264,256]{1,0:T(8,128)S(1)} %collective-permute-done.6.came_ref), channel_id=1, source_target_pairs={{0,8},{8,0},{16,24},{24,16},{32,40},{40,32},{48,56},{56,48},{64,72... | collective-permute-start | bytes 811016 | tf_op jit(solution)/shard_map/ppermute | solution.py:492
  126.9 1.4 collective-permute-done.7.swapped_ref
  128.3 0.6 chip_merge.6
  128.9 0.7 collective-permute-start.8
  129.6 0.0 collective-permute-done.8.came_ref
  129.6 2.0 %collective-permute-start.9 = (f32[264,256]{1,0:T(8,128)S(1)}, f32[264,256]{1,0:T(8,128)S(1)}, u32[]{:S(2)}, u32[]{:S(2)}) collective-permute-start(f32[264,256]{1,0:T(8,128)S(1)} %collective-permute-done.8.came_ref), channel_id=1, source_target_pairs={{0,8},{8,0},{16,24},{24,16},{32,40},{40,32},{48,56},{56,48},{64,72... | collective-permute-start | bytes 811016 | tf_op jit(solution)/shard_map/ppermute | solution.py:492
  131.7 1.4 collective-permute-done.9.swapped_ref
  133.1 0.6 chip_merge.7
  133.7 0.7 collective-permute-start.10
  134.4 0.0 collective-permute-done.10.came_ref
  134.4 2.0 %collective-permute-start.11 = (f32[184,256]{1,0:T(8,128)S(1)}, f32[184,256]{1,0:T(8,128)S(1)}, u32[]{:S(2)}, u32[]{:S(2)}) collective-permute-start(f32[184,256]{1,0:T(8,128)S(1)} %collective-permute-done.10.came_ref), channel_id=1, source_target_pairs={{0,8},{8,0},{16,24},{24,16},{32,40},{40,32},{48,56},{56,48},{64,72... | collective-permute-start | bytes 565256 | tf_op jit(solution)/shard_map/ppermute | solution.py:492
  136.4 1.3 collective-permute-done.11.swapped_ref
  137.7 0.6 last_merge.1
  138.3 1.3 collective-permute-start.12
  139.6 54.4 %collective-permute-done.12.brought_ref = f32[3,4,32]{2,1,0:T(4,128)S(1)} collective-permute-done((f32[3,4,32]{2,1,0:T(4,128)S(1)}, f32[3,4,32]{2,1,0:T(4,128)S(1)}, u32[]{:S(2)}, u32[]{:S(2)}) %collective-permute-start.12) | collective-permute-done | bytes 1568 | tf_op jit(solution)/shard_map/ppermute | solution.py:503
  194.0 1.1 pick.1
  (3 shorter events, 0.1 us)
Async XLA Ops:
  0.6 1.0 copy-start
  2.5 27.8 %all-to-all-start = ((bf16[8,2,32,512]{3,2,1,0:T(8,128)(2,1)}), bf16[8,2,32,512]{3,2,1,0:T(8,128)(2,1)S(1)}, u32[]{:S(2)}, u32[]{:S(2)}) async-start(bf16[8,2,32,512]{3,2,1,0:T(8,128)(2,1)} %shares.1), calls=%async_computation | async-start | bytes 1048576 | tf_op jit(solution)/shard_map/all_to_all | solution.py:424
  30.3 7.7 %collective-permute-start = (bf16[8,32,512]{2,1,0:T(8,128)(2,1)S(1)}, bf16[8,32,512]{2,1,0:T(8,128)(2,1)S(1)}, u32[]{:S(2)}, u32[]{:S(2)}) collective-permute-start(bf16[8,32,512]{2,1,0:T(8,128)(2,1)S(1)} %slice_bitcast_fusion), channel_id=1, source_target_pairs={{0,8},{8,16},{16,24},{24,32},{32,40},{40,48},{48,56},{56,64},{64,7... | collective-permute-start | bytes 786440 | tf_op jit(solution)/shard_map/ppermute | solution.py:476
  32.6 0.7 copy-start.2
  57.9 18.6 %copy-start.1 = (bf16[2,256,256]{2,1,0:T(8,128)(2,1)S(1)}, bf16[2,256,256]{2,1,0:T(8,128)(2,1)}, u32[]{:S(2)}) copy-start(bf16[2,256,256]{2,1,0:T(8,128)(2,1)} %coupling_ref.1) | copy-start | bytes 786436
  82.0 4.2 %collective-permute-start.1 = (f32[3,256,256]{2,1,0:T(8,128)S(1)}, f32[3,256,256]{2,1,0:T(8,128)S(1)}, u32[]{:S(2)}, u32[]{:S(2)}) collective-permute-start(f32[3,256,256]{2,1,0:T(8,128)S(1)} %leaf.1.own_ref), channel_id=1, source_target_pairs={{0,8},{8,0},{16,24},{24,16},{32,40},{40,32},{48,56},{56,48},{64,72... | collective-permute-start | bytes 2359304 | tf_op jit(solution)/shard_map/ppermute | solution.py:483
  90.7 13.4 %collective-permute-start.2 = (f32[264,256]{1,0:T(8,128)S(1)}, f32[264,256]{1,0:T(8,128)S(1)}, u32[]{:S(2)}, u32[]{:S(2)}) collective-permute-start(f32[264,256]{1,0:T(8,128)S(1)} %get-tuple-element.37), channel_id=1, source_target_pairs={{16,0},{24,8},{0,16},{8,24},{48,32},{56,40},{32,48},{40,56},{80,64... | collective-permute-start | bytes 811016 | tf_op jit(solution)/shard_map/ppermute | solution.py:491
  104.1 3.4 %collective-permute-start.3 = (f32[264,256]{1,0:T(8,128)S(1)}, f32[264,256]{1,0:T(8,128)S(1)}, u32[]{:S(2)}, u32[]{:S(2)}) collective-permute-start(f32[264,256]{1,0:T(8,128)S(1)} %collective-permute-done.2.came_ref), channel_id=1, source_target_pairs={{0,8},{8,0},{16,24},{24,16},{32,40},{40,32},{48,56},{56,48},{64,72... | collective-permute-start | bytes 811016 | tf_op jit(solution)/shard_map/ppermute | solution.py:492
  112.3 7.6 %collective-permute-start.4 = (f32[264,256]{1,0:T(8,128)S(1)}, f32[264,256]{1,0:T(8,128)S(1)}, u32[]{:S(2)}, u32[]{:S(2)}) collective-permute-start(f32[264,256]{1,0:T(8,128)S(1)} %get-tuple-element.39), channel_id=1, source_target_pairs={{32,0},{40,8},{16,48},{24,56},{96,64},{104,72},{80,112},{88,120},{... | collective-permute-start | bytes 811016 | tf_op jit(solution)/shard_map/ppermute | solution.py:491
  119.9 3.4 %collective-permute-start.5 = (f32[264,256]{1,0:T(8,128)S(1)}, f32[264,256]{1,0:T(8,128)S(1)}, u32[]{:S(2)}, u32[]{:S(2)}) collective-permute-start(f32[264,256]{1,0:T(8,128)S(1)} %collective-permute-done.4.came_ref), channel_id=1, source_target_pairs={{0,8},{8,0},{16,24},{24,16},{32,40},{40,32},{48,56},{56,48},{64,72... | collective-permute-start | bytes 811016 | tf_op jit(solution)/shard_map/ppermute | solution.py:492
  124.2 0.7 collective-permute-start.6
  124.9 3.4 %collective-permute-start.7 = (f32[264,256]{1,0:T(8,128)S(1)}, f32[264,256]{1,0:T(8,128)S(1)}, u32[]{:S(2)}, u32[]{:S(2)}) collective-permute-start(f32[264,256]{1,0:T(8,128)S(1)} %collective-permute-done.6.came_ref), channel_id=1, source_target_pairs={{0,8},{8,0},{16,24},{24,16},{32,40},{40,32},{48,56},{56,48},{64,72... | collective-permute-start | bytes 811016 | tf_op jit(solution)/shard_map/ppermute | solution.py:492
  128.9 0.7 collective-permute-start.8
  129.6 3.4 %collective-permute-start.9 = (f32[264,256]{1,0:T(8,128)S(1)}, f32[264,256]{1,0:T(8,128)S(1)}, u32[]{:S(2)}, u32[]{:S(2)}) collective-permute-start(f32[264,256]{1,0:T(8,128)S(1)} %collective-permute-done.8.came_ref), channel_id=1, source_target_pairs={{0,8},{8,0},{16,24},{24,16},{32,40},{40,32},{48,56},{56,48},{64,72... | collective-permute-start | bytes 811016 | tf_op jit(solution)/shard_map/ppermute | solution.py:492
  133.7 0.7 collective-permute-start.10
  134.4 3.3 %collective-permute-start.11 = (f32[184,256]{1,0:T(8,128)S(1)}, f32[184,256]{1,0:T(8,128)S(1)}, u32[]{:S(2)}, u32[]{:S(2)}) collective-permute-start(f32[184,256]{1,0:T(8,128)S(1)} %collective-permute-done.10.came_ref), channel_id=1, source_target_pairs={{0,8},{8,0},{16,24},{24,16},{32,40},{40,32},{48,56},{56,48},{64,72... | collective-permute-start | bytes 565256 | tf_op jit(solution)/shard_map/ppermute | solution.py:492
  138.3 55.7 %collective-permute-start.12 = (f32[3,4,32]{2,1,0:T(4,128)S(1)}, f32[3,4,32]{2,1,0:T(4,128)S(1)}, u32[]{:S(2)}, u32[]{:S(2)}) collective-permute-start(f32[3,4,32]{2,1,0:T(4,128)S(1)} %get-tuple-element.47), channel_id=1, source_target_pairs={{0,16},{8,24},{48,32},{56,40},{64,80},{72,88},{112,96},{120,104},{... | collective-permute-start | bytes 4616 | tf_op jit(solution)/shard_map/ppermute | solution.py:503

commit v8 on v6

--- a/solution.py
+++ b/solution.py
@@ -321,22 +321,6 @@
         compiler_params=PARAMS,
         name="last_merge",
     )(flags, own, came, swapped)
-
-
-def pick_kernel(level, flags_ref, mine_ref, brought_ref, a_ref, b_ref, c_ref):
-    for i, ref in enumerate((a_ref, b_ref, c_ref)):
-        ref[...] = jnp.where(flags_ref[4 + 2 * level] == 1, mine_ref[i], brought_ref[i])
-
-
-def pick(level, flags, mine, brought):
-    return pl.pallas_call(
-        functools.partial(pick_kernel, level),
-        out_shape=(jax.ShapeDtypeStruct(mine.shape[1:], F32),) * 3,
-        in_specs=[SMEM, VMEM, VMEM],
-        out_specs=(VMEM,) * 3,
-        compiler_params=pltpu.CompilerParams(vmem_limit_bytes=2**20),
-        name="pick",
-    )(flags, mine, brought)
 
 
 def shares_kernel(whole_ref, out_ref):
@@ -499,7 +483,8 @@
         if yi not in ENDS:
             pairs.append((spot(xi, yi ^ 1, ci), i))
     brought = lax.ppermute(for_next, "sector", pairs)
-    return tuple(block.T for block in pick(len(plan) - 1, flags, mine, brought))
+    result = mine + brought
+    return tuple(result[i].T for i in range(3))
 
 
 def solution(mesh):

time: 196 us -> 195 us (level)
  no operation moved by 1% of the time
where the time goes in v8:
time: 195 us
  waiting for transfers between devices  99 us (51%)
  blocking collectives  38.1 us (20%)
  starting transfers between devices  35.4 us (18%)
  Pallas kernels  18.7 us (10%)
  local copies, waits for them, and re-layouts  2.32 us (1%)
    ppermute x1, waiting for transfers between devices, per_device(): brought = lax.ppermute(for_next, 'sector', pairs)  54.4 us
    all_to_all x2, blocking collectives, exchange(): lax.all_to_all(array, 'chan', split_axis=0, concat_axis=0, tiled=True)  38.1 us
    all_to_all x1, waiting for transfers between devices, exchange(): lax.all_to_all(array, 'chan', split_axis=0, concat_axis=0, tiled=True)  17.5 us
    ppermute x5, waiting for transfers between devices, per_device(): came = lax.ppermute(send, 'sector', pairs)  13.1 us
    all_to_all x1, starting transfers between devices, exchange(): lax.all_to_all(array, 'chan', split_axis=0, concat_axis=0, tiled=True)  10.3 us
    ppermute x5, starting transfers between devices, per_device(): came = lax.ppermute(send, 'sector', pairs)  10 us
    ppermute x5, starting transfers between devices, per_device(): swapped = lax.ppermute(came, 'sector', cores)  9.95 us
    ppermute x5, waiting for transfers between devices, per_device(): swapped = lax.ppermute(came, 'sector', cores)  7.07 us
  transfers between devices with their start and end apart: 14, of which 11 were waited for; matrix products, arithmetic and copies ran while one was open for 0% of the time, Pallas kernels for 0%

profile of v8, /device:TPU:22, one launch (start us, length us, event | category | flops | bytes accessed | tf_op | source)
XLA Modules:
  0.0 194.5 jit_solution(589625300106823403)
XLA Ops:
  0.6 0.0 copy-start
  0.6 1.0 copy-done
  1.7 0.8 shares.1
  2.5 10.3 %all-to-all-start = ((bf16[8,2,32,512]{3,2,1,0:T(8,128)(2,1)}), bf16[8,2,32,512]{3,2,1,0:T(8,128)(2,1)S(1)}, u32[]{:S(2)}, u32[]{:S(2)}) async-start(bf16[8,2,32,512]{3,2,1,0:T(8,128)(2,1)} %shares.1), calls=%async_computation | async-start | bytes 1048576 | tf_op jit(solution)/shard_map/all_to_all | solution.py:406
  12.8 17.5 %all-to-all-done.own_ref = bf16[8,2,32,512]{3,2,1,0:T(8,128)(2,1)S(1)} async-done(((bf16[8,2,32,512]{3,2,1,0:T(8,128)(2,1)}), bf16[8,2,32,512]{3,2,1,0:T(8,128)(2,1)S(1)}, u32[]{:S(2)}, u32[]{:S(2)}) %all-to-all-start) | async-done | bytes 524320 | tf_op jit(solution)/shard_map/all_to_all | solution.py:406
  30.3 1.9 collective-permute-start
  32.3 0.3 inner_parts.1.inner_ref
  32.6 0.0 copy-start.2
  32.6 0.1 stack.50.flags_ref
  32.7 0.6 copy-done.2
  33.3 4.7 %collective-permute-done.before_ref = bf16[8,32,512]{2,1,0:T(8,128)(2,1)S(1)} collective-permute-done((bf16[8,32,512]{2,1,0:T(8,128)(2,1)S(1)}, bf16[8,32,512]{2,1,0:T(8,128)(2,1)S(1)}, u32[]{:S(2)}, u32[]{:S(2)}) %collective-permute-start) | collective-permute-done | bytes 262176 | tf_op jit(solution)/shard_map/ppermute | solution.py:458
  38.0 0.3 margin_parts.1
  38.3 19.6 %all_to_all.15.partial_ref = f32[8,2,32,256]{3,2,1,0:T(8,128)S(1)} all-to-all(f32[8,2,32,256]{3,2,1,0:T(8,128)S(1)} %margin_parts.1), channel_id=1, replica_groups=mesh['sector'=64,'chan'=8] {'chan'}, dimensions={0} | all-to-all | bytes 1048576 | tf_op jit(solution)/shard_map/all_to_all | solution.py:406
  57.9 0.0 copy-start.1
  57.9 18.6 %all_to_all.16.margin_ref = f32[8,2,32,256]{3,2,1,0:T(8,128)S(1)} all-to-all(f32[8,2,32,256]{3,2,1,0:T(8,128)S(1)} %total_for_all.1), channel_id=1, replica_groups=mesh['sector'=64,'chan'=8] {'chan'}, dimensions={0} | all-to-all | bytes 1048576 | tf_op jit(solution)/shard_map/all_to_all | solution.py:406
  76.5 0.0 copy-done.1
  76.5 5.4 %leaf.1.own_ref = f32[3,256,256]{2,1,0:T(8,128)S(1)} custom-call(s32[15]{0:T(128)S(1)} %stack.50.flags_ref, f32[8,2,32,256]{3,2,1,0:T(8,128)S(1)} %all_to_all.16.margin_ref, f32[2,256]{1,0:T(2,128)S(1)} %get-tuple-element.31.cot_ref, f32[2,256]{1,0:T(2,128)S(1)} %get-tuple-element.32.csc_ref, bf16[2,256,256]{2,1,0:T(8,128)(2,1)S(1)} %copy-done.1), custom_call_target="tpu_custom_call" | custom-call | tf_op jit(solution)/shard_map/leaf/pallas_call | solution.py:147
  81.9 1.9 collective-permute-start.1
  83.8 2.3 %collective-permute-done.1.other_ref = f32[3,256,256]{2,1,0:T(8,128)S(1)} collective-permute-done((f32[3,256,256]{2,1,0:T(8,128)S(1)}, f32[3,256,256]{2,1,0:T(8,128)S(1)}, u32[]{:S(2)}, u32[]{:S(2)}) %collective-permute-start.1) | collective-permute-done | bytes 786464 | tf_op jit(solution)/shard_map/ppermute | solution.py:465
  86.1 4.5 %core_merge.1 = (f32[3,256,256]{2,1,0:T(8,128)S(1)}, f32[264,256]{1,0:T(8,128)S(1)}) custom-call(s32[15]{0:T(128)S(1)} %stack.50.flags_ref, f32[3,256,256]{2,1,0:T(8,128)S(1)} %leaf.1.own_ref, f32[3,256,256]{2,1,0:T(8,128)S(1)} %collective-permute-done.1.other_ref), custom_call_target="tpu_custom_call" | custom-call | tf_op jit(solution)/shard_map/core_merge/pallas_call | solution.py:182
  90.6 6.7 %collective-permute-start.2 = (f32[264,256]{1,0:T(8,128)S(1)}, f32[264,256]{1,0:T(8,128)S(1)}, u32[]{:S(2)}, u32[]{:S(2)}) collective-permute-start(f32[264,256]{1,0:T(8,128)S(1)} %get-tuple-element.34), channel_id=1, source_target_pairs={{16,0},{24,8},{0,16},{8,24},{48,32},{56,40},{32,48},{40,56},{80,64... | collective-permute-start | bytes 811016 | tf_op jit(solution)/shard_map/ppermute | solution.py:473
  97.3 6.8 %collective-permute-done.2.came_ref = f32[264,256]{1,0:T(8,128)S(1)} collective-permute-done((f32[264,256]{1,0:T(8,128)S(1)}, f32[264,256]{1,0:T(8,128)S(1)}, u32[]{:S(2)}, u32[]{:S(2)}) %collective-permute-start.2) | collective-permute-done | bytes 270368 | tf_op jit(solution)/shard_map/ppermute | solution.py:473
  104.1 1.9 collective-permute-start.3
  106.0 1.5 collective-permute-done.3.swapped_ref
  107.5 4.8 %chip_merge.4 = (f32[3,256,256]{2,1,0:T(8,128)S(1)}, f32[264,256]{1,0:T(8,128)S(1)}) custom-call(s32[15]{0:T(128)S(1)} %stack.50.flags_ref, f32[3,256,256]{2,1,0:T(8,128)S(1)} %get-tuple-element.33.own_ref, f32[264,256]{1,0:T(8,128)S(1)} %collective-permute-done.2.came_ref, f32[264,256]{1,0:T(8,128)S(1)} %collective-permute-done.3.swapped_ref), custom_call_target="tpu_custom_call" | custom-call | tf_op jit(solution)/shard_map/chip_merge/pallas_call | solution.py:245
  112.3 1.3 collective-permute-start.4
  113.6 6.3 %collective-permute-done.4.came_ref = f32[264,256]{1,0:T(8,128)S(1)} collective-permute-done((f32[264,256]{1,0:T(8,128)S(1)}, f32[264,256]{1,0:T(8,128)S(1)}, u32[]{:S(2)}, u32[]{:S(2)}) %collective-permute-start.4) | collective-permute-done | bytes 270368 | tf_op jit(solution)/shard_map/ppermute | solution.py:473
  119.9 1.9 collective-permute-start.5
  121.8 1.5 collective-permute-done.5.swapped_ref
  123.3 0.8 chip_merge.5
  124.1 0.7 collective-permute-start.6
  124.8 0.0 collective-permute-done.6.came_ref
  124.8 2.0 %collective-permute-start.7 = (f32[264,256]{1,0:T(8,128)S(1)}, f32[264,256]{1,0:T(8,128)S(1)}, u32[]{:S(2)}, u32[]{:S(2)}) collective-permute-start(f32[264,256]{1,0:T(8,128)S(1)} %collective-permute-done.6.came_ref), channel_id=1, source_target_pairs={{0,8},{8,0},{16,24},{24,16},{32,40},{40,32},{48,56},{56,48},{64,72... | collective-permute-start | bytes 811016 | tf_op jit(solution)/shard_map/ppermute | solution.py:474
  126.9 1.4 collective-permute-done.7.swapped_ref
  128.3 0.6 chip_merge.6
  128.9 0.7 collective-permute-start.8
  129.6 0.0 collective-permute-done.8.came_ref
  129.6 2.0 %collective-permute-start.9 = (f32[264,256]{1,0:T(8,128)S(1)}, f32[264,256]{1,0:T(8,128)S(1)}, u32[]{:S(2)}, u32[]{:S(2)}) collective-permute-start(f32[264,256]{1,0:T(8,128)S(1)} %collective-permute-done.8.came_ref), channel_id=1, source_target_pairs={{0,8},{8,0},{16,24},{24,16},{32,40},{40,32},{48,56},{56,48},{64,72... | collective-permute-start | bytes 811016 | tf_op jit(solution)/shard_map/ppermute | solution.py:474
  131.6 1.4 collective-permute-done.9.swapped_ref
  133.0 0.6 chip_merge.7
  133.6 0.7 collective-permute-start.10
  134.3 0.0 collective-permute-done.10.came_ref
  134.3 2.0 %collective-permute-start.11 = (f32[184,256]{1,0:T(8,128)S(1)}, f32[184,256]{1,0:T(8,128)S(1)}, u32[]{:S(2)}, u32[]{:S(2)}) collective-permute-start(f32[184,256]{1,0:T(8,128)S(1)} %collective-permute-done.10.came_ref), channel_id=1, source_target_pairs={{0,8},{8,0},{16,24},{24,16},{32,40},{40,32},{48,56},{56,48},{64,72... | collective-permute-start | bytes 565256 | tf_op jit(solution)/shard_map/ppermute | solution.py:474
  136.4 1.3 collective-permute-done.11.swapped_ref
  137.6 0.6 last_merge.1
  138.2 1.3 collective-permute-start.12
  139.5 54.4 %collective-permute-done.12 = f32[3,4,32]{2,1,0:T(4,128)S(1)} collective-permute-done((f32[3,4,32]{2,1,0:T(4,128)S(1)}, f32[3,4,32]{2,1,0:T(4,128)S(1)}, u32[]{:S(2)}, u32[]{:S(2)}) %collective-permute-start.12) | collective-permute-done | bytes 1568 | tf_op jit(solution)/shard_map/ppermute | solution.py:485
  193.9 0.6 slice_bitcast_fusion.1
  (4 shorter events, 0.1 us)
Async XLA Ops:
  0.6 1.0 copy-start
  2.5 27.8 %all-to-all-start = ((bf16[8,2,32,512]{3,2,1,0:T(8,128)(2,1)}), bf16[8,2,32,512]{3,2,1,0:T(8,128)(2,1)S(1)}, u32[]{:S(2)}, u32[]{:S(2)}) async-start(bf16[8,2,32,512]{3,2,1,0:T(8,128)(2,1)} %shares.1), calls=%async_computation | async-start | bytes 1048576 | tf_op jit(solution)/shard_map/all_to_all | solution.py:406
  30.3 7.7 %collective-permute-start = (bf16[8,32,512]{2,1,0:T(8,128)(2,1)S(1)}, bf16[8,32,512]{2,1,0:T(8,128)(2,1)S(1)}, u32[]{:S(2)}, u32[]{:S(2)}) collective-permute-start(bf16[8,32,512]{2,1,0:T(8,128)(2,1)S(1)} %slice_bitcast_fusion), channel_id=1, source_target_pairs={{0,8},{8,16},{16,24},{24,32},{32,40},{40,48},{48,56},{56,64},{64,7... | collective-permute-start | bytes 786440 | tf_op jit(solution)/shard_map/ppermute | solution.py:458
  32.6 0.7 copy-start.2
  57.9 18.6 %copy-start.1 = (bf16[2,256,256]{2,1,0:T(8,128)(2,1)S(1)}, bf16[2,256,256]{2,1,0:T(8,128)(2,1)}, u32[]{:S(2)}) copy-start(bf16[2,256,256]{2,1,0:T(8,128)(2,1)} %coupling_ref.1) | copy-start | bytes 786436
  81.9 4.2 %collective-permute-start.1 = (f32[3,256,256]{2,1,0:T(8,128)S(1)}, f32[3,256,256]{2,1,0:T(8,128)S(1)}, u32[]{:S(2)}, u32[]{:S(2)}) collective-permute-start(f32[3,256,256]{2,1,0:T(8,128)S(1)} %leaf.1.own_ref), channel_id=1, source_target_pairs={{0,8},{8,0},{16,24},{24,16},{32,40},{40,32},{48,56},{56,48},{64,72... | collective-permute-start | bytes 2359304 | tf_op jit(solution)/shard_map/ppermute | solution.py:465
  90.6 13.4 %collective-permute-start.2 = (f32[264,256]{1,0:T(8,128)S(1)}, f32[264,256]{1,0:T(8,128)S(1)}, u32[]{:S(2)}, u32[]{:S(2)}) collective-permute-start(f32[264,256]{1,0:T(8,128)S(1)} %get-tuple-element.34), channel_id=1, source_target_pairs={{16,0},{24,8},{0,16},{8,24},{48,32},{56,40},{32,48},{40,56},{80,64... | collective-permute-start | bytes 811016 | tf_op jit(solution)/shard_map/ppermute | solution.py:473
  104.1 3.4 %collective-permute-start.3 = (f32[264,256]{1,0:T(8,128)S(1)}, f32[264,256]{1,0:T(8,128)S(1)}, u32[]{:S(2)}, u32[]{:S(2)}) collective-permute-start(f32[264,256]{1,0:T(8,128)S(1)} %collective-permute-done.2.came_ref), channel_id=1, source_target_pairs={{0,8},{8,0},{16,24},{24,16},{32,40},{40,32},{48,56},{56,48},{64,72... | collective-permute-start | bytes 811016 | tf_op jit(solution)/shard_map/ppermute | solution.py:474
  112.3 7.6 %collective-permute-start.4 = (f32[264,256]{1,0:T(8,128)S(1)}, f32[264,256]{1,0:T(8,128)S(1)}, u32[]{:S(2)}, u32[]{:S(2)}) collective-permute-start(f32[264,256]{1,0:T(8,128)S(1)} %get-tuple-element.36), channel_id=1, source_target_pairs={{32,0},{40,8},{16,48},{24,56},{96,64},{104,72},{80,112},{88,120},{... | collective-permute-start | bytes 811016 | tf_op jit(solution)/shard_map/ppermute | solution.py:473
  119.9 3.4 %collective-permute-start.5 = (f32[264,256]{1,0:T(8,128)S(1)}, f32[264,256]{1,0:T(8,128)S(1)}, u32[]{:S(2)}, u32[]{:S(2)}) collective-permute-start(f32[264,256]{1,0:T(8,128)S(1)} %collective-permute-done.4.came_ref), channel_id=1, source_target_pairs={{0,8},{8,0},{16,24},{24,16},{32,40},{40,32},{48,56},{56,48},{64,72... | collective-permute-start | bytes 811016 | tf_op jit(solution)/shard_map/ppermute | solution.py:474
  124.1 0.7 collective-permute-start.6
  124.8 3.4 %collective-permute-start.7 = (f32[264,256]{1,0:T(8,128)S(1)}, f32[264,256]{1,0:T(8,128)S(1)}, u32[]{:S(2)}, u32[]{:S(2)}) collective-permute-start(f32[264,256]{1,0:T(8,128)S(1)} %collective-permute-done.6.came_ref), channel_id=1, source_target_pairs={{0,8},{8,0},{16,24},{24,16},{32,40},{40,32},{48,56},{56,48},{64,72... | collective-permute-start | bytes 811016 | tf_op jit(solution)/shard_map/ppermute | solution.py:474
  128.9 0.7 collective-permute-start.8
  129.6 3.4 %collective-permute-start.9 = (f32[264,256]{1,0:T(8,128)S(1)}, f32[264,256]{1,0:T(8,128)S(1)}, u32[]{:S(2)}, u32[]{:S(2)}) collective-permute-start(f32[264,256]{1,0:T(8,128)S(1)} %collective-permute-done.8.came_ref), channel_id=1, source_target_pairs={{0,8},{8,0},{16,24},{24,16},{32,40},{40,32},{48,56},{56,48},{64,72... | collective-permute-start | bytes 811016 | tf_op jit(solution)/shard_map/ppermute | solution.py:474
  133.6 0.7 collective-permute-start.10
  134.3 3.3 %collective-permute-start.11 = (f32[184,256]{1,0:T(8,128)S(1)}, f32[184,256]{1,0:T(8,128)S(1)}, u32[]{:S(2)}, u32[]{:S(2)}) collective-permute-start(f32[184,256]{1,0:T(8,128)S(1)} %collective-permute-done.10.came_ref), channel_id=1, source_target_pairs={{0,8},{8,0},{16,24},{24,16},{32,40},{40,32},{48,56},{56,48},{64,72... | collective-permute-start | bytes 565256 | tf_op jit(solution)/shard_map/ppermute | solution.py:474
  138.2 55.7 %collective-permute-start.12 = (f32[3,4,32]{2,1,0:T(4,128)S(1)}, f32[3,4,32]{2,1,0:T(4,128)S(1)}, u32[]{:S(2)}, u32[]{:S(2)}) collective-permute-start(f32[3,4,32]{2,1,0:T(4,128)S(1)} %get-tuple-element.44), channel_id=1, source_target_pairs={{0,16},{8,24},{48,32},{56,40},{64,80},{72,88},{112,96},{120,104},{... | collective-permute-start | bytes 4616 | tf_op jit(solution)/shard_map/ppermute | solution.py:485

commit v9 on v8

--- a/solution.py
+++ b/solution.py
@@ -100,9 +100,17 @@
         def _():
             x_ref[...] = step_size(d_ref[...]) * unit(d_ref.shape[0])
 
-        x, residual = newton(parts(d_ref[...]), x_ref[...], dot6)
-        x_ref[...] = x
-        finish(x)
+        x_parts = parts(x_ref[...])
+        residual = unit(d_ref.shape[0]) - dot6(parts(d_ref[...]), x_parts)
+        rounded = residual.astype(BF16)
+        x_ref[...] = x_ref[...] + dot1(x_parts[0], rounded)
+
+        @pl.when(state[0] > 0)
+        def _():
+            rest = (residual - rounded.astype(F32)).astype(BF16)
+            x_ref[...] = x_ref[...] + (dot1(x_parts[0], rest) + dot1(x_parts[1], rounded))
+
+        finish(x_ref[...])
         return state[0] + 1, jnp.sum(residual * residual)
 
     lax.while_loop(going, again, (0, F32(1)))

time: 195 us -> 193 us (0.990)
  the two profiles are of different devices: /device:TPU:22 before, /device:TPU:16 now
where the time goes in v9:
time: 193 us
  waiting for transfers between devices  97.8 us (51%)
  blocking collectives  38.1 us (20%)
  starting transfers between devices  35.4 us (18%)
  Pallas kernels  17.9 us (9%)
  local copies, waits for them, and re-layouts  2.32 us (1%)
    ppermute x1, waiting for transfers between devices, per_device(): brought = lax.ppermute(for_next, 'sector', pairs)  53.2 us
    all_to_all x2, blocking collectives, exchange(): lax.all_to_all(array, 'chan', split_axis=0, concat_axis=0, tiled=True)  38.1 us
    all_to_all x1, waiting for transfers between devices, exchange(): lax.all_to_all(array, 'chan', split_axis=0, concat_axis=0, tiled=True)  17.5 us
    ppermute x5, waiting for transfers between devices, per_device(): came = lax.ppermute(send, 'sector', pairs)  13.1 us
    all_to_all x1, starting transfers between devices, exchange(): lax.all_to_all(array, 'chan', split_axis=0, concat_axis=0, tiled=True)  10.3 us
    ppermute x5, starting transfers between devices, per_device(): came = lax.ppermute(send, 'sector', pairs)  10 us
    ppermute x5, starting transfers between devices, per_device(): swapped = lax.ppermute(came, 'sector', cores)  9.95 us
    ppermute x5, waiting for transfers between devices, per_device(): swapped = lax.ppermute(came, 'sector', cores)  7.07 us
  transfers between devices with their start and end apart: 14, of which 11 were waited for; matrix products, arithmetic and copies ran while one was open for 0% of the time, Pallas kernels for 0%

profile of v9, /device:TPU:16, one launch (start us, length us, event | category | flops | bytes accessed | tf_op | source)
XLA Modules:
  0.0 192.5 jit_solution(13203080325476828350)
XLA Ops:
  0.6 0.0 copy-start
  0.6 1.0 copy-done
  1.7 0.8 shares.1
  2.5 10.3 %all-to-all-start = ((bf16[8,2,32,512]{3,2,1,0:T(8,128)(2,1)}), bf16[8,2,32,512]{3,2,1,0:T(8,128)(2,1)S(1)}, u32[]{:S(2)}, u32[]{:S(2)}) async-start(bf16[8,2,32,512]{3,2,1,0:T(8,128)(2,1)} %shares.1), calls=%async_computation | async-start | bytes 1048576 | tf_op jit(solution)/shard_map/all_to_all | solution.py:414
  12.8 17.5 %all-to-all-done.own_ref = bf16[8,2,32,512]{3,2,1,0:T(8,128)(2,1)S(1)} async-done(((bf16[8,2,32,512]{3,2,1,0:T(8,128)(2,1)}), bf16[8,2,32,512]{3,2,1,0:T(8,128)(2,1)S(1)}, u32[]{:S(2)}, u32[]{:S(2)}) %all-to-all-start) | async-done | bytes 524320 | tf_op jit(solution)/shard_map/all_to_all | solution.py:414
  30.3 1.9 collective-permute-start
  32.3 0.3 inner_parts.1.inner_ref
  32.6 0.0 copy-start.2
  32.6 0.1 stack.50.flags_ref
  32.7 0.6 copy-done.2
  33.3 4.7 %collective-permute-done.before_ref = bf16[8,32,512]{2,1,0:T(8,128)(2,1)S(1)} collective-permute-done((bf16[8,32,512]{2,1,0:T(8,128)(2,1)S(1)}, bf16[8,32,512]{2,1,0:T(8,128)(2,1)S(1)}, u32[]{:S(2)}, u32[]{:S(2)}) %collective-permute-start) | collective-permute-done | bytes 262176 | tf_op jit(solution)/shard_map/ppermute | solution.py:466
  38.0 0.3 margin_parts.1
  38.3 19.6 %all_to_all.15.partial_ref = f32[8,2,32,256]{3,2,1,0:T(8,128)S(1)} all-to-all(f32[8,2,32,256]{3,2,1,0:T(8,128)S(1)} %margin_parts.1), channel_id=1, replica_groups=mesh['sector'=64,'chan'=8] {'chan'}, dimensions={0} | all-to-all | bytes 1048576 | tf_op jit(solution)/shard_map/all_to_all | solution.py:414
  57.9 0.0 copy-start.1
  57.9 18.6 %all_to_all.16.margin_ref = f32[8,2,32,256]{3,2,1,0:T(8,128)S(1)} all-to-all(f32[8,2,32,256]{3,2,1,0:T(8,128)S(1)} %total_for_all.1), channel_id=1, replica_groups=mesh['sector'=64,'chan'=8] {'chan'}, dimensions={0} | all-to-all | bytes 1048576 | tf_op jit(solution)/shard_map/all_to_all | solution.py:414
  76.5 0.0 copy-done.1
  76.5 5.1 %leaf.1.own_ref = f32[3,256,256]{2,1,0:T(8,128)S(1)} custom-call(s32[15]{0:T(128)S(1)} %stack.50.flags_ref, f32[8,2,32,256]{3,2,1,0:T(8,128)S(1)} %all_to_all.16.margin_ref, f32[2,256]{1,0:T(2,128)S(1)} %get-tuple-element.31.cot_ref, f32[2,256]{1,0:T(2,128)S(1)} %get-tuple-element.32.csc_ref, bf16[2,256,256]{2,1,0:T(8,128)(2,1)S(1)} %copy-done.1), custom_call_target="tpu_custom_call" | custom-call | tf_op jit(solution)/shard_map/leaf/pallas_call | solution.py:155
  81.6 1.9 collective-permute-start.1
  83.5 2.3 %collective-permute-done.1.other_ref = f32[3,256,256]{2,1,0:T(8,128)S(1)} collective-permute-done((f32[3,256,256]{2,1,0:T(8,128)S(1)}, f32[3,256,256]{2,1,0:T(8,128)S(1)}, u32[]{:S(2)}, u32[]{:S(2)}) %collective-permute-start.1) | collective-permute-done | bytes 786464 | tf_op jit(solution)/shard_map/ppermute | solution.py:473
  85.7 4.2 %core_merge.1 = (f32[3,256,256]{2,1,0:T(8,128)S(1)}, f32[264,256]{1,0:T(8,128)S(1)}) custom-call(s32[15]{0:T(128)S(1)} %stack.50.flags_ref, f32[3,256,256]{2,1,0:T(8,128)S(1)} %leaf.1.own_ref, f32[3,256,256]{2,1,0:T(8,128)S(1)} %collective-permute-done.1.other_ref), custom_call_target="tpu_custom_call" | custom-call | tf_op jit(solution)/shard_map/core_merge/pallas_call | solution.py:190
  90.0 6.7 %collective-permute-start.2 = (f32[264,256]{1,0:T(8,128)S(1)}, f32[264,256]{1,0:T(8,128)S(1)}, u32[]{:S(2)}, u32[]{:S(2)}) collective-permute-start(f32[264,256]{1,0:T(8,128)S(1)} %get-tuple-element.34), channel_id=1, source_target_pairs={{16,0},{24,8},{0,16},{8,24},{48,32},{56,40},{32,48},{40,56},{80,64... | collective-permute-start | bytes 811016 | tf_op jit(solution)/shard_map/ppermute | solution.py:481
  96.7 6.8 %collective-permute-done.2.came_ref = f32[264,256]{1,0:T(8,128)S(1)} collective-permute-done((f32[264,256]{1,0:T(8,128)S(1)}, f32[264,256]{1,0:T(8,128)S(1)}, u32[]{:S(2)}, u32[]{:S(2)}) %collective-permute-start.2) | collective-permute-done | bytes 270368 | tf_op jit(solution)/shard_map/ppermute | solution.py:481
  103.4 1.9 collective-permute-start.3
  105.3 1.5 collective-permute-done.3.swapped_ref
  106.9 4.4 %chip_merge.4 = (f32[3,256,256]{2,1,0:T(8,128)S(1)}, f32[264,256]{1,0:T(8,128)S(1)}) custom-call(s32[15]{0:T(128)S(1)} %stack.50.flags_ref, f32[3,256,256]{2,1,0:T(8,128)S(1)} %get-tuple-element.33.own_ref, f32[264,256]{1,0:T(8,128)S(1)} %collective-permute-done.2.came_ref, f32[264,256]{1,0:T(8,128)S(1)} %collective-permute-done.3.swapped_ref), custom_call_target="tpu_custom_call" | custom-call | tf_op jit(solution)/shard_map/chip_merge/pallas_call | solution.py:253
  111.3 1.3 collective-permute-start.4
  112.6 6.3 %collective-permute-done.4.came_ref = f32[264,256]{1,0:T(8,128)S(1)} collective-permute-done((f32[264,256]{1,0:T(8,128)S(1)}, f32[264,256]{1,0:T(8,128)S(1)}, u32[]{:S(2)}, u32[]{:S(2)}) %collective-permute-start.4) | collective-permute-done | bytes 270368 | tf_op jit(solution)/shard_map/ppermute | solution.py:481
  118.9 1.9 collective-permute-start.5
  120.8 1.5 collective-permute-done.5.swapped_ref
  122.3 0.8 chip_merge.5
  123.1 0.7 collective-permute-start.6
  123.8 0.0 collective-permute-done.6.came_ref
  123.8 2.0 %collective-permute-start.7 = (f32[264,256]{1,0:T(8,128)S(1)}, f32[264,256]{1,0:T(8,128)S(1)}, u32[]{:S(2)}, u32[]{:S(2)}) collective-permute-start(f32[264,256]{1,0:T(8,128)S(1)} %collective-permute-done.6.came_ref), channel_id=1, source_target_pairs={{0,8},{8,0},{16,24},{24,16},{32,40},{40,32},{48,56},{56,48},{64,72... | collective-permute-start | bytes 811016 | tf_op jit(solution)/shard_map/ppermute | solution.py:482
  125.9 1.4 collective-permute-done.7.swapped_ref
  127.3 0.6 chip_merge.6
  127.9 0.7 collective-permute-start.8
  128.6 0.0 collective-permute-done.8.came_ref
  128.6 2.0 %collective-permute-start.9 = (f32[264,256]{1,0:T(8,128)S(1)}, f32[264,256]{1,0:T(8,128)S(1)}, u32[]{:S(2)}, u32[]{:S(2)}) collective-permute-start(f32[264,256]{1,0:T(8,128)S(1)} %collective-permute-done.8.came_ref), channel_id=1, source_target_pairs={{0,8},{8,0},{16,24},{24,16},{32,40},{40,32},{48,56},{56,48},{64,72... | collective-permute-start | bytes 811016 | tf_op jit(solution)/shard_map/ppermute | solution.py:482
  130.7 1.4 collective-permute-done.9.swapped_ref
  132.0 0.6 chip_merge.7
  132.7 0.7 collective-permute-start.10
  133.3 0.0 collective-permute-done.10.came_ref
  133.4 2.0 %collective-permute-start.11 = (f32[184,256]{1,0:T(8,128)S(1)}, f32[184,256]{1,0:T(8,128)S(1)}, u32[]{:S(2)}, u32[]{:S(2)}) collective-permute-start(f32[184,256]{1,0:T(8,128)S(1)} %collective-permute-done.10.came_ref), channel_id=1, source_target_pairs={{0,8},{8,0},{16,24},{24,16},{32,40},{40,32},{48,56},{56,48},{64,72... | collective-permute-start | bytes 565256 | tf_op jit(solution)/shard_map/ppermute | solution.py:482
  135.4 1.3 collective-permute-done.11.swapped_ref
  136.7 0.8 last_merge.1
  137.5 1.3 collective-permute-start.12
  138.8 53.2 %collective-permute-done.12 = f32[3,4,32]{2,1,0:T(4,128)S(1)} collective-permute-done((f32[3,4,32]{2,1,0:T(4,128)S(1)}, f32[3,4,32]{2,1,0:T(4,128)S(1)}, u32[]{:S(2)}, u32[]{:S(2)}) %collective-permute-start.12) | collective-permute-done | bytes 1568 | tf_op jit(solution)/shard_map/ppermute | solution.py:493
  192.0 0.6 slice_bitcast_fusion.1
  (4 shorter events, 0.1 us)
Async XLA Ops:
  0.6 1.0 copy-start
  2.5 27.8 %all-to-all-start = ((bf16[8,2,32,512]{3,2,1,0:T(8,128)(2,1)}), bf16[8,2,32,512]{3,2,1,0:T(8,128)(2,1)S(1)}, u32[]{:S(2)}, u32[]{:S(2)}) async-start(bf16[8,2,32,512]{3,2,1,0:T(8,128)(2,1)} %shares.1), calls=%async_computation | async-start | bytes 1048576 | tf_op jit(solution)/shard_map/all_to_all | solution.py:414
  30.3 7.7 %collective-permute-start = (bf16[8,32,512]{2,1,0:T(8,128)(2,1)S(1)}, bf16[8,32,512]{2,1,0:T(8,128)(2,1)S(1)}, u32[]{:S(2)}, u32[]{:S(2)}) collective-permute-start(bf16[8,32,512]{2,1,0:T(8,128)(2,1)S(1)} %slice_bitcast_fusion), channel_id=1, source_target_pairs={{0,8},{8,16},{16,24},{24,32},{32,40},{40,48},{48,56},{56,64},{64,7... | collective-permute-start | bytes 786440 | tf_op jit(solution)/shard_map/ppermute | solution.py:466
  32.6 0.7 copy-start.2
  57.9 18.6 %copy-start.1 = (bf16[2,256,256]{2,1,0:T(8,128)(2,1)S(1)}, bf16[2,256,256]{2,1,0:T(8,128)(2,1)}, u32[]{:S(2)}) copy-start(bf16[2,256,256]{2,1,0:T(8,128)(2,1)} %coupling_ref.1) | copy-start | bytes 786436
  81.6 4.2 %collective-permute-start.1 = (f32[3,256,256]{2,1,0:T(8,128)S(1)}, f32[3,256,256]{2,1,0:T(8,128)S(1)}, u32[]{:S(2)}, u32[]{:S(2)}) collective-permute-start(f32[3,256,256]{2,1,0:T(8,128)S(1)} %leaf.1.own_ref), channel_id=1, source_target_pairs={{0,8},{8,0},{16,24},{24,16},{32,40},{40,32},{48,56},{56,48},{64,72... | collective-permute-start | bytes 2359304 | tf_op jit(solution)/shard_map/ppermute | solution.py:473
  90.0 13.5 %collective-permute-start.2 = (f32[264,256]{1,0:T(8,128)S(1)}, f32[264,256]{1,0:T(8,128)S(1)}, u32[]{:S(2)}, u32[]{:S(2)}) collective-permute-start(f32[264,256]{1,0:T(8,128)S(1)} %get-tuple-element.34), channel_id=1, source_target_pairs={{16,0},{24,8},{0,16},{8,24},{48,32},{56,40},{32,48},{40,56},{80,64... | collective-permute-start | bytes 811016 | tf_op jit(solution)/shard_map/ppermute | solution.py:481
  103.4 3.4 %collective-permute-start.3 = (f32[264,256]{1,0:T(8,128)S(1)}, f32[264,256]{1,0:T(8,128)S(1)}, u32[]{:S(2)}, u32[]{:S(2)}) collective-permute-start(f32[264,256]{1,0:T(8,128)S(1)} %collective-permute-done.2.came_ref), channel_id=1, source_target_pairs={{0,8},{8,0},{16,24},{24,16},{32,40},{40,32},{48,56},{56,48},{64,72... | collective-permute-start | bytes 811016 | tf_op jit(solution)/shard_map/ppermute | solution.py:482
  111.3 7.6 %collective-permute-start.4 = (f32[264,256]{1,0:T(8,128)S(1)}, f32[264,256]{1,0:T(8,128)S(1)}, u32[]{:S(2)}, u32[]{:S(2)}) collective-permute-start(f32[264,256]{1,0:T(8,128)S(1)} %get-tuple-element.36), channel_id=1, source_target_pairs={{32,0},{40,8},{16,48},{24,56},{96,64},{104,72},{80,112},{88,120},{... | collective-permute-start | bytes 811016 | tf_op jit(solution)/shard_map/ppermute | solution.py:481
  118.9 3.4 %collective-permute-start.5 = (f32[264,256]{1,0:T(8,128)S(1)}, f32[264,256]{1,0:T(8,128)S(1)}, u32[]{:S(2)}, u32[]{:S(2)}) collective-permute-start(f32[264,256]{1,0:T(8,128)S(1)} %collective-permute-done.4.came_ref), channel_id=1, source_target_pairs={{0,8},{8,0},{16,24},{24,16},{32,40},{40,32},{48,56},{56,48},{64,72... | collective-permute-start | bytes 811016 | tf_op jit(solution)/shard_map/ppermute | solution.py:482
  123.1 0.7 collective-permute-start.6
  123.8 3.4 %collective-permute-start.7 = (f32[264,256]{1,0:T(8,128)S(1)}, f32[264,256]{1,0:T(8,128)S(1)}, u32[]{:S(2)}, u32[]{:S(2)}) collective-permute-start(f32[264,256]{1,0:T(8,128)S(1)} %collective-permute-done.6.came_ref), channel_id=1, source_target_pairs={{0,8},{8,0},{16,24},{24,16},{32,40},{40,32},{48,56},{56,48},{64,72... | collective-permute-start | bytes 811016 | tf_op jit(solution)/shard_map/ppermute | solution.py:482
  127.9 0.7 collective-permute-start.8
  128.6 3.4 %collective-permute-start.9 = (f32[264,256]{1,0:T(8,128)S(1)}, f32[264,256]{1,0:T(8,128)S(1)}, u32[]{:S(2)}, u32[]{:S(2)}) collective-permute-start(f32[264,256]{1,0:T(8,128)S(1)} %collective-permute-done.8.came_ref), channel_id=1, source_target_pairs={{0,8},{8,0},{16,24},{24,16},{32,40},{40,32},{48,56},{56,48},{64,72... | collective-permute-start | bytes 811016 | tf_op jit(solution)/shard_map/ppermute | solution.py:482
  132.7 0.7 collective-permute-start.10
  133.4 3.3 %collective-permute-start.11 = (f32[184,256]{1,0:T(8,128)S(1)}, f32[184,256]{1,0:T(8,128)S(1)}, u32[]{:S(2)}, u32[]{:S(2)}) collective-permute-start(f32[184,256]{1,0:T(8,128)S(1)} %collective-permute-done.10.came_ref), channel_id=1, source_target_pairs={{0,8},{8,0},{16,24},{24,16},{32,40},{40,32},{48,56},{56,48},{64,72... | collective-permute-start | bytes 565256 | tf_op jit(solution)/shard_map/ppermute | solution.py:482
  137.5 54.5 %collective-permute-start.12 = (f32[3,4,32]{2,1,0:T(4,128)S(1)}, f32[3,4,32]{2,1,0:T(4,128)S(1)}, u32[]{:S(2)}, u32[]{:S(2)}) collective-permute-start(f32[3,4,32]{2,1,0:T(4,128)S(1)} %get-tuple-element.44), channel_id=1, source_target_pairs={{0,16},{8,24},{48,32},{56,40},{64,80},{72,88},{112,96},{120,104},{... | collective-permute-start | bytes 4616 | tf_op jit(solution)/shard_map/ppermute | solution.py:493
